TPU v7x, 128 devices: a whole 4x4x4 slice. The times are simulated.
128 devices in a mesh: lat: 4 (over z), lon: 32 (over y, x, core).
Axes of the slice: x: 4, y: 4, z: 4, core: 2. Of those that a mesh axis runs over, the one named last changes fastest.
Arguments:
- grid_feat: bfloat16 [262144, 512], P(('lat', 'lon')), may hold values from -6 to 6
- mesh_feat: bfloat16 [32768, 512], P(('lat', 'lon')), may hold values from -6 to 6
- g2m_src: int32 [524288], P(('lat', 'lon')), may hold values from 0 to 262143, as said below
- g2m_dst: int32 [524288], P(('lat', 'lon')), may hold values from 0 to 32767, as said below
- g2m_weight: float32 [524288], P(('lat', 'lon')), may hold values from 0.25 to 1.75
- mesh_src: int32 [128, 128, 32], P(('lat', 'lon')), may hold values from 0 to 32767, as said below
- mesh_dst: int32 [128, 128, 32], P(('lat', 'lon')), may hold values from 0 to 32767, as said below
- mesh_count: int32 [128, 128], P(('lat', 'lon')), may hold values from 1 to 32, as said below
- m2g_src: int32 [262144, 3], P(('lat', 'lon')), may hold values from 0 to 32767, as said below
- m2g_weight: float32 [262144, 3], P(('lat', 'lon')), may hold values from 0.25 to 1.75
- w_in: bfloat16 [512, 512], replicated, may hold values from -0.25 to 0.25
- w_enc: bfloat16 [512, 512], replicated, may hold values from -0.25 to 0.25
- w_send: bfloat16 [512, 512], replicated, may hold values from -0.25 to 0.25
- w_recv: bfloat16 [512, 512], replicated, may hold values from -0.25 to 0.25
- w_edge: bfloat16 [512, 512], replicated, may hold values from -0.25 to 0.25
- w_node: bfloat16 [512, 512], replicated, may hold values from -0.25 to 0.25
- w_dec: bfloat16 [512, 512], replicated, may hold values from -0.25 to 0.25
- w_out: bfloat16 [512, 512], replicated, may hold values from -0.25 to 0.25
- gain_enc: float32 [512], replicated, may hold values from 0.1 to 1.9
- gain_node: float32 [512], replicated, may hold values from 0.1 to 1.9
- gain_out: float32 [512], replicated, may hold values from 0.1 to 1.9
Outputs:
- grid_out: bfloat16 [262144, 512], P(('lat', 'lon'))
- mesh_out: bfloat16 [32768, 512], P(('lat', 'lon'))
Inputs may be any that keep to these rules, and one draw needn't show every extreme that they name: `g2m_src`: the edges of tile t's shard have senders on tile t; every grid node of a tile sends at least one edge. `g2m_dst`: each receiver is owned by a tile at most one latitude band and one longitude sector (periodically) away from the sender's tile; bands do not wrap. mesh_src[s, t, k] is owned by tile s. mesh_dst[s, t, k] is owned by tile t. `mesh_count`: every tile pair has at least one live slot; some pairs fill all 32. `m2g_src`: each sender is owned by a tile at most one latitude band and one longitude sector (periodically) away from the grid node's tile; bands do not wrap.
All inputs are finite; a program needn't handle non-finite values.
Results may differ from a plain program's by a relative error of at most 0.013.
Values may be sent and summed in bfloat16 or wider, within the bound.
No kernel may reach another device: no remote copies, remote signals or barrier semaphores. Data moves between devices by JAX's collectives and lax.ppermute only.
A program may use at most 128 MiB of HBM per device.

v0:
```python
import jax
import jax.numpy as jnp
from jax import lax
from jax.sharding import PartitionSpec as P


def shifted(block, axis, distance):
    devices = range(lax.axis_size(axis))
    route = [((i - distance) % len(devices), i) for i in devices]
    return lax.ppermute(block, axis, route)


def shifted_2(shard, axis, by):
    size = lax.axis_size(axis)
    pairs = [(i, i + by) for i in range(size) if 0 <= i + by < size]
    return lax.ppermute(shard, axis, pairs)


def padded(shard, sides, width):
    for axis, dim in sides:
        size, length = (lax.axis_size(axis), shard.shape[dim])
        up = [(i, (i + 1) % size) for i in range(size)]
        down = [(j, i) for i, j in up]
        last = lax.slice_in_dim(shard, length - width, length, axis=dim)
        leading = lax.slice_in_dim(shard, 0, width, axis=dim)
        before = lax.ppermute(last, axis, up)
        after = lax.ppermute(leading, axis, down)
        shard = jnp.concatenate([before, shard, after], axis=dim)
    return shard


def layer_norm(values):
    center = values - jnp.mean(values, axis=-1, keepdims=True)
    spread = jnp.mean(center * center, axis=-1, keepdims=True)
    return center * lax.rsqrt(spread + 1e-05)


def on_device(
    grid_feat,
    mesh_feat,
    g2m_src,
    g2m_dst,
    g2m_weight,
    mesh_src,
    mesh_dst,
    mesh_count,
    m2g_src,
    m2g_weight,
    w_in,
    w_enc,
    w_send,
    w_recv,
    w_edge,
    w_node,
    w_dec,
    w_out,
    gain_enc,
    gain_node,
    gain_out,
):
    grid_rows = grid_feat.shape[0]
    mesh_rows = mesh_feat.shape[0]
    latent = grid_feat.shape[1]
    lat_count = lax.axis_size("lat")
    lon_count = lax.axis_size("lon")
    all_tiles = lat_count * lon_count
    lat_band = lax.axis_index("lat")
    lon_sector = lax.axis_index("lon")
    device_id = lat_band * lon_count + lon_sector

    def tile_slot(node_ids):
        owner_tile = node_ids // mesh_rows
        step_lat = owner_tile // lon_count - lat_band
        step_lon = (owner_tile % lon_count - lon_sector + 1) % lon_count - 1
        return ((step_lat + 1) * 3 + step_lon + 1) * mesh_rows + node_ids % mesh_rows

    hidden = jax.nn.silu(jnp.dot(grid_feat, w_in, preferred_element_type=jnp.float32)).astype(
        jnp.bfloat16
    )
    local_src = g2m_src - device_id * grid_rows
    messages = (g2m_weight[:, None] * hidden[local_src].astype(jnp.float32)).astype(jnp.bfloat16)
    edge_count = messages.shape[0]
    msg_blocks = messages.reshape(4, edge_count // 4, latent)
    slot_blocks = tile_slot(g2m_dst).reshape(4, edge_count // 4)
    slot_iota = jnp.arange(9 * mesh_rows, dtype=jnp.int32)

    def add_block(totals, inputs):
        msg_blk, slot_blk = inputs
        onehot = (slot_blk[:, None] == slot_iota[None, :]).astype(jnp.bfloat16)
        return (
            totals
            + lax.dot_general(
                onehot, msg_blk, (((0,), (0,)), ((), ())), preferred_element_type=jnp.float32
            ),
            None,
        )

    partial9, _ = lax.scan(
        add_block, jnp.zeros((9 * mesh_rows, latent), jnp.float32), (msg_blocks, slot_blocks)
    )
    pieces = partial9.reshape(3, 3, mesh_rows, latent)
    column = pieces[:, 1] + shifted(pieces[:, 2], "lon", 1) + shifted(pieces[:, 0], "lon", -1)
    pooled = column[1] + shifted_2(column[2], "lat", 1) + shifted_2(column[0], "lat", -1)
    update = jax.nn.silu(
        jnp.dot(pooled.astype(jnp.bfloat16), w_enc, preferred_element_type=jnp.float32)
    )
    first = (mesh_feat.astype(jnp.float32) + gain_enc * layer_norm(update)).astype(jnp.bfloat16)
    sent_proj = jnp.dot(first, w_send, preferred_element_type=jnp.float32).astype(jnp.bfloat16)
    recv_proj = jnp.dot(first, w_recv, preferred_element_type=jnp.float32)
    capacity = mesh_src.shape[2]
    sender_rows = sent_proj[mesh_src[0] - device_id * mesh_rows]
    live = lax.broadcasted_iota(jnp.int32, (all_tiles, capacity), 1) < mesh_count[0][:, None]
    targets = jnp.where(live, mesh_dst[0] % mesh_rows, mesh_rows)
    rows_in = lax.all_to_all(sender_rows, ("lat", "lon"), split_axis=0, concat_axis=0, tiled=True)
    target_in = lax.all_to_all(targets, ("lat", "lon"), split_axis=0, concat_axis=0, tiled=True)
    near_proj = recv_proj[jnp.minimum(target_in, mesh_rows - 1)]
    joined = jax.nn.silu(rows_in.astype(jnp.float32) + near_proj).astype(jnp.bfloat16)
    edge_msg = jnp.einsum("pcd,de->pce", joined, w_edge, preferred_element_type=jnp.float32).astype(
        jnp.bfloat16
    )
    edge_msg, target_in = (edge_msg, target_in)
    flat_target = target_in.reshape(-1)
    node_iota = jnp.arange(mesh_rows, dtype=jnp.int32)
    receive_table = (flat_target[:, None] == node_iota[None, :]).astype(jnp.bfloat16)
    pooled_two = lax.dot_general(
        receive_table,
        edge_msg.reshape(-1, latent),
        (((0,), (0,)), ((), ())),
        preferred_element_type=jnp.float32,
    )
    node_upd = jax.nn.silu(
        jnp.dot(pooled_two.astype(jnp.bfloat16), w_node, preferred_element_type=jnp.float32)
    )
    mesh_out = (first.astype(jnp.float32) + gain_node * layer_norm(node_upd)).astype(jnp.bfloat16)
    decoded = jnp.dot(mesh_out, w_dec, preferred_element_type=jnp.float32).astype(jnp.bfloat16)
    beside_all = padded(decoded.reshape(1, 1, mesh_rows, latent), (("lat", 0), ("lon", 1)), 1)
    around_rows = beside_all.reshape(9 * mesh_rows, latent)
    source_slots = tile_slot(m2g_src)
    gathered = m2g_weight[:, 0:1] * around_rows[source_slots[:, 0]].astype(jnp.float32)
    gathered = gathered + m2g_weight[:, 1:2] * around_rows[source_slots[:, 1]].astype(jnp.float32)
    gathered = gathered + m2g_weight[:, 2:3] * around_rows[source_slots[:, 2]].astype(jnp.float32)
    grid_upd = jax.nn.silu(
        jnp.dot(gathered.astype(jnp.bfloat16), w_out, preferred_element_type=jnp.float32)
    )
    grid_out = (grid_feat.astype(jnp.float32) + gain_out * layer_norm(grid_upd)).astype(
        jnp.bfloat16
    )
    return (grid_out, mesh_out)


def solution(mesh):
    return jax.shard_map(
        on_device,
        mesh=mesh,
        in_specs=(
            P(("lat", "lon"), None),
            P(("lat", "lon"), None),
            P(("lat", "lon")),
            P(("lat", "lon")),
            P(("lat", "lon")),
            P(("lat", "lon"), None, None),
            P(("lat", "lon"), None, None),
            P(("lat", "lon"), None),
            P(("lat", "lon"), None),
            P(("lat", "lon"), None),
            P(),
            P(),
            P(),
            P(),
            P(),
            P(),
            P(),
            P(),
            P(),
            P(),
            P(),
        ),
        out_specs=(P(("lat", "lon"), None), P(("lat", "lon"), None)),
        check_vma=False,
    )
```

profile of v0, /device:TPU:0, one launch (start us, length us, event | category | flops | bytes accessed | tf_op | source)
XLA Modules:
  0.0 271.1 jit_solution(5409231903337065856)
XLA Ops:
  0.6 0.0 copy-start
  0.7 0.8 fusion.53
  1.5 0.7 mul.152
  2.2 0.7 fusion.58
  3.0 3.5 %multiply_convert_fusion.1 = bf16[2048,512]{1,0:T(8,128)(2,1)S(1)} fusion(bf16[2048,512]{1,0:T(8,128)(2,1)} %param.23, bf16[512,512]{1,0:T(8,128)(2,1)} %param.33), kind=kOutput, calls=%fused_computation.25 | convolution fusion | flops 1078984704 | bytes 4718592 | tf_op jit(solution)/shard_map/dot_general | solution.py:77
  6.5 17.4 %gather_fusion = bf16[4096,512]{1,0:T(8,128)(2,1)} fusion(bf16[2048,512]{1,0:T(8,128)(2,1)S(1)} %multiply_convert_fusion.1, s32[4096]{0:T(1024)S(1)} %fusion.58), kind=kCustom, calls=%fused_computation | custom fusion | bytes 8404992 | tf_op jit(solution)/shard_map/gather | solution.py:81
  23.9 4.1 %fusion.8 = bf16[4,1024,512]{2,1,0:T(8,128)(2,1)} fusion(bf16[4,1024,512]{2,1,0:T(8,128)(2,1)} %bitcast.83, f32[4,1024]{1,0:T(4,128)S(1)} %mul.152), kind=kLoop, calls=%fused_computation.16 | loop fusion | flops 6291456 | bytes 8404992 | tf_op jit(solution)/shard_map/convert_element_type | solution.py:81
  27.9 26.8 %while.11 = (s32[]{:T(128)}, f32[2304,512]{1,0:T(8,128)}, s32[4,1024]{1,0:T(4,128)S(1)}, bf16[4,1024,512]{2,1,0:T(8,128)(2,1)}, s32[]{:T(128)}, /*index=5*/s32[]{:T(128)}) while((s32[]{:T(128)}, f32[2304,512]{1,0:T(8,128)}, s32[4,1024]{1,0:T(4,128)S(1)}, bf16[4,1024,512]{2,1,0:T(8,128)(2,1)}, s32[]{:T(128)}, ...), condition=%wide.region_1.2_spmd.clone, body=%wide.region_0.1_spmd.clone.sunk | while | flops 2420637696 | bytes 10498143 | solution.py:98
  28.0 6.2 %fusion.83 = f32[2304,512]{1,0:T(8,128)} fusion(f32[2304,512]{1,0:T(8,128)} %get-tuple-element.105, s32[1024]{0:T(1024)S(1)} %bitcast.89, pred[]{:T(512)S(6)} %compare.24, bf16[4,1024,512]{2,1,0:T(8,128)(2,1)} %get-tuple-element.113, s32[]{:T(128)S(6)} %copy.56), kind=kOutput, calls=%fused_computation.9.clone.1 | convolution fusion | flops 2420637696 | bytes 10489861 | tf_op jit(solution)/shard_map/while/body/eval_jaxpr/dot_general | solution.py:92
  34.1 6.9 %fusion.83 = f32[2304,512]{1,0:T(8,128)} fusion(f32[2304,512]{1,0:T(8,128)} %get-tuple-element.105, s32[1024]{0:T(1024)S(1)} %bitcast.89, pred[]{:T(512)S(6)} %compare.24, bf16[4,1024,512]{2,1,0:T(8,128)(2,1)} %get-tuple-element.113, s32[]{:T(128)S(6)} %copy.56), kind=kOutput, calls=%fused_computation.9.clone.1 | convolution fusion | flops 2420637696 | bytes 10489861 | tf_op jit(solution)/shard_map/while/body/eval_jaxpr/dot_general | solution.py:92
  41.0 6.9 %fusion.83 = f32[2304,512]{1,0:T(8,128)} fusion(f32[2304,512]{1,0:T(8,128)} %get-tuple-element.105, s32[1024]{0:T(1024)S(1)} %bitcast.89, pred[]{:T(512)S(6)} %compare.24, bf16[4,1024,512]{2,1,0:T(8,128)(2,1)} %get-tuple-element.113, s32[]{:T(128)S(6)} %copy.56), kind=kOutput, calls=%fused_computation.9.clone.1 | convolution fusion | flops 2420637696 | bytes 10489861 | tf_op jit(solution)/shard_map/while/body/eval_jaxpr/dot_general | solution.py:92
  47.9 6.9 %fusion.83 = f32[2304,512]{1,0:T(8,128)} fusion(f32[2304,512]{1,0:T(8,128)} %get-tuple-element.105, s32[1024]{0:T(1024)S(1)} %bitcast.89, pred[]{:T(512)S(6)} %compare.24, bf16[4,1024,512]{2,1,0:T(8,128)(2,1)} %get-tuple-element.113, s32[]{:T(128)S(6)} %copy.56), kind=kOutput, calls=%fused_computation.9.clone.1 | convolution fusion | flops 2420637696 | bytes 10489861 | tf_op jit(solution)/shard_map/while/body/eval_jaxpr/dot_general | solution.py:92
  54.8 4.1 %slice_bitcast_fusion.1 = (f32[3,256,512]{2,1,0:T(8,128)}, f32[3,256,512]{2,1,0:T(8,128)}) fusion(f32[3,3,256,512]{3,2,1,0:T(8,128)} %bitcast.84), kind=kLoop, calls=%fused_computation.35 | loop fusion | bytes 6291456 | tf_op jit(solution)/shard_map/squeeze | solution.py:102
  58.9 5.1 %collective-permute-start.1 = (f32[3,256,512]{2,1,0:T(8,128)}, f32[3,256,512]{2,1,0:T(8,128)}, u32[]{:S(2)}, u32[]{:S(2)}) collective-permute-start(f32[3,256,512]{2,1,0:T(8,128)} %get-tuple-element.56), channel_id=1, source_target_pairs={{1,0},{2,1},{3,2},{4,3},{5,4},{6,5},{7,6},{8,7},{9,8},{10,9},{11,1... | collective-permute-start | bytes 4718600 | tf_op jit(solution)/shard_map/ppermute | solution.py:10
  64.0 0.1 copy.41
  64.1 18.2 %collective-permute-done = f32[3,256,512]{2,1,0:T(8,128)S(1)} collective-permute-done((f32[3,256,512]{2,1,0:T(8,128)}, f32[3,256,512]{2,1,0:T(8,128)S(1)}, u32[]{:S(2)}, u32[]{:S(2)}) %collective-permute-start) | collective-permute-done | bytes 1572896 | tf_op jit(solution)/shard_map/ppermute | solution.py:10
  82.3 1.1 copy-done.2
  83.4 2.9 %fusion.21 = f32[3,256,512]{2,1,0:T(8,128)S(1)} fusion(f32[3,256,512]{2,1,0:T(8,128)} %collective-permute-done.1, f32[3,256,512]{2,1,0:T(8,128)} %copy-done.2, f32[3,3,256,512]{3,2,1,0:T(8,128)} %bitcast.85), kind=kLoop, calls=%fused_computation.38 | loop fusion | flops 786432 | bytes 6291456 | tf_op jit(solution)/shard_map/add | solution.py:102
  86.4 0.9 slice_bitcast_fusion.4
  87.2 4.7 %collective-permute-start.2 = (f32[256,512]{1,0:T(8,128)}, f32[256,512]{1,0:T(8,128)}, u32[]{:S(2)}, u32[]{:S(2)}) collective-permute-start(f32[256,512]{1,0:T(8,128)} %get-tuple-element.57), channel_id=1, source_target_pairs={{0,32},{32,64},{64,96},{1,33},{33,65},{65,97},{2,34},{34,66},{66,9... | collective-permute-start | bytes 1572872 | tf_op jit(solution)/shard_map/ppermute | solution.py:16
  91.9 1.3 collective-permute-start.3
  93.2 0.9 compare_select_fusion.2
  94.1 9.6 %all-to-all-start = ((s32[128,1,32]{2,1,0:T(1,128)}), s32[128,1,32]{2,1,0:T(1,128)S(1)}, u32[]{:S(2)}, u32[]{:S(2)}) async-start(s32[128,1,32]{2,1,0:T(1,128)} %compare_select_fusion.2), calls=%async_computation | async-start | bytes 131072 | tf_op jit(solution)/shard_map/all_to_all | solution.py:115
  103.7 0.1 copy.42
  103.8 0.1 reshape.224
  103.9 1.0 collective-permute-done.3
  104.9 1.8 fusion.64
  106.8 0.2 multiply_reduce_fusion.2
  107.0 1.1 add_convert_fusion.6
  108.1 0.3 convolution_convert_fusion.1
  108.4 17.3 %gather_fusion.1 = bf16[4096,512]{1,0:T(8,128)(2,1)} fusion(bf16[256,512]{1,0:T(8,128)(2,1)S(1)} %convolution_convert_fusion.1, s32[4096]{0:T(1024)S(1)} %broadcast_clamp_fusion.1), kind=kCustom, calls=%fused_computation.1 | custom fusion | bytes 8404992 | tf_op jit(solution)/shard_map/gather | solution.py:111
  125.8 10.2 %all-to-all-start.1 = ((bf16[128,32,512]{2,1,0:T(8,128)(2,1)}), bf16[128,32,512]{2,1,0:T(8,128)(2,1)}, u32[]{:S(2)}, u32[]{:S(2)}) async-start(bf16[128,32,512]{2,1,0:T(8,128)(2,1)} %bitcast.82), calls=%async_computation.1 | async-start | bytes 8388608 | tf_op jit(solution)/shard_map/all_to_all | solution.py:114
  136.0 0.2 fusion.43
  136.2 0.5 broadcast.306
  136.7 0.8 fusion.62
  137.5 0.1 eq.40
  137.6 0.1 reshape.232
  137.7 0.3 fusion.67
  138.0 16.9 %gather_fusion.2 = f32[4096,512]{1,0:T(8,128)} fusion(f32[256,512]{1,0:T(8,128)S(1)} %fusion.67, s32[4096]{0:T(1024)S(1)} %broadcast_clamp_fusion), kind=kCustom, calls=%fused_computation.2 | custom fusion | bytes 16793600 | tf_op jit(solution)/shard_map/gather | solution.py:116
  154.9 33.5 %all-to-all-done.1 = bf16[128,32,512]{2,1,0:T(8,128)(2,1)} async-done(((bf16[128,32,512]{2,1,0:T(8,128)(2,1)}), bf16[128,32,512]{2,1,0:T(8,128)(2,1)}, u32[]{:S(2)}, u32[]{:S(2)}) %all-to-all-start.1) | async-done | bytes 4194336 | tf_op jit(solution)/shard_map/all_to_all | solution.py:114
  188.4 6.3 %multiply_convert_fusion = bf16[128,32,512]{2,1,0:T(8,128)(2,1)S(1)} fusion(f32[128,32,512]{2,1,0:T(8,128)} %bitcast.81, bf16[128,32,512]{2,1,0:T(8,128)(2,1)} %all-to-all-done.1), kind=kLoop, calls=%fused_computation.17 | loop fusion | flops 14680064 | bytes 16777216 | tf_op jit(solution)/shard_map/convert_element_type | solution.py:117
  194.7 5.3 %fusion.12 = bf16[128,32,512]{2,0,1:T(8,128)(2,1)S(1)} fusion(bf16[128,32,512]{2,1,0:T(8,128)(2,1)S(1)} %multiply_convert_fusion, bf16[512,512]{1,0:T(8,128)(2,1)S(1)} %copy-done), kind=kOutput, calls=%fused_computation.27 | convolution fusion | flops 2149580800 | bytes 8912896 | tf_op jit(solution)/shard_map/pcd,de->pce/dot_general | solution.py:118
  200.1 4.4 %copy.44 = bf16[128,32,512]{2,1,0:T(8,128)(2,1)} copy(bf16[128,32,512]{2,0,1:T(8,128)(2,1)S(1)} %fusion.12) | data formatting | bytes 8388608 | tf_op jit(solution)/shard_map/convert_element_type | solution.py:118
  204.4 4.6 %fusion.65 = (f32[256]{0:T(256)S(1)}, f32[256,512]{1,0:T(8,128)S(1)}) fusion(bf16[512,512]{1,0:T(8,128)(2,1)S(1)} %copy-done.15, bf16[4096,512]{1,0:T(8,128)(2,1)} %bitcast.86, s32[4096]{0:T(1024)S(1)} %eq.40), kind=kOutput, calls=%fused_computation.143 | convolution fusion | flops 1209794304 | bytes 5260288 | tf_op jit(solution)/shard_map/dot_general | solution.py:132
  209.1 0.2 multiply_reduce_fusion.1
  209.3 0.2 add_convert_fusion.5
  209.5 0.3 fusion.23
  209.8 0.7 collective-permute-start.5
  210.5 1.4 collective-permute-start.4
  212.0 5.7 %collective-permute-done.5 = bf16[1,1,256,512]{3,2,1,0:T(8,128)(2,1)S(1)} collective-permute-done((bf16[1,1,256,512]{3,2,1,0:T(8,128)(2,1)S(1)}, bf16[1,1,256,512]{3,2,1,0:T(8,128)(2,1)S(1)}, u32[]{:S(2)}, u32[]{:S(2)}) %collective-permute-start.5) | collective-permute-done | bytes 262176 | tf_op jit(solution)/shard_map/ppermute | solution.py:27
  217.7 1.6 collective-permute-done.4
  219.3 0.1 pad_maximum_fusion.1
  219.4 0.3 collective-permute-start.7
  219.6 0.3 collective-permute-start.6
  220.0 9.1 %collective-permute-done.7 = bf16[3,1,256,512]{3,2,1,0:T(8,128)(2,1)S(1)} collective-permute-done((bf16[3,1,256,512]{3,2,1,0:T(8,128)(2,1)S(1)}, bf16[3,1,256,512]{3,2,1,0:T(8,128)(2,1)S(1)}, u32[]{:S(2)}, u32[]{:S(2)}) %collective-permute-start.7) | collective-permute-done | bytes 786464 | tf_op jit(solution)/shard_map/ppermute | solution.py:27
  229.1 5.2 %collective-permute-done.6 = bf16[3,1,256,512]{3,2,1,0:T(8,128)(2,1)S(1)} collective-permute-done((bf16[3,1,256,512]{3,2,1,0:T(8,128)(2,1)S(1)}, bf16[3,1,256,512]{3,2,1,0:T(8,128)(2,1)S(1)}, u32[]{:S(2)}, u32[]{:S(2)}) %collective-permute-start.6) | collective-permute-done | bytes 786464 | tf_op jit(solution)/shard_map/ppermute | solution.py:26
  234.3 0.3 pad_maximum_fusion
  234.7 9.2 %gather_fusion.5 = bf16[2048,512]{1,0:T(8,128)(2,1)} fusion(bf16[2304,512]{1,0:T(8,128)(2,1)S(1)} %bitcast.78, s32[2048]{0:T(1024)S(1)} %broadcast_clamp_fusion.2), kind=kCustom, calls=%fused_computation.5 | custom fusion | bytes 4202496 | tf_op jit(solution)/shard_map/gather | solution.py:141
  243.9 9.2 %gather_fusion.4 = bf16[2048,512]{1,0:T(8,128)(2,1)} fusion(bf16[2304,512]{1,0:T(8,128)(2,1)S(1)} %bitcast.79, s32[2048]{0:T(1024)S(1)} %broadcast_clamp_fusion.3), kind=kCustom, calls=%fused_computation.4 | custom fusion | bytes 4202496 | tf_op jit(solution)/shard_map/gather | solution.py:140
  253.1 9.2 %gather_fusion.3 = bf16[2048,512]{1,0:T(8,128)(2,1)} fusion(bf16[2304,512]{1,0:T(8,128)(2,1)S(1)} %bitcast.80, s32[2048]{0:T(1024)S(1)} %broadcast_clamp_fusion.4), kind=kCustom, calls=%fused_computation.3 | custom fusion | bytes 4202496 | tf_op jit(solution)/shard_map/gather | solution.py:139
  262.2 5.4 %fusion.66 = (f32[2048]{0:T(1024)S(1)}, f32[2048,512]{1,0:T(8,128)S(1)}) fusion(bf16[512,512]{1,0:T(8,128)(2,1)} %param.40, bf16[2048,512]{1,0:T(8,128)(2,1)} %gather_fusion.5, bf16[2048,512]{1,0:T(8,128)(2,1)} %gather_fusion.4, bf16[2048,512]{1,0:T(8,128)(2,1)} %gather_fusion.3, f32[2048]{0:T(1024)S(1)} %bitcast.94, f32[2048]{0:T(1024)S(1)} %bitcast.95, ...), kind=kOutput, calls=%fused_computation.144 | convolution fusion | flops 1088419840 | bytes 11042816 | tf_op jit(solution)/shard_map/dot_general | solution.py:143
  267.6 0.8 multiply_reduce_fusion
  268.5 0.7 copy-done.1
  269.2 1.9 add_convert_fusion
  (54 shorter events, 0.3 us)
Async XLA Ops:
  0.6 194.1 %copy-start = (bf16[512,512]{1,0:T(8,128)(2,1)S(1)}, bf16[512,512]{1,0:T(8,128)(2,1)}, u32[]{:S(2)}) copy-start(bf16[512,512]{1,0:T(8,128)(2,1)} %param.37) | copy-start | bytes 1572868
  54.8 9.2 %copy-start.9 = (s32[1,128,32]{1,2,0:T(8,128)S(1)}, s32[1,128,32]{1,2,0:T(8,128)}, u32[]{:S(2)}) copy-start(s32[1,128,32]{1,2,0:T(8,128)} %param.29) | copy-start | bytes 49156
  58.9 23.4 %collective-permute-start = (f32[3,256,512]{2,1,0:T(8,128)}, f32[3,256,512]{2,1,0:T(8,128)S(1)}, u32[]{:S(2)}, u32[]{:S(2)}) collective-permute-start(f32[3,256,512]{2,1,0:T(8,128)} %get-tuple-element.55), channel_id=1, source_target_pairs={{31,0},{0,1},{1,2},{2,3},{3,4},{4,5},{5,6},{6,7},{7,8},{8,9},{9,10... | collective-permute-start | bytes 4718600 | tf_op jit(solution)/shard_map/ppermute | solution.py:10
  58.9 24.5 %collective-permute-start.1 = (f32[3,256,512]{2,1,0:T(8,128)}, f32[3,256,512]{2,1,0:T(8,128)}, u32[]{:S(2)}, u32[]{:S(2)}) collective-permute-start(f32[3,256,512]{2,1,0:T(8,128)} %get-tuple-element.56), channel_id=1, source_target_pairs={{1,0},{2,1},{3,2},{4,3},{5,4},{6,5},{7,6},{8,7},{9,8},{10,9},{11,1... | collective-permute-start | bytes 4718600 | tf_op jit(solution)/shard_map/ppermute | solution.py:10
  64.1 29.1 %copy-start.14 = (s32[1,128]{1,0:T(1,128)S(1)}, s32[1,128]{1,0:T(1,128)}, u32[]{:S(2)}) copy-start(s32[1,128]{1,0:T(1,128)} %param.30) | copy-start | bytes 1540
  64.1 39.6 %copy-start.10 = (s32[1,128,32]{1,2,0:T(8,128)S(1)}, s32[1,128,32]{1,2,0:T(8,128)}, u32[]{:S(2)}) copy-start(s32[1,128,32]{1,2,0:T(8,128)} %param.28) | copy-start | bytes 49156
  82.3 1.1 copy-start.2
  86.4 20.6 %copy-start.11 = (f32[512]{0:T(512)S(1)}, f32[512]{0:T(512)}, u32[]{:S(2)}) copy-start(f32[512]{0:T(512)} %param.41) | copy-start | bytes 6148
  86.4 21.8 %copy-start.4 = (bf16[512,512]{1,0:T(8,128)(2,1)S(1)}, bf16[512,512]{1,0:T(8,128)(2,1)}, u32[]{:S(2)}) copy-start(bf16[512,512]{1,0:T(8,128)(2,1)} %param.35) | copy-start | bytes 1572868
  87.2 16.7 %collective-permute-start.2 = (f32[256,512]{1,0:T(8,128)}, f32[256,512]{1,0:T(8,128)}, u32[]{:S(2)}, u32[]{:S(2)}) collective-permute-start(f32[256,512]{1,0:T(8,128)} %get-tuple-element.57), channel_id=1, source_target_pairs={{0,32},{32,64},{64,96},{1,33},{33,65},{65,97},{2,34},{34,66},{66,9... | collective-permute-start | bytes 1572872 | tf_op jit(solution)/shard_map/ppermute | solution.py:16
  91.9 13.0 %collective-permute-start.3 = (f32[256,512]{1,0:T(8,128)S(1)}, f32[256,512]{1,0:T(8,128)}, u32[]{:S(2)}, u32[]{:S(2)}) collective-permute-start(f32[256,512]{1,0:T(8,128)S(1)} %get-tuple-element.58), channel_id=1, source_target_pairs={{32,0},{64,32},{96,64},{33,1},{65,33},{97,65},{34,2},{66,34},{98,6... | collective-permute-start | bytes 1572872 | tf_op jit(solution)/shard_map/ppermute | solution.py:16
  94.1 31.7 %all-to-all-start = ((s32[128,1,32]{2,1,0:T(1,128)}), s32[128,1,32]{2,1,0:T(1,128)S(1)}, u32[]{:S(2)}, u32[]{:S(2)}) async-start(s32[128,1,32]{2,1,0:T(1,128)} %compare_select_fusion.2), calls=%async_computation | async-start | bytes 131072 | tf_op jit(solution)/shard_map/all_to_all | solution.py:115
  125.8 10.2 %copy-start.7 = (s32[2048,3]{0,1:T(4,128)S(1)}, s32[2048,3]{0,1:T(4,128)}, u32[]{:S(2)}) copy-start(s32[2048,3]{0,1:T(4,128)} %param.31) | copy-start | bytes 73732
  125.8 11.9 %copy-start.5 = (bf16[512,512]{1,0:T(8,128)(2,1)S(1)}, bf16[512,512]{1,0:T(8,128)(2,1)}, u32[]{:S(2)}) copy-start(bf16[512,512]{1,0:T(8,128)(2,1)} %param.36) | copy-start | bytes 1572868
  125.8 62.6 %all-to-all-start.1 = ((bf16[128,32,512]{2,1,0:T(8,128)(2,1)}), bf16[128,32,512]{2,1,0:T(8,128)(2,1)}, u32[]{:S(2)}, u32[]{:S(2)}) async-start(bf16[128,32,512]{2,1,0:T(8,128)(2,1)} %bitcast.82), calls=%async_computation.1 | async-start | bytes 8388608 | tf_op jit(solution)/shard_map/all_to_all | solution.py:114
  200.1 4.4 %copy-start.15 = (bf16[512,512]{1,0:T(8,128)(2,1)S(1)}, bf16[512,512]{1,0:T(8,128)(2,1)}, u32[]{:S(2)}) copy-start(bf16[512,512]{1,0:T(8,128)(2,1)} %param.38) | copy-start | bytes 1572868
  204.4 4.9 %copy-start.12 = (f32[512]{0:T(512)S(1)}, f32[512]{0:T(512)}, u32[]{:S(2)}) copy-start(f32[512]{0:T(512)} %param.42) | copy-start | bytes 6148
  204.4 5.1 %copy-start.6 = (bf16[512,512]{1,0:T(8,128)(2,1)S(1)}, bf16[512,512]{1,0:T(8,128)(2,1)}, u32[]{:S(2)}) copy-start(bf16[512,512]{1,0:T(8,128)(2,1)} %param.39) | copy-start | bytes 1572868
  209.1 10.9 %copy-start.8 = (f32[2048,3]{0,1:T(4,128)S(1)}, f32[2048,3]{0,1:T(4,128)}, u32[]{:S(2)}) copy-start(f32[2048,3]{0,1:T(4,128)} %param.32) | copy-start | bytes 73732
  209.5 34.4 %copy-start.3 = (bf16[256,512]{1,0:T(8,128)(2,1)}, bf16[256,512]{1,0:T(8,128)(2,1)S(1)}, u32[]{:S(2)}) copy-start(bf16[256,512]{1,0:T(8,128)(2,1)S(1)} %add_convert_fusion.5) | copy-start | bytes 786436
  209.8 7.9 %collective-permute-start.5 = (bf16[1,1,256,512]{3,2,1,0:T(8,128)(2,1)S(1)}, bf16[1,1,256,512]{3,2,1,0:T(8,128)(2,1)S(1)}, u32[]{:S(2)}, u32[]{:S(2)}) collective-permute-start(bf16[1,1,256,512]{3,2,1,0:T(8,128)(2,1)S(1)} %fusion.23), channel_id=1, source_target_pairs={{32,0},{64,32},{96,64},{0,96},{33,1},{65,33},{97,65},{1,97},{34,2}... | collective-permute-start | bytes 786440 | tf_op jit(solution)/shard_map/ppermute | solution.py:27
  210.5 8.8 %collective-permute-start.4 = (bf16[1,1,256,512]{3,2,1,0:T(8,128)(2,1)S(1)}, bf16[1,1,256,512]{3,2,1,0:T(8,128)(2,1)S(1)}, u32[]{:S(2)}, u32[]{:S(2)}) collective-permute-start(bf16[1,1,256,512]{3,2,1,0:T(8,128)(2,1)S(1)} %fusion.23), channel_id=1, source_target_pairs={{0,32},{32,64},{64,96},{96,0},{1,33},{33,65},{65,97},{97,1},{2,34}... | collective-permute-start | bytes 786440 | tf_op jit(solution)/shard_map/ppermute | solution.py:26
  219.4 9.8 %collective-permute-start.7 = (bf16[3,1,256,512]{3,2,1,0:T(8,128)(2,1)S(1)}, bf16[3,1,256,512]{3,2,1,0:T(8,128)(2,1)S(1)}, u32[]{:S(2)}, u32[]{:S(2)}) collective-permute-start(bf16[3,1,256,512]{3,2,1,0:T(8,128)(2,1)S(1)} %pad_maximum_fusion.1), channel_id=1, source_target_pairs={{1,0},{2,1},{3,2},{4,3},{5,4},{6,5},{7,6},{8,7},{9,8},{10,9},{11,1... | collective-permute-start | bytes 2359304 | tf_op jit(solution)/shard_map/ppermute | solution.py:27
  219.6 14.7 %collective-permute-start.6 = (bf16[3,1,256,512]{3,2,1,0:T(8,128)(2,1)S(1)}, bf16[3,1,256,512]{3,2,1,0:T(8,128)(2,1)S(1)}, u32[]{:S(2)}, u32[]{:S(2)}) collective-permute-start(bf16[3,1,256,512]{3,2,1,0:T(8,128)(2,1)S(1)} %pad_maximum_fusion.1), channel_id=1, source_target_pairs={{0,1},{1,2},{2,3},{3,4},{4,5},{5,6},{6,7},{7,8},{8,9},{9,10},{10,1... | collective-permute-start | bytes 2359304 | tf_op jit(solution)/shard_map/ppermute | solution.py:26
  267.6 1.6 copy-start.1
  267.6 1.6 copy-start.13
where the time goes:
time: 272 us; the launch traced here: 271 us
  local copies, waits for them, and re-layouts  92.2 us (34%)
  waiting for transfers between devices  74.3 us (27%)
  matrix products  48.3 us (18%)
  starting transfers between devices  33.5 us (12%)
  other arithmetic  21.7 us (8%)
    all_to_all x1, waiting for transfers between devices, on_device(): lax.all_to_all(sender_rows, ('lat', 'lon'), split_axis=0, concat_axis=0,...  33.5 us
    dot_general x4, matrix products, add_block(): lax.dot_general(onehot, msg_blk, (((0,), (0,)), ((), ())), preferred_elem...  26.8 us
    ppermute x2, waiting for transfers between devices, shifted(): return lax.ppermute(block, axis, route)  18.2 us
    gather x1, local copies, waits for them, and re-layouts, on_device(): hidden[local_src].astype(jnp.float32)  17.4 us
    gather x1, local copies, waits for them, and re-layouts, on_device(): sender_rows = sent_proj[mesh_src[0] - device_id * mesh_rows]  17.3 us
    gather x1, local copies, waits for them, and re-layouts, on_device(): near_proj = recv_proj[jnp.minimum(target_in, mesh_rows - 1)]  16.9 us
    ppermute x2, waiting for transfers between devices, padded(): after = lax.ppermute(leading, axis, down)  14.9 us
    all_to_all x1, starting transfers between devices, on_device(): lax.all_to_all(sender_rows, ('lat', 'lon'), split_axis=0, concat_axis=0,...  10.2 us
  transfers between devices with their start and end apart: 10, of which 7 were waited for; matrix products, arithmetic and copies ran while one was open for 15% of the time, Pallas kernels for 0%

commit v1 on v0

v1 whole, which is shorter than its diff:
```python
import functools

import jax
import jax.numpy as jnp
from jax import lax
from jax.experimental import pallas as pl
from jax.experimental.pallas import tpu as pltpu
from jax.sharding import PartitionSpec as P

BF16 = jnp.bfloat16
F32 = jnp.float32
LANES = 128
VMEM_LIMIT = 56 * 1024 * 1024
VMEM = pltpu.VMEM
SMEM = pltpu.SMEM


def silu(v):
    half = 0.5 * v
    return half + half * jnp.tanh(half)


def layer_norm(values):
    center = values - jnp.mean(values, axis=-1, keepdims=True)
    spread = jnp.mean(center * center, axis=-1, keepdims=True)
    return center * lax.rsqrt(spread + 1e-05)


def whole(space=VMEM):
    return pl.BlockSpec(memory_space=space)


def scatter_kernel(src_ref, dst_ref, wgt_ref, grid_ref, w_ref, *refs, unroll):
    outs, (y_ref, acc_a, acc_b) = refs[:3], refs[3:]
    rows, latent = grid_ref.shape
    parts = latent // LANES
    step = 256

    def project(i, carry):
        base = pl.multiple_of(i * step, step)
        y = silu(jnp.dot(grid_ref[pl.ds(base, step), :], w_ref[...], preferred_element_type=F32))
        for j in range(parts):
            y_ref[pl.ds(base * parts + j, step, stride=parts), :] = y[:, j * LANES : (j + 1) * LANES]
        return carry

    lax.fori_loop(0, rows // step, project, 0)

    slots = acc_a.shape[0] // parts
    zero = jnp.zeros((step * parts, LANES), F32)

    def clear(i, carry):
        base = pl.multiple_of(i * step * parts, step * parts)
        acc_a[pl.ds(base, step * parts), :] = zero
        acc_b[pl.ds(base, step * parts), :] = zero
        return carry

    lax.fori_loop(0, slots // step, clear, 0)

    edges = src_ref.shape[0]

    def add_edges(i, carry):
        for u in range(unroll):
            e = i * unroll + u
            acc = (acc_a, acc_b)[u % 2]
            s = pl.multiple_of(src_ref[e], parts)
            d = pl.multiple_of(dst_ref[e], parts)
            acc[pl.ds(d, parts), :] += wgt_ref[e] * y_ref[pl.ds(s, parts), :]
        return carry

    lax.fori_loop(0, edges // unroll, add_edges, 0)

    for n, out in enumerate(outs):
        per = out.shape[0]

        def emit(i, carry, n=n, out=out, per=per):
            base = pl.multiple_of(i * step, step)
            for j in range(parts):
                rows_j = pl.ds((n * per + base) * parts + j, step, stride=parts)
                total = acc_a[rows_j, :] + acc_b[rows_j, :]
                out[pl.ds(base, step), j * LANES : (j + 1) * LANES] = total.astype(out.dtype)
            return carry

        lax.fori_loop(0, per // step, emit, 0)


def scatter(src4, dst4, weight, grid_feat, w_in, slots):
    rows, latent = grid_feat.shape
    parts = latent // LANES
    out = jax.ShapeDtypeStruct((slots // 3, latent), BF16)
    return pl.pallas_call(
        functools.partial(scatter_kernel, unroll=16),
        out_shape=(out, out, out),
        in_specs=[whole(SMEM)] * 3 + [whole()] * 2,
        out_specs=(whole(),) * 3,
        scratch_shapes=[
            pltpu.VMEM((rows * parts, LANES), F32),
            pltpu.VMEM((slots * parts, LANES), F32),
            pltpu.VMEM((slots * parts, LANES), F32),
        ],
        compiler_params=pltpu.CompilerParams(vmem_limit_bytes=VMEM_LIMIT),
        name="grid_to_mesh",
    )(src4, dst4, weight, grid_feat, w_in)


def node_kernel(src_ref, a_ref, b_ref, c_ref, mesh_ref, w_enc, w_send, w_recv, gain, first_ref, q_ref, rows_ref, p_ref):
    @pl.when(pl.program_id(0) == 0)
    def _():
        pooled = a_ref[...].astype(F32) + b_ref[...].astype(F32) + c_ref[...].astype(F32)
        update = silu(jnp.dot(pooled.astype(BF16), w_enc[...], preferred_element_type=F32))
        first = (mesh_ref[...].astype(F32) + gain[...] * layer_norm(update)).astype(BF16)
        first_ref[...] = first
        p_ref[...] = jnp.dot(first, w_send[...], preferred_element_type=F32).astype(BF16)
        q_ref[...] = jnp.dot(first, w_recv[...], preferred_element_type=F32).astype(BF16)

    block = rows_ref.shape[0]
    nodes = p_ref.shape[0]
    picks = src_ref[0]
    table = (lax.broadcasted_iota(jnp.int32, (nodes, block), 0) == picks).astype(BF16)
    rows_ref[...] = lax.dot_general(
        table, p_ref[...], (((0,), (0,)), ((), ())), preferred_element_type=F32
    ).astype(BF16)


def node_stage(src, a, b, c, mesh_feat, w_enc, w_send, w_recv, gain):
    nodes, latent = mesh_feat.shape
    edges = src.size
    block = 512
    full = pl.BlockSpec((nodes, latent), lambda i: (0, 0))
    weight = pl.BlockSpec((latent, latent), lambda i: (0, 0))
    vec = pl.BlockSpec((1, latent), lambda i: (0, 0))
    return pl.pallas_call(
        node_kernel,
        grid=(edges // block,),
        out_shape=(
            jax.ShapeDtypeStruct((nodes, latent), BF16),
            jax.ShapeDtypeStruct((nodes, latent), BF16),
            jax.ShapeDtypeStruct((edges, latent), BF16),
        ),
        in_specs=[pl.BlockSpec((1, 1, block), lambda i: (i, 0, 0)), full, full, full, full, weight, weight, weight, vec],
        out_specs=(full, full, pl.BlockSpec((block, latent), lambda i: (i, 0))),
        scratch_shapes=[pltpu.VMEM((nodes, latent), BF16)],
        compiler_params=pltpu.CompilerParams(vmem_limit_bytes=VMEM_LIMIT),
        name="mesh_encoder",
    )(src.reshape(edges // block, 1, block), a, b, c, mesh_feat, w_enc, w_send, w_recv, gain.reshape(1, latent))


def edge_kernel(dst_ref, rows_ref, q_ref, first_ref, w_edge, w_node, w_dec, gain, mesh_ref, dec_ref, sum_ref):
    i = pl.program_id(0)

    @pl.when(i == 0)
    def _():
        sum_ref[...] = jnp.zeros_like(sum_ref)

    block = rows_ref.shape[0]
    nodes = q_ref.shape[0]
    table = (lax.broadcasted_iota(jnp.int32, (nodes, block), 0) == dst_ref[0]).astype(BF16)
    near = lax.dot_general(table, q_ref[...], (((0,), (0,)), ((), ())), preferred_element_type=F32)
    joined = silu(rows_ref[...].astype(F32) + near).astype(BF16)
    sum_ref[...] += jnp.dot(table, joined, preferred_element_type=F32)

    @pl.when(i == pl.num_programs(0) - 1)
    def _():
        pooled = jnp.dot(sum_ref[...].astype(BF16), w_edge[...], preferred_element_type=F32)
        update = silu(jnp.dot(pooled.astype(BF16), w_node[...], preferred_element_type=F32))
        out = (first_ref[...].astype(F32) + gain[...] * layer_norm(update)).astype(BF16)
        mesh_ref[...] = out
        dec_ref[...] = jnp.dot(out, w_dec[...], preferred_element_type=F32).astype(BF16)


def edge_stage(dst, rows, q, first, w_edge, w_node, w_dec, gain):
    nodes, latent = first.shape
    edges = rows.shape[0]
    block = 512
    full = pl.BlockSpec((nodes, latent), lambda i: (0, 0))
    weight = pl.BlockSpec((latent, latent), lambda i: (0, 0))
    vec = pl.BlockSpec((1, latent), lambda i: (0, 0))
    out = jax.ShapeDtypeStruct((nodes, latent), BF16)
    return pl.pallas_call(
        edge_kernel,
        grid=(edges // block,),
        out_shape=(out, out),
        in_specs=[
            pl.BlockSpec((1, 1, block), lambda i: (i, 0, 0)),
            pl.BlockSpec((block, latent), lambda i: (i, 0)),
            full, full, weight, weight, weight, vec,
        ],
        out_specs=(full, full),
        scratch_shapes=[pltpu.VMEM((nodes, latent), F32)],
        compiler_params=pltpu.CompilerParams(vmem_limit_bytes=VMEM_LIMIT),
        name="mesh_edges",
    )(dst.reshape(edges // block, 1, block), rows, q, first, w_edge, w_node, w_dec, gain.reshape(1, latent))


def table_kernel(slot_ref, wgt_ref, out_ref):
    rows, slots = out_ref.shape
    ids = lax.broadcasted_iota(jnp.int32, (rows, slots), 1)
    total = jnp.zeros((rows, slots), F32)
    for k in range(slot_ref.shape[1]):
        total += jnp.where(ids == slot_ref[:, k : k + 1], wgt_ref[:, k : k + 1], 0.0)
    out_ref[...] = total.astype(BF16)


def decoder_table(slot, weight, slots):
    rows, k = slot.shape
    block = 256
    return pl.pallas_call(
        table_kernel,
        grid=(rows // block,),
        out_shape=jax.ShapeDtypeStruct((rows, slots), BF16),
        in_specs=[pl.BlockSpec((block, k), lambda i: (i, 0))] * 2,
        out_specs=pl.BlockSpec((block, slots), lambda i: (i, 0)),
        compiler_params=pltpu.CompilerParams(vmem_limit_bytes=VMEM_LIMIT),
        cost_estimate=pl.CostEstimate(flops=9 * rows * slots, bytes_accessed=2 * rows * slots, transcendentals=0),
        name="decoder_table",
    )(slot, weight)


def grid_kernel(table_ref, a_ref, b_ref, c_ref, grid_ref, w_out, gain, out_ref):
    per = a_ref.shape[0]
    total = jnp.dot(table_ref[:, :per], a_ref[...], preferred_element_type=F32)
    total += jnp.dot(table_ref[:, per : 2 * per], b_ref[...], preferred_element_type=F32)
    total += jnp.dot(table_ref[:, 2 * per :], c_ref[...], preferred_element_type=F32)
    update = silu(jnp.dot(total.astype(BF16), w_out[...], preferred_element_type=F32))
    out_ref[...] = (grid_ref[...].astype(F32) + gain[...] * layer_norm(update)).astype(BF16)


def grid_stage(table, west, mid, east, grid_feat, w_out, gain):
    rows, latent = grid_feat.shape
    slots = table.shape[1]
    block = 256
    full = pl.BlockSpec((slots // 3, latent), lambda i: (0, 0))
    return pl.pallas_call(
        grid_kernel,
        grid=(rows // block,),
        out_shape=jax.ShapeDtypeStruct((rows, latent), BF16),
        in_specs=[
            pl.BlockSpec((block, slots), lambda i: (i, 0)),
            full, full, full,
            pl.BlockSpec((block, latent), lambda i: (i, 0)),
            pl.BlockSpec((latent, latent), lambda i: (0, 0)),
            pl.BlockSpec((1, latent), lambda i: (0, 0)),
        ],
        out_specs=pl.BlockSpec((block, latent), lambda i: (i, 0)),
        compiler_params=pltpu.CompilerParams(vmem_limit_bytes=VMEM_LIMIT),
        name="mesh_to_grid",
    )(table, west, mid, east, grid_feat, w_out, gain.reshape(1, latent))


def ring(block, axis, distance):
    size = lax.axis_size(axis)
    return lax.ppermute(block, axis, [(i, (i + distance) % size) for i in range(size)])


def on_device(
    grid_feat, mesh_feat, g2m_src, g2m_dst, g2m_weight, mesh_src, mesh_dst, mesh_count, m2g_src, m2g_weight,
    w_in, w_enc, w_send, w_recv, w_edge, w_node, w_dec, w_out, gain_enc, gain_node, gain_out,
):
    grid_rows, latent = grid_feat.shape
    nodes = mesh_feat.shape[0]
    parts = latent // LANES
    lon_count = lax.axis_size("lon")
    tiles = lax.axis_size("lat") * lon_count
    band = lax.axis_index("lat")
    sector = lax.axis_index("lon")
    tile = band * lon_count + sector

    def tile_slot(ids):
        owner = ids // nodes
        step_lat = owner // lon_count - band + 1
        step_lon = (owner % lon_count - sector + 1) % lon_count
        return (step_lon * 3 + step_lat) * nodes + ids % nodes

    src4 = (g2m_src - tile * grid_rows) * parts
    dst4 = tile_slot(g2m_dst) * parts
    west, own, east = scatter(src4, dst4, g2m_weight, grid_feat, w_in, 9 * nodes)
    from_west = ring(east, "lon", 1)
    from_east = ring(west, "lon", -1)
    column = own.astype(F32) + from_west.astype(F32) + from_east.astype(F32)
    below = column[:nodes].astype(BF16)
    above = column[2 * nodes :].astype(BF16)
    center = column[nodes : 2 * nodes]
    from_below = ring(above, "lat", 1)
    from_above = ring(below, "lat", -1)

    capacity = mesh_src.shape[2]
    live = lax.broadcasted_iota(jnp.int32, (tiles, capacity), 1) < mesh_count[0][:, None]
    targets = jnp.where(live, mesh_dst[0] % nodes, nodes)
    target_in = lax.all_to_all(targets, ("lat", "lon"), split_axis=0, concat_axis=0, tiled=True)

    first, q, rows = node_stage(
        mesh_src[0] - tile * nodes, center, from_below, from_above, mesh_feat, w_enc, w_send, w_recv, gain_enc
    )
    rows_in = lax.all_to_all(
        rows.reshape(tiles, capacity, latent), ("lat", "lon"), split_axis=0, concat_axis=0, tiled=True
    ).reshape(tiles * capacity, latent)
    table = decoder_table(tile_slot(m2g_src), m2g_weight, 9 * nodes)

    mesh_out, decoded = edge_stage(target_in, rows_in, q, first, w_edge, w_node, w_dec, gain_node)

    mid = jnp.concatenate([ring(decoded, "lat", 1), decoded, ring(decoded, "lat", -1)], axis=0)
    grid_out = grid_stage(table, ring(mid, "lon", 1), mid, ring(mid, "lon", -1), grid_feat, w_out, gain_out)
    return (grid_out, mesh_out)


def solution(mesh):
    tile = ("lat", "lon")
    rows, flat, cube = P(tile, None), P(tile), P(tile, None, None)
    return jax.shard_map(
        on_device,
        mesh=mesh,
        in_specs=(rows, rows, flat, flat, flat, cube, cube, rows, rows, rows) + (P(),) * 11,
        out_specs=(rows, rows),
        check_vma=False,
    )
```

time: 272 us -> 179 us (0.66)
  local copies, waits for them, and re-layouts: 92.2 us -> 7.83 us
  Pallas kernels: 0 us -> 61.6 us
  matrix products: 48.3 us -> 0 us
  other arithmetic: 21.7 us -> 8.01 us
  waiting for transfers between devices: 74.3 us -> 66.2 us
    gather x6 -> x0, local copies, waits for them, and re-layouts: 79.1 us -> none  [the longest x1 17.4 us: on_device(): hidden[local_src].astype(jnp.float32)]
    pallas_call x0 -> x5, Pallas kernels: none -> 61.6 us  [the longest x1 17.3 us: scatter(): pl.pallas_call(functools.partial(scatter_kernel, unroll=16), out_shape=(o...]
    dot_general x12 -> x0, matrix products: 48.3 us -> none  [the longest x4 26.8 us: add_block(): lax.dot_general(onehot, msg_blk, (((0,), (0,)), ((), ())), preferred_elem...]
    ppermute x8, waiting for transfers between devices: 40.8 us -> 15.8 us  [ring(): lax.ppermute(block, axis, [(i, (i + distance) % size) for i in range(size)])]
    all_to_all x1, waiting for transfers between devices: 33.5 us -> 50.4 us  [on_device(): lax.all_to_all(rows.reshape(tiles, capacity, latent), ('lat', 'lon'), spl...]
    convert_element_type x5 -> x0, other arithmetic: 13.6 us -> none  [the longest x1 6.3 us: on_device(): jax.nn.silu(rows_in.astype(jnp.float32) + near_proj).astype(jnp.bfloat16)]
    squeeze x2 -> x0, local copies, waits for them, and re-layouts: 5 us -> none  [the longest x1 4.14 us: on_device(): pieces[:, 2]]
    convert_element_type x1 -> x0, local copies, waits for them, and re-layouts: 4.37 us -> none  [on_device(): jnp.einsum('pcd,de->pce', joined, w_edge, preferred_element_type=jnp.floa...]
  transfers between devices with their start and end apart: 10 -> 10, of which waited for: 7 -> 3; matrix products, arithmetic and copies ran while one was open for 15% -> 6% of each run, Pallas kernels for 0% -> 12%
where the time goes in v1:
time: 179 us; the launch traced here: 177 us
  waiting for transfers between devices  66.2 us (37%)
  Pallas kernels  61.6 us (34%)
  starting transfers between devices  32.6 us (18%)
  other arithmetic  8.01 us (4%)
  local copies, waits for them, and re-layouts  7.83 us (4%)
    all_to_all x1, waiting for transfers between devices, on_device(): lax.all_to_all(rows.reshape(tiles, capacity, latent), ('lat', 'lon'), spl...  50.4 us
    pallas_call x1, Pallas kernels, scatter(): pl.pallas_call(functools.partial(scatter_kernel, unroll=16), out_shape=(o...  17.3 us
    ppermute x8, waiting for transfers between devices, ring(): lax.ppermute(block, axis, [(i, (i + distance) % size) for i in range(size)])  15.8 us
    pallas_call x1, Pallas kernels, grid_stage(): pl.pallas_call(grid_kernel, grid=(rows // block,), out_shape=jax.ShapeDty...  13.4 us
    ppermute x8, starting transfers between devices, ring(): lax.ppermute(block, axis, [(i, (i + distance) % size) for i in range(size)])  13.1 us
    pallas_call x1, Pallas kernels, decoder_table(): pl.pallas_call(table_kernel, grid=(rows // block,), out_shape=jax.ShapeDt...  12.5 us
    pallas_call x1, Pallas kernels, edge_stage(): pl.pallas_call(edge_kernel, grid=(edges // block,), out_shape=(out, out),...  10.5 us
    all_to_all x1, starting transfers between devices, on_device(): lax.all_to_all(rows.reshape(tiles, capacity, latent), ('lat', 'lon'), spl...  10.3 us
  transfers between devices with their start and end apart: 10, of which 3 were waited for; matrix products, arithmetic and copies ran while one was open for 6% of the time, Pallas kernels for 12%

profile of v1, /device:TPU:0, one launch (start us, length us, event | category | flops | bytes accessed | tf_op | source)
XLA Modules:
  0.0 177.0 jit_solution(7078508977569226640)
XLA Ops:
  0.6 0.0 copy-start.6
  0.6 1.4 fusion.20
  2.0 17.3 %grid_to_mesh.1 = (bf16[768,512]{1,0:T(8,128)(2,1)}, bf16[768,512]{1,0:T(8,128)(2,1)}, bf16[768,512]{1,0:T(8,128)(2,1)}) custom-call(s32[4096]{0:T(1024)} %get-tuple-element.23.src_ref, s32[4096]{0:T(1024)} %get-tuple-element.22.dst_ref, f32[4096]{0:T(1024)} %wgt_ref.2, bf16[2048,512]{1,0:T(8,128)(2,1)} %grid_ref.3, bf16[512,512]{1,0:T(8,128)(2,1)} %w_ref.1), custom_call_target="tpu_custom_call" | custom-call | tf_op jit(solution)/shard_map/grid_to_mesh/pallas_call | solution.py:90
  19.3 0.0 collective-permute-start
  19.4 5.1 %collective-permute-start.1 = (bf16[768,512]{1,0:T(8,128)(2,1)}, bf16[768,512]{1,0:T(8,128)(2,1)S(1)}, u32[]{:S(2)}, u32[]{:S(2)}) collective-permute-start(bf16[768,512]{1,0:T(8,128)(2,1)} %get-tuple-element.12), channel_id=1, source_target_pairs={{0,31},{1,0},{2,1},{3,2},{4,3},{5,4},{6,5},{7,6},{8,7},{9,8},{10,9... | collective-permute-start | bytes 2359304 | tf_op jit(solution)/shard_map/ppermute | solution.py:251
  24.4 0.0 copy-done.6
  24.4 0.1 copy.66
  24.5 9.8 %collective-permute-done = bf16[768,512]{1,0:T(8,128)(2,1)S(1)} collective-permute-done((bf16[768,512]{1,0:T(8,128)(2,1)}, bf16[768,512]{1,0:T(8,128)(2,1)S(1)}, u32[]{:S(2)}, u32[]{:S(2)}) %collective-permute-start) | collective-permute-done | bytes 786464 | tf_op jit(solution)/shard_map/ppermute | solution.py:251
  34.3 0.0 collective-permute-done.1
  34.3 0.0 copy-start.8
  34.3 0.0 copy-start.7
  34.3 1.5 fusion.26
  35.9 4.2 %collective-permute-start.3 = (bf16[256,512]{1,0:T(8,128)(2,1)S(1)}, bf16[256,512]{1,0:T(8,128)(2,1)S(1)}, u32[]{:S(2)}, u32[]{:S(2)}) collective-permute-start(bf16[256,512]{1,0:T(8,128)(2,1)S(1)} %get-tuple-element.20), channel_id=1, source_target_pairs={{0,96},{32,0},{64,32},{96,64},{1,97},{33,1},{65,33},{97,65},{2,98}... | collective-permute-start | bytes 786440 | tf_op jit(solution)/shard_map/ppermute | solution.py:251
  40.1 0.0 collective-permute-start.2
  40.1 0.0 copy-done.8
  40.1 0.8 compare_select_fusion.2
  40.9 9.1 %all-to-all-start = ((s32[128,1,32]{2,1,0:T(1,128)}), s32[128,1,32]{2,1,0:T(1,128)S(1)}, u32[]{:S(2)}, u32[]{:S(2)}) async-start(s32[128,1,32]{2,1,0:T(1,128)} %compare_select_fusion.2), calls=%async_computation | async-start | bytes 131072 | tf_op jit(solution)/shard_map/all_to_all | solution.py:288
  50.0 0.0 copy-done.7
  50.1 0.1 copy.67
  50.2 0.7 sub.83.src_ref
  50.9 0.8 slice.14.a_ref
  51.7 0.0 collective-permute-done.3.c_ref
  51.7 0.0 copy-start.2
  51.7 0.0 collective-permute-done.2.b_ref
  51.7 0.0 copy-start.3
  51.7 0.7 copy-done.2
  52.4 0.1 copy-done.3
  52.5 7.9 %mesh_encoder.1 = (bf16[256,512]{1,0:T(8,128)(2,1)}, bf16[256,512]{1,0:T(8,128)(2,1)}, bf16[4096,512]{1,0:T(8,128)(2,1)}) custom-call(s32[8,1,512]{2,1,0:T(1,128)} %sub.83.src_ref, f32[256,512]{1,0:T(8,128)} %slice.14.a_ref, bf16[256,512]{1,0:T(8,128)(2,1)} %copy-done.3, bf16[256,512]{1,0:T(8,128)(2,1)} %copy-done.2, bf16[256,512]{1,0:T(8,128)(2,1)} %mesh_ref.1, ...), custom_call_target="tpu_custom_call" | custom-call | tf_op jit(solution)/shard_map/mesh_encoder/pallas_call | solution.py:131
  60.4 0.0 all-to-all-done
  60.4 10.3 %all-to-all-start.1 = ((bf16[128,32,512]{2,1,0:T(8,128)(2,1)}), bf16[128,32,512]{2,1,0:T(8,128)(2,1)}, u32[]{:S(2)}, u32[]{:S(2)}) async-start(bf16[128,32,512]{2,1,0:T(8,128)(2,1)} %bitcast.7), calls=%async_computation.1 | async-start | bytes 8388608 | tf_op jit(solution)/shard_map/all_to_all | solution.py:293
  70.7 0.5 broadcast.140
  71.2 0.8 reduce.3
  72.0 0.7 reshape.135.dst_ref
  72.7 50.4 %all-to-all-done.1 = bf16[128,32,512]{2,1,0:T(8,128)(2,1)} async-done(((bf16[128,32,512]{2,1,0:T(8,128)(2,1)}), bf16[128,32,512]{2,1,0:T(8,128)(2,1)}, u32[]{:S(2)}, u32[]{:S(2)}) %all-to-all-start.1) | async-done | bytes 4194336 | tf_op jit(solution)/shard_map/all_to_all | solution.py:293
  123.1 10.5 %mesh_edges.1 = (bf16[256,512]{1,0:T(8,128)(2,1)}, bf16[256,512]{1,0:T(8,128)(2,1)}) custom-call(s32[8,1,512]{2,1,0:T(1,128)} %reshape.135.dst_ref, bf16[4096,512]{1,0:T(8,128)(2,1)} %bitcast.4.rows_ref, bf16[256,512]{1,0:T(8,128)(2,1)} %get-tuple-element.14.q_ref, bf16[256,512]{1,0:T(8,128)(2,1)} %get-tuple-element.15.first_ref, bf16[512,512]{1,0:T(8,128)(2,1)} %w_edge.1, ...), custom_call_target="tpu_custom_call" | custom-call | tf_op jit(solution)/shard_map/mesh_edges/pallas_call | solution.py:178
  133.6 0.0 copy-start.4
  133.6 0.0 copy-start.5
  133.6 0.4 collective-permute-start.4
  134.0 2.9 %collective-permute-start.5 = (bf16[256,512]{1,0:T(8,128)(2,1)}, bf16[256,512]{1,0:T(8,128)(2,1)S(1)}, u32[]{:S(2)}, u32[]{:S(2)}) collective-permute-start(bf16[256,512]{1,0:T(8,128)(2,1)} %get-tuple-element.16), channel_id=1, source_target_pairs={{0,96},{32,0},{64,32},{96,64},{1,97},{33,1},{65,33},{97,65},{2,98}... | collective-permute-start | bytes 786440 | tf_op jit(solution)/shard_map/ppermute | solution.py:251
  136.9 6.0 %collective-permute-done.4 = bf16[256,512]{1,0:T(8,128)(2,1)S(1)} collective-permute-done((bf16[256,512]{1,0:T(8,128)(2,1)}, bf16[256,512]{1,0:T(8,128)(2,1)S(1)}, u32[]{:S(2)}, u32[]{:S(2)}) %collective-permute-start.4) | collective-permute-done | bytes 262176 | tf_op jit(solution)/shard_map/ppermute | solution.py:251
  142.9 1.0 constant_dynamic-update-slice_fusion.1
  143.9 0.0 collective-permute-done.5
  143.9 0.0 copy-start
  143.9 0.2 collective-permute-start.7
  144.1 0.4 collective-permute-start.6
  144.5 0.0 copy-done.4
  144.5 0.4 copy.57
  144.9 0.5 copy.62
  145.4 0.0 copy-done.5
  145.4 1.4 copy.65.wgt_ref
  146.8 3.4 %fusion.6.slot_ref = s32[2048,3]{1,0:T(8,128)} fusion(pred[2048,3]{1,0:T(8,128)(4,1)S(1)} %copy.62, s32[2048,3]{1,0:T(8,128)S(1)} %copy.57, s32[]{:T(128)S(6)} %axis_index.25, s32[]{:T(128)S(6)} %axis_index.22), kind=kLoop, calls=%fused_computation.20 | loop fusion | flops 344064 | bytes 55304 | tf_op jit(solution)/shard_map/add | solution.py:271
  150.2 0.0 copy-done
  150.2 12.5 %decoder_table.1.table_ref = bf16[2048,2304]{1,0:T(8,128)(2,1)} custom-call(s32[2048,3]{1,0:T(8,128)} %fusion.6.slot_ref, f32[2048,3]{1,0:T(8,128)} %copy.65.wgt_ref), custom_call_target="tpu_custom_call" | custom-call | flops 42467328 | bytes 9437184 | tf_op jit(solution)/shard_map/decoder_table/pallas_call | solution.py:206
  162.7 0.0 collective-permute-done.7.c_ref
  162.8 0.0 copy-start.1
  162.8 0.0 collective-permute-done.6.a_ref
  162.8 0.9 copy-done.1
  163.6 13.4 %mesh_to_grid.1 = bf16[2048,512]{1,0:T(8,128)(2,1)} custom-call(bf16[2048,2304]{1,0:T(8,128)(2,1)} %decoder_table.1.table_ref, bf16[768,512]{1,0:T(8,128)(2,1)} %collective-permute-done.6.a_ref, bf16[768,512]{1,0:T(8,128)(2,1)} %copy-done, bf16[768,512]{1,0:T(8,128)(2,1)} %copy-done.1, bf16[2048,512]{1,0:T(8,128)(2,1)} %grid_ref.3, bf16[512,512]{1,0:T(8,128)(2,1)} %w_out.1, ...), custom_call_target="tpu_custom_call" | custom-call | tf_op jit(solution)/shard_map/mesh_to_grid/pallas_call | solution.py:232
  (5 shorter events, 0.1 us)
Async XLA Ops:
  0.6 23.8 %copy-start.6 = (s32[1,128,32]{1,2,0:T(8,128)S(1)}, s32[1,128,32]{1,2,0:T(8,128)}, u32[]{:S(2)}) copy-start(s32[1,128,32]{1,2,0:T(8,128)} %param.27) | copy-start | bytes 49156
  19.3 14.9 %collective-permute-start = (bf16[768,512]{1,0:T(8,128)(2,1)}, bf16[768,512]{1,0:T(8,128)(2,1)S(1)}, u32[]{:S(2)}, u32[]{:S(2)}) collective-permute-start(bf16[768,512]{1,0:T(8,128)(2,1)} %get-tuple-element.11), channel_id=1, source_target_pairs={{0,1},{1,2},{2,3},{3,4},{4,5},{5,6},{6,7},{7,8},{8,9},{9,10},{10,1... | collective-permute-start | bytes 2359304 | tf_op jit(solution)/shard_map/ppermute | solution.py:251
  19.4 14.9 %collective-permute-start.1 = (bf16[768,512]{1,0:T(8,128)(2,1)}, bf16[768,512]{1,0:T(8,128)(2,1)S(1)}, u32[]{:S(2)}, u32[]{:S(2)}) collective-permute-start(bf16[768,512]{1,0:T(8,128)(2,1)} %get-tuple-element.12), channel_id=1, source_target_pairs={{0,31},{1,0},{2,1},{3,2},{4,3},{5,4},{6,5},{7,6},{8,7},{9,8},{10,9... | collective-permute-start | bytes 2359304 | tf_op jit(solution)/shard_map/ppermute | solution.py:251
  34.3 5.8 %copy-start.8 = (s32[1,128]{1,0:T(1,128)S(1)}, s32[1,128]{1,0:T(1,128)}, u32[]{:S(2)}) copy-start(s32[1,128]{1,0:T(1,128)} %param.28) | copy-start | bytes 1540
  34.3 15.8 %copy-start.7 = (s32[1,128,32]{1,2,0:T(8,128)S(1)}, s32[1,128,32]{1,2,0:T(8,128)}, u32[]{:S(2)}) copy-start(s32[1,128,32]{1,2,0:T(8,128)} %param.26) | copy-start | bytes 49156
  35.9 15.8 %collective-permute-start.3 = (bf16[256,512]{1,0:T(8,128)(2,1)S(1)}, bf16[256,512]{1,0:T(8,128)(2,1)S(1)}, u32[]{:S(2)}, u32[]{:S(2)}) collective-permute-start(bf16[256,512]{1,0:T(8,128)(2,1)S(1)} %get-tuple-element.20), channel_id=1, source_target_pairs={{0,96},{32,0},{64,32},{96,64},{1,97},{33,1},{65,33},{97,65},{2,98}... | collective-permute-start | bytes 786440 | tf_op jit(solution)/shard_map/ppermute | solution.py:251
  40.1 11.6 %collective-permute-start.2 = (bf16[256,512]{1,0:T(8,128)(2,1)S(1)}, bf16[256,512]{1,0:T(8,128)(2,1)S(1)}, u32[]{:S(2)}, u32[]{:S(2)}) collective-permute-start(bf16[256,512]{1,0:T(8,128)(2,1)S(1)} %get-tuple-element.21), channel_id=1, source_target_pairs={{0,32},{32,64},{64,96},{96,0},{1,33},{33,65},{65,97},{97,1},{2,34}... | collective-permute-start | bytes 786440 | tf_op jit(solution)/shard_map/ppermute | solution.py:251
  40.9 19.5 %all-to-all-start = ((s32[128,1,32]{2,1,0:T(1,128)}), s32[128,1,32]{2,1,0:T(1,128)S(1)}, u32[]{:S(2)}, u32[]{:S(2)}) async-start(s32[128,1,32]{2,1,0:T(1,128)} %compare_select_fusion.2), calls=%async_computation | async-start | bytes 131072 | tf_op jit(solution)/shard_map/all_to_all | solution.py:288
  51.7 0.7 copy-start.2
  51.7 0.8 copy-start.3
  60.4 62.7 %all-to-all-start.1 = ((bf16[128,32,512]{2,1,0:T(8,128)(2,1)}), bf16[128,32,512]{2,1,0:T(8,128)(2,1)}, u32[]{:S(2)}, u32[]{:S(2)}) async-start(bf16[128,32,512]{2,1,0:T(8,128)(2,1)} %bitcast.7), calls=%async_computation.1 | async-start | bytes 8388608 | tf_op jit(solution)/shard_map/all_to_all | solution.py:293
  133.6 10.9 %copy-start.4 = (s32[2048,3]{0,1:T(4,128)S(1)}, s32[2048,3]{0,1:T(4,128)}, u32[]{:S(2)}) copy-start(s32[2048,3]{0,1:T(4,128)} %param.29) | copy-start | bytes 73732
  133.6 11.8 %copy-start.5 = (f32[2048,3]{0,1:T(4,128)S(1)}, f32[2048,3]{0,1:T(4,128)}, u32[]{:S(2)}) copy-start(f32[2048,3]{0,1:T(4,128)} %param.30) | copy-start | bytes 73732
  133.6 9.3 %collective-permute-start.4 = (bf16[256,512]{1,0:T(8,128)(2,1)}, bf16[256,512]{1,0:T(8,128)(2,1)S(1)}, u32[]{:S(2)}, u32[]{:S(2)}) collective-permute-start(bf16[256,512]{1,0:T(8,128)(2,1)} %get-tuple-element.16), channel_id=1, source_target_pairs={{0,32},{32,64},{64,96},{96,0},{1,33},{33,65},{65,97},{97,1},{2,34}... | collective-permute-start | bytes 786440 | tf_op jit(solution)/shard_map/ppermute | solution.py:251
  134.0 9.9 %collective-permute-start.5 = (bf16[256,512]{1,0:T(8,128)(2,1)}, bf16[256,512]{1,0:T(8,128)(2,1)S(1)}, u32[]{:S(2)}, u32[]{:S(2)}) collective-permute-start(bf16[256,512]{1,0:T(8,128)(2,1)} %get-tuple-element.16), channel_id=1, source_target_pairs={{0,96},{32,0},{64,32},{96,64},{1,97},{33,1},{65,33},{97,65},{2,98}... | collective-permute-start | bytes 786440 | tf_op jit(solution)/shard_map/ppermute | solution.py:251
  143.9 6.3 %copy-start = (bf16[768,512]{1,0:T(8,128)(2,1)}, bf16[768,512]{1,0:T(8,128)(2,1)S(1)}, u32[]{:S(2)}) copy-start(bf16[768,512]{1,0:T(8,128)(2,1)S(1)} %constant_dynamic-update-slice_fusion.b_ref) | copy-start | bytes 2359300
  143.9 18.8 %collective-permute-start.7 = (bf16[768,512]{1,0:T(8,128)(2,1)S(1)}, bf16[768,512]{1,0:T(8,128)(2,1)S(1)}, u32[]{:S(2)}, u32[]{:S(2)}) collective-permute-start(bf16[768,512]{1,0:T(8,128)(2,1)S(1)} %constant_dynamic-update-slice_fusion.b_ref), channel_id=1, source_target_pairs={{0,31},{1,0},{2,1},{3,2},{4,3},{5,4},{6,5},{7,6},{8,7},{9,8},{10,9... | collective-permute-start | bytes 2359304 | tf_op jit(solution)/shard_map/ppermute | solution.py:251
  144.1 18.6 %collective-permute-start.6 = (bf16[768,512]{1,0:T(8,128)(2,1)S(1)}, bf16[768,512]{1,0:T(8,128)(2,1)}, u32[]{:S(2)}, u32[]{:S(2)}) collective-permute-start(bf16[768,512]{1,0:T(8,128)(2,1)S(1)} %constant_dynamic-update-slice_fusion.b_ref), channel_id=1, source_target_pairs={{0,1},{1,2},{2,3},{3,4},{4,5},{5,6},{6,7},{7,8},{8,9},{9,10},{10,1... | collective-permute-start | bytes 2359304 | tf_op jit(solution)/shard_map/ppermute | solution.py:251
  162.8 0.9 copy-start.1

commit v2 on v1

v2 whole, which is shorter than its diff:
```python
import functools

import jax
import jax.numpy as jnp
from jax import lax
from jax.experimental import pallas as pl
from jax.experimental.pallas import tpu as pltpu
from jax.sharding import PartitionSpec as P

BF16 = jnp.bfloat16
F32 = jnp.float32
LANES = 128
MARKS = 8
MIB = 1024 * 1024
VMEM = pltpu.VMEM
SMEM = pltpu.SMEM
HBM = pltpu.HBM


def silu(v):
    half = 0.5 * v
    return half + half * jnp.tanh(half)


def layer_norm(values):
    center = values - jnp.mean(values, axis=-1, keepdims=True)
    spread = jnp.mean(center * center, axis=-1, keepdims=True)
    return center * lax.rsqrt(spread + 1e-05)


def whole(space=VMEM):
    return pl.BlockSpec(memory_space=space)


NEAR_A, NEAR_B, FAR_A, FAR_B, NEAR, FAR, A, OWN, B = range(9)
BY_PLACE = (NEAR_A, NEAR, NEAR_B, A, OWN, B, FAR_A, FAR, FAR_B)


def around_index(owner, band, sector, lon_count):
    step_lat = lax.shift_right_logical(owner, lon_count.bit_length() - 1) - band
    step_lon = ((owner - sector + 1) & (lon_count - 1)) - 1
    lat_at = 1 + step_lat * (2 * (band & 1) - 1)
    lon_at = 1 + step_lon * (2 * (sector & 1) - 1)
    place = lon_at * 3 + lat_at
    index = jnp.zeros_like(place)
    for at, tile in enumerate(BY_PLACE):
        if tile:
            index = jnp.where(place == at, tile, index)
    return index


def scatter_kernel(where_ref, src_hbm, dst_hbm, wgt_hbm, grid_hbm, w_hbm, *refs, nodes, lon_count):
    outs = refs[:5]
    accs = refs[5:9]
    y_ref, grid_ref, w_ref, src_v, dst_v, src_s, dst_s, wgt_s, grid_sem, sem = refs[9:]
    rows, latent = grid_ref.shape
    parts = latent // LANES
    step = 256
    chunks = rows // step

    def grid_copy(i):
        part = pl.ds(pl.multiple_of(i * step, step), step)
        return pltpu.make_async_copy(grid_hbm.at[part], grid_ref.at[part], grid_sem.at[i])

    src_in = pltpu.make_async_copy(src_hbm, src_v, sem.at[0])
    dst_in = pltpu.make_async_copy(dst_hbm, dst_v, sem.at[1])
    wgt_in = pltpu.make_async_copy(wgt_hbm, wgt_s, sem.at[2])
    w_in = pltpu.make_async_copy(w_hbm, w_ref, sem.at[3])
    for copy in (src_in, dst_in, wgt_in, w_in):
        copy.start()
    for i in range(chunks):
        grid_copy(i).start()
    band, sector, tile = where_ref[0], where_ref[1], where_ref[2]
    src_in.wait()
    src_v[...] = (src_v[...] - tile * rows) * parts
    src_out = pltpu.make_async_copy(src_v, src_s, sem.at[4])
    src_out.start()
    dst_in.wait()
    dst = dst_v[...]
    shift = nodes.bit_length() - 1
    index = around_index(lax.shift_right_logical(dst, shift), band, sector, lon_count)
    dst_v[...] = (index * nodes + (dst & (nodes - 1))) * parts
    dst_out = pltpu.make_async_copy(dst_v, dst_s, sem.at[5])
    dst_out.start()
    w_in.wait()

    span = accs[0].shape[0] // chunks
    zero = jnp.zeros((span, LANES), F32)

    def project(i, carry):
        grid_copy(i).wait()
        base = pl.multiple_of(i * step, step)
        y = silu(jnp.dot(grid_ref[pl.ds(base, step), :], w_ref[...], preferred_element_type=F32))
        for j in range(parts):
            y_ref[pl.ds(base * parts + j, step, stride=parts), :] = y[:, j * LANES : (j + 1) * LANES]
        for acc in accs:
            acc[pl.ds(pl.multiple_of(i * span, span), span), :] = zero
        return carry

    lax.fori_loop(0, chunks, project, 0)
    wgt_in.wait()
    src_out.wait()
    dst_out.wait()

    count = len(accs)
    lines, width = src_s.shape

    def add_edges(i, carry):
        for u in range(0, width, count):
            places, sums = [], []
            for n, acc in enumerate(accs):
                s = pl.multiple_of(src_s[i, u + n], parts)
                d = pl.multiple_of(dst_s[i, u + n], parts)
                places.append(d)
                sums.append(acc[pl.ds(d, parts), :] + wgt_s[i, u + n] * y_ref[pl.ds(s, parts), :])
            for acc, d, total in zip(accs, places, sums):
                acc[pl.ds(d, parts), :] = total
        return carry

    lax.fori_loop(0, lines, add_edges, 0)

    start = 0
    for out in outs:
        per = out.shape[0]

        def emit(i, carry, start=start, out=out):
            base = pl.multiple_of(i * step, step)
            for j in range(parts):
                rows_j = pl.ds((start + base) * parts + j, step, stride=parts)
                total = (accs[0][rows_j, :] + accs[1][rows_j, :]) + (accs[2][rows_j, :] + accs[3][rows_j, :])
                out[pl.ds(base, step), j * LANES : (j + 1) * LANES] = total.astype(out.dtype)
            return carry

        lax.fori_loop(0, per // step, emit, 0)
        start += per


def scatter(where, src, dst, weight, grid_feat, w_in, nodes, lon_count):
    rows, latent = grid_feat.shape
    parts = latent // LANES
    slots = 9 * nodes
    lines = src.shape[0] // LANES
    outs = tuple(jax.ShapeDtypeStruct((n * nodes, latent), BF16) for n in (2, 2, 1, 1, 3))
    ints = pltpu.VMEM((lines, LANES), jnp.int32)
    return pl.pallas_call(
        functools.partial(scatter_kernel, nodes=nodes, lon_count=lon_count),
        out_shape=outs,
        in_specs=[whole(SMEM)] + [whole(HBM)] * 5,
        out_specs=(whole(),) * 5,
        scratch_shapes=[pltpu.VMEM((slots * parts, LANES), F32)] * 4
        + [
            pltpu.VMEM((rows * parts, LANES), F32),
            pltpu.VMEM((rows, latent), BF16),
            pltpu.VMEM(w_in.shape, BF16),
            ints,
            ints,
            pltpu.SMEM((lines, LANES), jnp.int32),
            pltpu.SMEM((lines, LANES), jnp.int32),
            pltpu.SMEM((lines, LANES), F32),
            pltpu.SemaphoreType.DMA((rows // 256,)),
            pltpu.SemaphoreType.DMA((6,)),
        ],
        compiler_params=pltpu.CompilerParams(vmem_limit_bytes=60 * MIB),
        name="grid_to_mesh",
    )(where, *(v.reshape(lines, LANES) for v in (src, dst, weight)), grid_feat, w_in)


def column_kernel(own_ref, near_ref, far_ref, a_ref, b_ref):
    nodes = a_ref.shape[0]
    for n, out in enumerate((a_ref, b_ref)):
        part = slice(n * nodes, (n + 1) * nodes)
        mine = own_ref[2 * n * nodes : (2 * n + 1) * nodes, :].astype(F32)
        out[...] = (mine + near_ref[part, :].astype(F32) + far_ref[part, :].astype(F32)).astype(BF16)


def column_sums(own, near, far):
    nodes, latent = own.shape[0] // 3, own.shape[1]
    out = jax.ShapeDtypeStruct((nodes, latent), BF16)
    return pl.pallas_call(
        column_kernel,
        out_shape=(out, out),
        in_specs=[whole()] * 3,
        out_specs=(whole(),) * 2,
        compiler_params=pltpu.CompilerParams(vmem_limit_bytes=8 * MIB),
        name="column_sums",
    )(own, near, far)


def node_kernel(src_ref, mark_ref, own_ref, a_ref, b_ref, near_ref, far_ref, mesh_ref, enc_hbm, send_hbm, recv_hbm, gain, first_ref, q_ref, rows_hbm, rows_ref, w_enc, w_send, w_recv, sem, w_sem):
    tiles, _, _ = rows_ref.shape
    capacity = (rows_ref.shape[1] - MARKS) * LANES // mesh_ref.shape[1]
    parts = mesh_ref.shape[1] // LANES
    loads = [
        pltpu.make_async_copy(hbm, ref, w_sem.at[n])
        for n, (hbm, ref) in enumerate(((enc_hbm, w_enc), (send_hbm, w_send), (recv_hbm, w_recv)))
    ]
    for load in loads:
        load.start()
    nodes = mesh_ref.shape[0]
    pooled = own_ref[nodes : 2 * nodes, :].astype(F32)
    for ref in (a_ref, b_ref, near_ref, far_ref):
        pooled += ref[...].astype(F32)
    loads[0].wait()
    update = silu(jnp.dot(pooled.astype(BF16), w_enc[...], preferred_element_type=F32))
    first = (mesh_ref[...].astype(F32) + gain[...] * layer_norm(update)).astype(BF16)
    first_ref[...] = first
    loads[1].wait()
    p = jnp.dot(first, w_send[...], preferred_element_type=F32).astype(BF16)
    blocks, _, block = src_ref.shape
    per = block // capacity
    ids = lax.broadcasted_iota(jnp.int32, (nodes, block), 0)
    copies = []
    for i in range(blocks):
        table = (ids == src_ref[i]).astype(BF16)
        part = pl.ds(i * per, per)
        rows = lax.dot_general(table, p, (((0,), (0,)), ((), ())), preferred_element_type=F32).astype(BF16)
        for j in range(parts):
            rows_ref[part, j * capacity : (j + 1) * capacity, :] = rows[:, j * LANES : (j + 1) * LANES].reshape(
                per, capacity, LANES
            )
        mark = mark_ref[i * per : (i + 1) * per, :]
        rows_ref[part, parts * capacity :, :] = jnp.broadcast_to(mark[:, None, :], (per, MARKS, LANES)).astype(BF16)
        copies.append(pltpu.make_async_copy(rows_ref.at[part], rows_hbm.at[part], sem.at[i]))
        copies[-1].start()
    loads[2].wait()
    q_ref[...] = jnp.dot(first, w_recv[...], preferred_element_type=F32).astype(BF16)
    for copy in copies:
        copy.wait()


def node_stage(src, marks, sums, mesh_feat, w_enc, w_send, w_recv, gain):
    nodes, latent = mesh_feat.shape
    tiles, capacity = src.shape
    block = 512
    steps = tiles * capacity // block
    out = jax.ShapeDtypeStruct((nodes, latent), BF16)
    sent = (tiles, capacity * latent // LANES + MARKS, LANES)
    return pl.pallas_call(
        node_kernel,
        out_shape=(out, out, jax.ShapeDtypeStruct(sent, BF16)),
        in_specs=[whole()] * 8 + [whole(HBM)] * 3 + [whole()],
        out_specs=(whole(), whole(), whole(HBM)),
        scratch_shapes=[pltpu.VMEM(sent, BF16)]
        + [pltpu.VMEM((latent, latent), BF16)] * 3
        + [pltpu.SemaphoreType.DMA((steps,)), pltpu.SemaphoreType.DMA((3,))],
        compiler_params=pltpu.CompilerParams(vmem_limit_bytes=60 * MIB),
        name="mesh_encoder",
    )(src.reshape(steps, 1, block), marks, *sums, mesh_feat, w_enc, w_send, w_recv, gain.reshape(1, latent))


def edge_kernel(rows_ref, q_ref, first_ref, w_sum, w_dec, gain, mesh_ref, dec_ref, sum_ref):
    i = pl.program_id(0)
    tiles, height, _ = rows_ref.shape
    nodes, latent = q_ref.shape
    parts = latent // LANES
    capacity = (height - MARKS) // parts
    side = LANES // capacity
    per = 2 * side
    lane = lax.broadcasted_iota(jnp.int32, (MARKS, LANES), 1)
    ids = lax.broadcasted_iota(jnp.int32, (nodes // MARKS, MARKS, LANES), 0) * MARKS
    ids = (ids + lax.broadcasted_iota(jnp.int32, ids.shape, 1)).astype(F32)
    total = jnp.zeros(sum_ref.shape, F32)
    for b in range(tiles // per):
        halves = []
        for h in range(2):
            at = b * per + h * side
            mark = rows_ref[at, parts * capacity :, :].astype(F32)
            for k in range(1, side):
                mark = jnp.where(lane < k * capacity, mark, rows_ref[at + k, parts * capacity :, :].astype(F32))
            halves.append((ids == mark[None]).astype(BF16).reshape(nodes, LANES))
        table = jnp.concatenate(halves, axis=1)
        near = lax.dot_general(table, q_ref[...], (((0,), (0,)), ((), ())), preferred_element_type=F32)
        joined = []
        for j in range(parts):
            rows = rows_ref[b * per : (b + 1) * per, j * capacity : (j + 1) * capacity, :].reshape(per * capacity, LANES)
            joined.append(silu(rows.astype(F32) + near[:, j * LANES : (j + 1) * LANES]).astype(BF16))
        total += jnp.dot(table, jnp.concatenate(joined, axis=1), preferred_element_type=F32)

    @pl.when(i == 0)
    def _():
        sum_ref[...] = total

    @pl.when(i > 0)
    def _():
        sum_ref[...] += total

    @pl.when(i == pl.num_programs(0) - 1)
    def _():
        update = silu(jnp.dot(sum_ref[...].astype(BF16), w_sum[...], preferred_element_type=F32))
        out = (first_ref[...].astype(F32) + gain[...] * layer_norm(update)).astype(BF16)
        mesh_ref[...] = out
        dec_ref[...] = jnp.dot(out, w_dec[...], preferred_element_type=F32).astype(BF16)


def edge_stage(rows, q, first, w_sum, w_dec, gain):
    nodes, latent = first.shape
    tiles, height, _ = rows.shape
    block = 32
    full = pl.BlockSpec((nodes, latent), lambda i: (0, 0))
    weight = pl.BlockSpec((latent, latent), lambda i: (0, 0))
    vec = pl.BlockSpec((1, latent), lambda i: (0, 0))
    out = jax.ShapeDtypeStruct((nodes, latent), BF16)
    return pl.pallas_call(
        edge_kernel,
        grid=(tiles // block,),
        out_shape=(out, out),
        in_specs=[pl.BlockSpec((block, height, LANES), lambda i: (i, 0, 0)), full, full, weight, weight, vec],
        out_specs=(full, full),
        scratch_shapes=[pltpu.VMEM((nodes, latent), F32)],
        compiler_params=pltpu.CompilerParams(vmem_limit_bytes=14 * MIB),
        name="mesh_edges",
    )(rows, q, first, w_sum, w_dec, gain.reshape(1, latent))


def pick_table(picks, first_tile, tiles, nodes):
    rows, count = picks.shape[0], picks.shape[1] // 2
    ids = lax.broadcasted_iota(jnp.int32, (rows, LANES), 1).astype(jnp.int16)
    slots = [jnp.broadcast_to(picks[:, k : k + 1], (rows, LANES)).astype(jnp.int32).astype(jnp.int16) for k in range(count)]
    weights = [jnp.broadcast_to(picks[:, count + k : count + k + 1], (rows, LANES)).astype(BF16) for k in range(count)]
    blocks = []
    for j in range(first_tile * nodes // LANES, (first_tile + tiles) * nodes // LANES):
        at = ids + jnp.int16(j * LANES)
        block = jnp.zeros((rows, LANES), BF16)
        for slot, weight in zip(slots, weights):
            block = jnp.where(slot == at, weight, block)
        blocks.append(block)
    return jnp.concatenate(blocks, axis=1)


def first_kernel(picks_ref, near_ref, far_ref, a_ref, own_ref, b_ref, out_ref, *, inner):
    nodes = own_ref.shape[0]
    for i in range(out_ref.shape[0] // inner):
        part = slice(i * inner, (i + 1) * inner)
        table = pick_table(picks_ref[part, :], NEAR, 5, nodes)
        total = jnp.zeros((inner, out_ref.shape[1]), F32)
        for k, ref in enumerate((near_ref, far_ref, a_ref, own_ref, b_ref)):
            total += jnp.dot(table[:, k * nodes : (k + 1) * nodes], ref[...], preferred_element_type=F32)
        out_ref[part, :] = total.astype(BF16)


def first_stage(picks, near, far, a, own, b):
    rows = picks.shape[0]
    nodes, latent = own.shape
    block = 1024
    full = pl.BlockSpec((nodes, latent), lambda i: (0, 0))
    return pl.pallas_call(
        functools.partial(first_kernel, inner=256),
        grid=(rows // block,),
        out_shape=jax.ShapeDtypeStruct((rows, latent), BF16),
        in_specs=[pl.BlockSpec((block, picks.shape[1]), lambda i: (i, 0))] + [full] * 5,
        out_specs=pl.BlockSpec((block, latent), lambda i: (i, 0)),
        compiler_params=pltpu.CompilerParams(vmem_limit_bytes=16 * MIB),
        cost_estimate=pl.CostEstimate(flops=10 * rows * nodes * latent, bytes_accessed=8 * rows * latent, transcendentals=0),
        name="mesh_to_grid_first",
    )(picks, near, far, a, own, b)


def grid_kernel(picks_ref, part_ref, near_ref, far_ref, grid_ref, gain, out_ref, *, inner):
    nodes = near_ref.shape[0] // 2
    for i in range(out_ref.shape[0] // inner):
        part = slice(i * inner, (i + 1) * inner)
        table = pick_table(picks_ref[part, :], NEAR_A, 4, nodes)
        total = part_ref[part, :].astype(F32)
        total += jnp.dot(table[:, : 2 * nodes], near_ref[...], preferred_element_type=F32)
        total += jnp.dot(table[:, 2 * nodes :], far_ref[...], preferred_element_type=F32)
        update = silu(total)
        out_ref[part, :] = (grid_ref[part, :].astype(F32) + gain[...] * layer_norm(update)).astype(BF16)


def grid_stage(picks, part, near, far, grid_feat, gain):
    rows, latent = grid_feat.shape
    block = 512
    full = pl.BlockSpec(near.shape, lambda i: (0, 0))
    wide = pl.BlockSpec((block, latent), lambda i: (i, 0))
    return pl.pallas_call(
        functools.partial(grid_kernel, inner=256),
        grid=(rows // block,),
        out_shape=jax.ShapeDtypeStruct((rows, latent), BF16),
        in_specs=[
            pl.BlockSpec((block, picks.shape[1]), lambda i: (i, 0)),
            wide, full, full, wide,
            pl.BlockSpec((1, latent), lambda i: (0, 0)),
        ],
        out_specs=wide,
        compiler_params=pltpu.CompilerParams(vmem_limit_bytes=16 * MIB),
        name="mesh_to_grid",
    )(picks, part, near, far, grid_feat, gain.reshape(1, latent))


def swap(block, axis, first):
    size = lax.axis_size(axis)
    pairs = [(i, (i + 1 if (i % 2 == 0) == first else i - 1) % size) for i in range(size)]
    return lax.ppermute(block, axis, pairs)


def on_device(
    grid_feat, mesh_feat, g2m_src, g2m_dst, g2m_weight, mesh_src, mesh_dst, mesh_count, m2g_src, m2g_weight,
    w_in, w_enc, w_send, w_recv, w_edge, w_node, w_dec, w_out, gain_enc, gain_node, gain_out,
):
    grid_rows, latent = grid_feat.shape
    nodes = mesh_feat.shape[0]
    lon_count = lax.axis_size("lon")
    tiles = lax.axis_size("lat") * lon_count
    band = lax.axis_index("lat")
    sector = lax.axis_index("lon")
    tile = band * lon_count + sector
    where = jnp.stack([band, sector, tile]).astype(jnp.int32)

    near_ab, far_ab, near, far, own = scatter(where, g2m_src, g2m_dst, g2m_weight, grid_feat, w_in, nodes, lon_count)
    from_far_ab = swap(far_ab, "lon", False)
    from_near_ab = swap(near_ab, "lon", True)
    from_far = swap(far, "lon", False)
    from_near = swap(near, "lon", True)

    capacity = mesh_src.shape[2]
    live = lax.broadcasted_iota(jnp.int32, (tiles, capacity), 1) < mesh_count[0][:, None]
    marks = jnp.where(live, mesh_dst[0] & (nodes - 1), nodes).astype(F32)
    marks = jnp.tile(marks, (1, LANES // capacity))

    to_a, to_b = column_sums(own, from_near_ab, from_far_ab)
    sums = (own, swap(to_a, "lat", True), swap(to_b, "lat", False), from_near, from_far)

    first, q, rows = node_stage(
        mesh_src[0] - tile * nodes, marks, sums, mesh_feat, w_enc, w_send, w_recv, gain_enc
    )
    rows_in = lax.all_to_all(rows, ("lat", "lon"), split_axis=0, concat_axis=0, tiled=True)

    m2g_src, m2g_weight, first, w_edge, w_dec = lax.optimization_barrier((m2g_src, m2g_weight, first, w_edge, w_dec))
    shift = nodes.bit_length() - 1
    index = around_index(lax.shift_right_logical(m2g_src, shift), band, sector, lon_count)
    slots = index * nodes + (m2g_src & (nodes - 1))
    columns, weights = [slots[:, k] for k in range(slots.shape[1])], [m2g_weight[:, k] for k in range(slots.shape[1])]
    for i in range(len(columns)):
        for j in range(i + 1, len(columns)):
            same = columns[i] == columns[j]
            weights[i] = weights[i] + jnp.where(same, weights[j], 0.0)
            columns[j] = jnp.where(same, -1 - j, columns[j])
    picks = jnp.stack([c.astype(F32) for c in columns] + weights, axis=1)
    edge_node = jnp.dot(w_edge, w_node, preferred_element_type=F32).astype(BF16)
    dec_out = jnp.dot(w_dec, w_out, preferred_element_type=F32).astype(BF16)
    rows_in, picks, edge_node, dec_out = lax.optimization_barrier((rows_in, picks, edge_node, dec_out))

    mesh_out, decoded = edge_stage(rows_in, q, first, edge_node, dec_out, gain_node)

    from_a, from_b = swap(decoded, "lat", True), swap(decoded, "lat", False)
    far, near = swap(decoded, "lon", False), swap(decoded, "lon", True)
    ab = jnp.concatenate([from_a, from_b], axis=0)
    ab, near, far = lax.optimization_barrier((ab, near, far))
    far_ab, near_ab = swap(ab, "lon", False), swap(ab, "lon", True)
    part = first_stage(picks, near, far, from_a, decoded, from_b)
    grid_out = grid_stage(picks, part, near_ab, far_ab, grid_feat, gain_out)
    return (grid_out, mesh_out)


def solution(mesh):
    tile = ("lat", "lon")
    rows, flat, cube = P(tile, None), P(tile), P(tile, None, None)
    return jax.shard_map(
        on_device,
        mesh=mesh,
        in_specs=(rows, rows, flat, flat, flat, cube, cube, rows, rows, rows) + (P(),) * 11,
        out_specs=(rows, rows),
        check_vma=False,
    )
```

time: 179 us -> 151 us (0.84)
  Pallas kernels: 61.6 us -> 41.1 us
  starting transfers between devices: 32.6 us -> 23.5 us
  waiting for transfers between devices: 66.2 us -> 75.2 us
  other arithmetic: 8.01 us -> 1.64 us
    pallas_call x5 -> x6, Pallas kernels: 61.6 us -> 41.1 us  [the longest x1 16 us: scatter(): pl.pallas_call(functools.partial(scatter_kernel, nodes=nodes, lon_count=l...]
    all_to_all x2 -> x1, starting transfers between devices: 19.4 us -> 8.81 us  [on_device(): lax.all_to_all(rows, ('lat', 'lon'), split_axis=0, concat_axis=0, tiled=T...]
    ppermute x8 -> x12, waiting for transfers between devices: 15.8 us -> 21.2 us  [swap(): return lax.ppermute(block, axis, pairs)]
    all_to_all x2 -> x1, waiting for transfers between devices: 50.4 us -> 54.1 us  [on_device(): lax.all_to_all(rows, ('lat', 'lon'), split_axis=0, concat_axis=0, tiled=T...]
    add x1 -> x2, other arithmetic: 3.44 us -> 0.12 us  [the longest x1 0.08 us: on_device(): slots = index * nodes + (m2g_src & nodes - 1)]
    ppermute x8 -> x12, starting transfers between devices: 13.1 us -> 14.6 us  [swap(): return lax.ppermute(block, axis, pairs)]
    unnamed x23 -> x46, local copies, waits for them, and re-layouts: 4.47 us -> 5.21 us
  transfers between devices with their start and end apart: 10 -> 13, of which waited for: 3 -> 6; matrix products, arithmetic and copies ran while one was open for 6% -> 3% of each run, Pallas kernels for 12% -> 2%
where the time goes in v2:
time: 151 us; the launch traced here: 150 us
  waiting for transfers between devices  75.2 us (50%)
  Pallas kernels  41.1 us (27%)
  starting transfers between devices  23.5 us (16%)
  local copies, waits for them, and re-layouts  7.18 us (5%)
  other arithmetic  1.64 us (1%)
    all_to_all x1, waiting for transfers between devices, on_device(): lax.all_to_all(rows, ('lat', 'lon'), split_axis=0, concat_axis=0, tiled=T...  54.1 us
    ppermute x12, waiting for transfers between devices, swap(): return lax.ppermute(block, axis, pairs)  21.2 us
    pallas_call x1, Pallas kernels, scatter(): pl.pallas_call(functools.partial(scatter_kernel, nodes=nodes, lon_count=l...  16 us
    ppermute x12, starting transfers between devices, swap(): return lax.ppermute(block, axis, pairs)  14.6 us
    all_to_all x1, starting transfers between devices, on_device(): lax.all_to_all(rows, ('lat', 'lon'), split_axis=0, concat_axis=0, tiled=T...  8.81 us
    pallas_call x1, Pallas kernels, edge_stage(): pl.pallas_call(edge_kernel, grid=(tiles // block,), out_shape=(out, out),...  8.67 us
    pallas_call x1, Pallas kernels, node_stage(): pl.pallas_call(node_kernel, out_shape=(out, out, jax.ShapeDtypeStruct(sen...  6.69 us
    pallas_call x1, Pallas kernels, grid_stage(): pl.pallas_call(functools.partial(grid_kernel, inner=256), grid=(rows // b...  6 us
  transfers between devices with their start and end apart: 13, of which 6 were waited for; matrix products, arithmetic and copies ran while one was open for 3% of the time, Pallas kernels for 2%

profile of v2, /device:TPU:0, one launch (start us, length us, event | category | flops | bytes accessed | tf_op | source)
XLA Modules:
  0.0 150.4 jit_solution(1819581613097802527)
XLA Ops:
  0.6 0.0 copy-start
  0.7 0.6 pad_add_fusion.where_ref
  1.3 16.0 %grid_to_mesh.1 = (bf16[512,512]{1,0:T(8,128)(2,1)}, bf16[512,512]{1,0:T(8,128)(2,1)}, bf16[256,512]{1,0:T(8,128)(2,1)}, bf16[256,512]{1,0:T(8,128)(2,1)}, bf16[768,512]{1,0:T(8,128)(2,1)}) custom-call(s32[3]{0:T(128)} %pad_add_fusion.where_ref, s32[32,128]{1,0:T(8,128)} %bitcast.22, s32[32,128]{1,0:T(8,128)} %bitcast.23, f32[32,128]{1,0:T(8,128)} %bitcast.24, ...), custom_call_target="tpu_custom_call" | custom-call | tf_op jit(solution)/shard_map/grid_to_mesh/pallas_call | solution.py:145
  17.4 0.1 collective-permute-start
  17.4 5.4 %collective-permute-start.1 = (bf16[512,512]{1,0:T(8,128)(2,1)}, bf16[512,512]{1,0:T(8,128)(2,1)S(1)}, u32[]{:S(2)}, u32[]{:S(2)}) collective-permute-start(bf16[512,512]{1,0:T(8,128)(2,1)} %get-tuple-element.28), channel_id=1, source_target_pairs={{0,31},{1,2},{2,1},{3,4},{4,3},{5,6},{6,5},{7,8},{8,7},{9,10},{10,... | collective-permute-start | bytes 1572872 | tf_op jit(solution)/shard_map/ppermute | solution.py:393
  22.8 0.0 collective-permute-start.4
  22.8 0.9 collective-permute-start.5
  23.8 0.0 collective-permute-done.near_ref
  23.8 6.1 %collective-permute-done.1.far_ref = bf16[512,512]{1,0:T(8,128)(2,1)S(1)} collective-permute-done((bf16[512,512]{1,0:T(8,128)(2,1)}, bf16[512,512]{1,0:T(8,128)(2,1)S(1)}, u32[]{:S(2)}, u32[]{:S(2)}) %collective-permute-start.1) | collective-permute-done | bytes 524320 | tf_op jit(solution)/shard_map/ppermute | solution.py:393
  29.9 1.1 copy-done.2
  31.0 0.2 column_sums.1
  31.2 2.0 %collective-permute-start.2 = (bf16[256,512]{1,0:T(8,128)(2,1)S(1)}, bf16[256,512]{1,0:T(8,128)(2,1)S(1)}, u32[]{:S(2)}, u32[]{:S(2)}) collective-permute-start(bf16[256,512]{1,0:T(8,128)(2,1)S(1)} %get-tuple-element.29), channel_id=1, source_target_pairs={{0,32},{32,0},{64,96},{96,64},{1,33},{33,1},{65,97},{97,65},{2,34}... | collective-permute-start | bytes 786440 | tf_op jit(solution)/shard_map/ppermute | solution.py:393
  33.2 2.5 %collective-permute-start.3 = (bf16[256,512]{1,0:T(8,128)(2,1)S(1)}, bf16[256,512]{1,0:T(8,128)(2,1)S(1)}, u32[]{:S(2)}, u32[]{:S(2)}) collective-permute-start(bf16[256,512]{1,0:T(8,128)(2,1)S(1)} %get-tuple-element.30), channel_id=1, source_target_pairs={{0,96},{32,64},{64,32},{96,0},{1,97},{33,65},{65,33},{97,1},{2,98}... | collective-permute-start | bytes 786440 | tf_op jit(solution)/shard_map/ppermute | solution.py:393
  35.8 0.1 copy.50
  35.9 0.7 sub.47.src_ref
  36.6 0.0 copy-done.21
  36.6 0.7 copy.52.mark_ref
  37.3 0.0 collective-permute-done.4.near_ref
  37.3 0.0 collective-permute-done.5.far_ref
  37.3 0.0 copy-start.15
  37.3 0.3 collective-permute-done.2.a_ref
  37.7 3.1 %collective-permute-done.3.b_ref = bf16[256,512]{1,0:T(8,128)(2,1)S(1)} collective-permute-done((bf16[256,512]{1,0:T(8,128)(2,1)S(1)}, bf16[256,512]{1,0:T(8,128)(2,1)S(1)}, u32[]{:S(2)}, u32[]{:S(2)}) %collective-permute-start.3) | collective-permute-done | bytes 262176 | tf_op jit(solution)/shard_map/ppermute | solution.py:393
  40.8 0.0 copy-done.15
  40.8 0.7 copy-done.17
  41.5 6.7 %mesh_encoder.1 = (bf16[256,512]{1,0:T(8,128)(2,1)}, bf16[256,512]{1,0:T(8,128)(2,1)}, bf16[128,136,128]{2,1,0:T(8,128)(2,1)}) custom-call(s32[8,1,512]{2,1,0:T(1,128)} %sub.47.src_ref, f32[128,128]{1,0:T(8,128)} %copy.52.mark_ref, bf16[768,512]{1,0:T(8,128)(2,1)} %get-tuple-element.26.own_ref, bf16[256,512]{1,0:T(8,128)(2,1)} %copy-done.16, ...), custom_call_target="tpu_custom_call" | custom-call | tf_op jit(solution)/shard_map/mesh_encoder/pallas_call | solution.py:238
  48.2 0.0 copy-start.18
  48.3 0.0 copy-start.19
  48.3 0.0 copy-start.11
  48.3 0.0 copy-start.12
  48.3 0.0 copy-start.13
  48.3 8.8 %all-to-all-start = ((bf16[128,136,128]{2,1,0:T(8,128)(2,1)}), bf16[128,136,128]{2,1,0:T(8,128)(2,1)}, u32[]{:S(2)}, u32[]{:S(2)}) async-start(bf16[128,136,128]{2,1,0:T(8,128)(2,1)} %get-tuple-element.33), calls=%async_computation | async-start | bytes 8912896 | tf_op jit(solution)/shard_map/all_to_all | solution.py:426
  57.1 0.0 copy-start.3
  57.1 0.0 copy-start.4
  57.1 0.0 copy-start.5
  57.2 0.0 copy-done.18
  57.2 0.1 and_add_fusion
  57.3 0.0 copy-done.19
  57.4 0.1 stack.24
  57.4 0.0 copy-done
  57.5 0.0 copy-done.11
  57.5 0.4 convolution_convert_fusion.1.w_sum
  57.9 0.4 convolution_convert_fusion.w_dec
  58.4 54.1 %all-to-all-done.rows_ref = bf16[128,136,128]{2,1,0:T(8,128)(2,1)} async-done(((bf16[128,136,128]{2,1,0:T(8,128)(2,1)}), bf16[128,136,128]{2,1,0:T(8,128)(2,1)}, u32[]{:S(2)}, u32[]{:S(2)}) %all-to-all-start) | async-done | bytes 4456480 | tf_op jit(solution)/shard_map/all_to_all | solution.py:426
  112.4 8.7 %mesh_edges.1 = (bf16[256,512]{1,0:T(8,128)(2,1)}, bf16[256,512]{1,0:T(8,128)(2,1)S(1)}) custom-call(bf16[128,136,128]{2,1,0:T(8,128)(2,1)} %all-to-all-done.rows_ref, bf16[256,512]{1,0:T(8,128)(2,1)S(1)} %copy-done.4, bf16[256,512]{1,0:T(8,128)(2,1)S(1)} %copy-done.3, bf16[512,512]{1,0:T(8,128)(2,1)S(1)} %convolution_convert_fusion.1.w_sum, ...), custom_call_target="tpu_custom_call" | custom-call | tf_op jit(solution)/shard_map/mesh_edges/pallas_call | solution.py:303
  121.1 0.6 collective-permute-start.7
  121.7 0.0 collective-permute-start.6
  121.7 0.0 collective-permute-start.8
  121.7 1.5 collective-permute-start.9
  123.1 6.9 %collective-permute-done.7.b_ref = bf16[256,512]{1,0:T(8,128)(2,1)S(1)} collective-permute-done((bf16[256,512]{1,0:T(8,128)(2,1)S(1)}, bf16[256,512]{1,0:T(8,128)(2,1)S(1)}, u32[]{:S(2)}, u32[]{:S(2)}) %collective-permute-start.7) | collective-permute-done | bytes 262176 | tf_op jit(solution)/shard_map/ppermute | solution.py:393
  130.1 0.0 collective-permute-done.6.a_ref
  130.1 0.8 pad_maximum_fusion
  130.9 0.0 collective-permute-done.8.near_ref
  130.9 0.7 copy-done.7
  131.6 0.0 collective-permute-done.9.far_ref
  131.6 0.7 copy-done.9
  132.3 0.0 collective-permute-start.10
  132.3 1.7 %collective-permute-start.11 = (bf16[512,512]{1,0:T(8,128)(2,1)}, bf16[512,512]{1,0:T(8,128)(2,1)S(1)}, u32[]{:S(2)}, u32[]{:S(2)}) collective-permute-start(bf16[512,512]{1,0:T(8,128)(2,1)} %pad_maximum_fusion), channel_id=1, source_target_pairs={{0,31},{1,2},{2,1},{3,4},{4,3},{5,6},{6,5},{7,8},{8,7},{9,10},{10,... | collective-permute-start | bytes 1572872 | tf_op jit(solution)/shard_map/ppermute | solution.py:393
  134.0 0.4 copy.54.picks_ref
  134.3 0.9 copy-done.8
  135.3 0.9 copy-done.10
  136.2 3.5 %mesh_to_grid_first.1.part_ref = bf16[2048,512]{1,0:T(8,128)(2,1)S(1)} custom-call(f32[2048,6]{1,0:T(8,128)S(1)} %copy.54.picks_ref, bf16[256,512]{1,0:T(8,128)(2,1)S(1)} %copy-done.8, bf16[256,512]{1,0:T(8,128)(2,1)S(1)} %copy-done.10, bf16[256,512]{1,0:T(8,128)(2,1)S(1)} %collective-permute-done.6.a_ref, bf16[256,512]{1,0:T(8,128)(2,1)S(1)} %get-tuple-element.45.own_ref, ...), custom_call_target="tpu_custom_call" | custom-call | flops 2684354560 | bytes 8388608 | tf_op jit(solution)/shard_map/mesh_to_grid_first/pallas_call | solution.py:346
  139.8 0.0 collective-permute-done.10.near_ref
  139.8 4.6 %collective-permute-done.11.far_ref = bf16[512,512]{1,0:T(8,128)(2,1)S(1)} collective-permute-done((bf16[512,512]{1,0:T(8,128)(2,1)}, bf16[512,512]{1,0:T(8,128)(2,1)S(1)}, u32[]{:S(2)}, u32[]{:S(2)}) %collective-permute-start.11) | collective-permute-done | bytes 524320 | tf_op jit(solution)/shard_map/ppermute | solution.py:393
  144.4 6.0 %mesh_to_grid.1 = bf16[2048,512]{1,0:T(8,128)(2,1)} custom-call(f32[2048,6]{1,0:T(8,128)S(1)} %copy.54.picks_ref, bf16[2048,512]{1,0:T(8,128)(2,1)S(1)} %mesh_to_grid_first.1.part_ref, bf16[512,512]{1,0:T(8,128)(2,1)S(1)} %collective-permute-done.10.near_ref, bf16[512,512]{1,0:T(8,128)(2,1)S(1)} %collective-permute-done.11.far_ref, ...), custom_call_target="tpu_custom_call" | custom-call | tf_op jit(solution)/shard_map/mesh_to_grid/pallas_call | solution.py:375
  (29 shorter events, 0.1 us)
Async XLA Ops:
  0.6 56.8 %copy-start = (bf16[512,512]{1,0:T(8,128)(2,1)S(1)}, bf16[512,512]{1,0:T(8,128)(2,1)}, u32[]{:S(2)}) copy-start(bf16[512,512]{1,0:T(8,128)(2,1)} %param.35) | copy-start | bytes 1572868
  1.3 34.5 %copy-start.20 = (s32[1,128,32]{1,2,0:T(8,128)S(1)}, s32[1,128,32]{1,2,0:T(8,128)}, u32[]{:S(2)}) copy-start(s32[1,128,32]{1,2,0:T(8,128)} %param.26) | copy-start | bytes 49156
  1.3 35.3 %copy-start.21 = (s32[1,128,32]{1,2,0:T(8,128)S(1)}, s32[1,128,32]{1,2,0:T(8,128)}, u32[]{:S(2)}) copy-start(s32[1,128,32]{1,2,0:T(8,128)} %param.27) | copy-start | bytes 49156
  1.3 35.3 %copy-start.22 = (s32[1,128]{1,0:T(1,128)S(1)}, s32[1,128]{1,0:T(1,128)}, u32[]{:S(2)}) copy-start(s32[1,128]{1,0:T(1,128)} %param.28) | copy-start | bytes 1540
  17.4 6.4 %collective-permute-start = (bf16[512,512]{1,0:T(8,128)(2,1)}, bf16[512,512]{1,0:T(8,128)(2,1)S(1)}, u32[]{:S(2)}, u32[]{:S(2)}) collective-permute-start(bf16[512,512]{1,0:T(8,128)(2,1)} %get-tuple-element.27), channel_id=1, source_target_pairs={{0,1},{1,0},{2,3},{3,2},{4,5},{5,4},{6,7},{7,6},{8,9},{9,8},{10,11... | collective-permute-start | bytes 1572872 | tf_op jit(solution)/shard_map/ppermute | solution.py:393
  17.4 12.5 %collective-permute-start.1 = (bf16[512,512]{1,0:T(8,128)(2,1)}, bf16[512,512]{1,0:T(8,128)(2,1)S(1)}, u32[]{:S(2)}, u32[]{:S(2)}) collective-permute-start(bf16[512,512]{1,0:T(8,128)(2,1)} %get-tuple-element.28), channel_id=1, source_target_pairs={{0,31},{1,2},{2,1},{3,4},{4,3},{5,6},{6,5},{7,8},{8,7},{9,10},{10,... | collective-permute-start | bytes 1572872 | tf_op jit(solution)/shard_map/ppermute | solution.py:393
  22.8 14.5 %collective-permute-start.4 = (bf16[256,512]{1,0:T(8,128)(2,1)}, bf16[256,512]{1,0:T(8,128)(2,1)S(1)}, u32[]{:S(2)}, u32[]{:S(2)}) collective-permute-start(bf16[256,512]{1,0:T(8,128)(2,1)} %get-tuple-element.31), channel_id=1, source_target_pairs={{0,1},{1,0},{2,3},{3,2},{4,5},{5,4},{6,7},{7,6},{8,9},{9,8},{10,11... | collective-permute-start | bytes 786440 | tf_op jit(solution)/shard_map/ppermute | solution.py:393
  22.8 14.5 %collective-permute-start.5 = (bf16[256,512]{1,0:T(8,128)(2,1)}, bf16[256,512]{1,0:T(8,128)(2,1)S(1)}, u32[]{:S(2)}, u32[]{:S(2)}) collective-permute-start(bf16[256,512]{1,0:T(8,128)(2,1)} %get-tuple-element.32), channel_id=1, source_target_pairs={{0,31},{1,2},{2,1},{3,4},{4,3},{5,6},{6,5},{7,8},{8,7},{9,10},{10,... | collective-permute-start | bytes 786440 | tf_op jit(solution)/shard_map/ppermute | solution.py:393
  29.9 1.1 copy-start.2
  31.2 6.5 %collective-permute-start.2 = (bf16[256,512]{1,0:T(8,128)(2,1)S(1)}, bf16[256,512]{1,0:T(8,128)(2,1)S(1)}, u32[]{:S(2)}, u32[]{:S(2)}) collective-permute-start(bf16[256,512]{1,0:T(8,128)(2,1)S(1)} %get-tuple-element.29), channel_id=1, source_target_pairs={{0,32},{32,0},{64,96},{96,64},{1,33},{33,1},{65,97},{97,65},{2,34}... | collective-permute-start | bytes 786440 | tf_op jit(solution)/shard_map/ppermute | solution.py:393
  33.2 7.6 %collective-permute-start.3 = (bf16[256,512]{1,0:T(8,128)(2,1)S(1)}, bf16[256,512]{1,0:T(8,128)(2,1)S(1)}, u32[]{:S(2)}, u32[]{:S(2)}) collective-permute-start(bf16[256,512]{1,0:T(8,128)(2,1)S(1)} %get-tuple-element.30), channel_id=1, source_target_pairs={{0,96},{32,64},{64,32},{96,0},{1,97},{33,65},{65,33},{97,1},{2,98}... | collective-permute-start | bytes 786440 | tf_op jit(solution)/shard_map/ppermute | solution.py:393
  37.3 3.5 %copy-start.14 = (bf16[256,512]{1,0:T(8,128)(2,1)}, bf16[256,512]{1,0:T(8,128)(2,1)S(1)}, u32[]{:S(2)}) copy-start(bf16[256,512]{1,0:T(8,128)(2,1)S(1)} %collective-permute-done.4.near_ref) | copy-start | bytes 786436
  37.3 3.5 %copy-start.15 = (bf16[256,512]{1,0:T(8,128)(2,1)}, bf16[256,512]{1,0:T(8,128)(2,1)S(1)}, u32[]{:S(2)}) copy-start(bf16[256,512]{1,0:T(8,128)(2,1)S(1)} %collective-permute-done.5.far_ref) | copy-start | bytes 786436
  37.7 3.1 %copy-start.16 = (bf16[256,512]{1,0:T(8,128)(2,1)}, bf16[256,512]{1,0:T(8,128)(2,1)S(1)}, u32[]{:S(2)}) copy-start(bf16[256,512]{1,0:T(8,128)(2,1)S(1)} %collective-permute-done.2.a_ref) | copy-start | bytes 786436
  40.8 0.7 copy-start.17
  48.2 8.9 %copy-start.18 = (s32[2048,3]{0,1:T(4,128)S(1)}, s32[2048,3]{0,1:T(4,128)}, u32[]{:S(2)}) copy-start(s32[2048,3]{0,1:T(4,128)} %param.29) | copy-start | bytes 73732
  48.3 9.0 %copy-start.19 = (f32[2048,3]{0,1:T(4,128)S(1)}, f32[2048,3]{0,1:T(4,128)}, u32[]{:S(2)}) copy-start(f32[2048,3]{0,1:T(4,128)} %param.30) | copy-start | bytes 73732
  48.3 9.2 %copy-start.11 = (bf16[512,512]{1,0:T(8,128)(2,1)S(1)}, bf16[512,512]{1,0:T(8,128)(2,1)}, u32[]{:S(2)}) copy-start(bf16[512,512]{1,0:T(8,128)(2,1)} %param.36) | copy-start | bytes 1572868
  48.3 9.6 %copy-start.12 = (bf16[512,512]{1,0:T(8,128)(2,1)S(1)}, bf16[512,512]{1,0:T(8,128)(2,1)}, u32[]{:S(2)}) copy-start(bf16[512,512]{1,0:T(8,128)(2,1)} %param.37) | copy-start | bytes 1572868
  48.3 9.6 %copy-start.13 = (bf16[512,512]{1,0:T(8,128)(2,1)S(1)}, bf16[512,512]{1,0:T(8,128)(2,1)}, u32[]{:S(2)}) copy-start(bf16[512,512]{1,0:T(8,128)(2,1)} %param.38) | copy-start | bytes 1572868
  48.3 64.1 %all-to-all-start = ((bf16[128,136,128]{2,1,0:T(8,128)(2,1)}), bf16[128,136,128]{2,1,0:T(8,128)(2,1)}, u32[]{:S(2)}, u32[]{:S(2)}) async-start(bf16[128,136,128]{2,1,0:T(8,128)(2,1)} %get-tuple-element.33), calls=%async_computation | async-start | bytes 8912896 | tf_op jit(solution)/shard_map/all_to_all | solution.py:426
  57.1 55.3 %copy-start.3 = (bf16[256,512]{1,0:T(8,128)(2,1)S(1)}, bf16[256,512]{1,0:T(8,128)(2,1)}, u32[]{:S(2)}) copy-start(bf16[256,512]{1,0:T(8,128)(2,1)} %get-tuple-element.42.first_ref) | copy-start | bytes 786436
  57.1 55.3 %copy-start.4 = (bf16[256,512]{1,0:T(8,128)(2,1)S(1)}, bf16[256,512]{1,0:T(8,128)(2,1)}, u32[]{:S(2)}) copy-start(bf16[256,512]{1,0:T(8,128)(2,1)} %get-tuple-element.41.q_ref) | copy-start | bytes 786436
  57.1 55.3 %copy-start.5 = (f32[512]{0:T(512)S(1)}, f32[512]{0:T(512)}, u32[]{:S(2)}) copy-start(f32[512]{0:T(512)} %param.40) | copy-start | bytes 6148
  121.1 9.0 %collective-permute-start.7 = (bf16[256,512]{1,0:T(8,128)(2,1)S(1)}, bf16[256,512]{1,0:T(8,128)(2,1)S(1)}, u32[]{:S(2)}, u32[]{:S(2)}) collective-permute-start(bf16[256,512]{1,0:T(8,128)(2,1)S(1)} %get-tuple-element.45.own_ref), channel_id=1, source_target_pairs={{0,96},{32,64},{64,32},{96,0},{1,97},{33,65},{65,33},{97,1},{2,98}... | collective-permute-start | bytes 786440 | tf_op jit(solution)/shard_map/ppermute | solution.py:393
  121.7 8.4 %collective-permute-start.6 = (bf16[256,512]{1,0:T(8,128)(2,1)S(1)}, bf16[256,512]{1,0:T(8,128)(2,1)S(1)}, u32[]{:S(2)}, u32[]{:S(2)}) collective-permute-start(bf16[256,512]{1,0:T(8,128)(2,1)S(1)} %get-tuple-element.45.own_ref), channel_id=1, source_target_pairs={{0,32},{32,0},{64,96},{96,64},{1,33},{33,1},{65,97},{97,65},{2,34}... | collective-permute-start | bytes 786440 | tf_op jit(solution)/shard_map/ppermute | solution.py:393
  121.7 9.2 %collective-permute-start.8 = (bf16[256,512]{1,0:T(8,128)(2,1)S(1)}, bf16[256,512]{1,0:T(8,128)(2,1)S(1)}, u32[]{:S(2)}, u32[]{:S(2)}) collective-permute-start(bf16[256,512]{1,0:T(8,128)(2,1)S(1)} %get-tuple-element.45.own_ref), channel_id=1, source_target_pairs={{0,1},{1,0},{2,3},{3,2},{4,5},{5,4},{6,7},{7,6},{8,9},{9,8},{10,11... | collective-permute-start | bytes 786440 | tf_op jit(solution)/shard_map/ppermute | solution.py:393
  121.7 9.9 %collective-permute-start.9 = (bf16[256,512]{1,0:T(8,128)(2,1)S(1)}, bf16[256,512]{1,0:T(8,128)(2,1)S(1)}, u32[]{:S(2)}, u32[]{:S(2)}) collective-permute-start(bf16[256,512]{1,0:T(8,128)(2,1)S(1)} %get-tuple-element.45.own_ref), channel_id=1, source_target_pairs={{0,31},{1,2},{2,1},{3,4},{4,3},{5,6},{6,5},{7,8},{8,7},{9,10},{10,... | collective-permute-start | bytes 786440 | tf_op jit(solution)/shard_map/ppermute | solution.py:393
  130.9 0.7 copy-start.7
  131.6 0.7 copy-start.9
  132.3 7.5 %collective-permute-start.10 = (bf16[512,512]{1,0:T(8,128)(2,1)}, bf16[512,512]{1,0:T(8,128)(2,1)S(1)}, u32[]{:S(2)}, u32[]{:S(2)}) collective-permute-start(bf16[512,512]{1,0:T(8,128)(2,1)} %pad_maximum_fusion), channel_id=1, source_target_pairs={{0,1},{1,0},{2,3},{3,2},{4,5},{5,4},{6,7},{7,6},{8,9},{9,8},{10,11... | collective-permute-start | bytes 1572872 | tf_op jit(solution)/shard_map/ppermute | solution.py:393
  132.3 12.1 %collective-permute-start.11 = (bf16[512,512]{1,0:T(8,128)(2,1)}, bf16[512,512]{1,0:T(8,128)(2,1)S(1)}, u32[]{:S(2)}, u32[]{:S(2)}) collective-permute-start(bf16[512,512]{1,0:T(8,128)(2,1)} %pad_maximum_fusion), channel_id=1, source_target_pairs={{0,31},{1,2},{2,1},{3,4},{4,3},{5,6},{6,5},{7,8},{8,7},{9,10},{10,... | collective-permute-start | bytes 1572872 | tf_op jit(solution)/shard_map/ppermute | solution.py:393
  134.3 1.0 copy-start.8
  135.3 0.9 copy-start.10
  136.2 8.2 %copy-start.1 = (bf16[2048,512]{1,0:T(8,128)(2,1)S(1)}, bf16[2048,512]{1,0:T(8,128)(2,1)}, u32[]{:S(2)}) copy-start(bf16[2048,512]{1,0:T(8,128)(2,1)} %grid_ref.1) | copy-start | bytes 6291460
  136.2 8.2 %copy-start.6 = (f32[512]{0:T(512)S(1)}, f32[512]{0:T(512)}, u32[]{:S(2)}) copy-start(f32[512]{0:T(512)} %param.41) | copy-start | bytes 6148

commit v3 on v2

v3 whole, which is shorter than its diff:
```python
import functools

import jax
import jax.numpy as jnp
from jax import lax
from jax.experimental import pallas as pl
from jax.experimental.pallas import tpu as pltpu
from jax.sharding import PartitionSpec as P

BF16 = jnp.bfloat16
F32 = jnp.float32
LANES = 128
MARKS = 8
MIB = 1024 * 1024
EDGE_MIB = 24
NODE_MIB = 57
VMEM = pltpu.VMEM
SMEM = pltpu.SMEM
HBM = pltpu.HBM


def silu(v):
    half = v * jnp.asarray(0.5, v.dtype)
    return half + half * jnp.tanh(half)


def layer_norm(values):
    center = values - jnp.mean(values, axis=-1, keepdims=True)
    spread = jnp.mean(center * center, axis=-1, keepdims=True)
    return center * lax.rsqrt(spread + 1e-05)


def whole(space=VMEM):
    return pl.BlockSpec(memory_space=space)


NEAR_A, NEAR_B, NEAR, FAR_A, FAR_B, FAR, A, B, OWN = range(9)
BY_PLACE = (NEAR_A, NEAR, NEAR_B, A, OWN, B, FAR_A, FAR, FAR_B)


def around_index(owner, band, sector, lon_count):
    step_lat = lax.shift_right_logical(owner, lon_count.bit_length() - 1) - band
    step_lon = ((owner - sector + 1) & (lon_count - 1)) - 1
    lat_at = 1 + step_lat * (2 * (band & 1) - 1)
    lon_at = 1 + step_lon * (2 * (sector & 1) - 1)
    place = lon_at * 3 + lat_at
    index = jnp.zeros_like(place)
    for at, tile in enumerate(BY_PLACE):
        if tile:
            index = jnp.where(place == at, tile, index)
    return index


def scatter_kernel(src_hbm, dst_hbm, wgt_hbm, grid_hbm, w_hbm, *refs, nodes, lon_count):
    count = len(refs) - 16
    outs = refs[:count]
    accs = refs[count : count + 4]
    y_ref, stage_ref, grid_ref, w_ref, src_v, dst_v, src_s, dst_s, wgt_s, grid_sem, out_sem, sem = refs[count + 4 :]
    rows, latent = grid_ref.shape
    parts = latent // LANES
    step = 256
    chunks = rows // step

    def grid_copy(i):
        part = pl.ds(pl.multiple_of(i * step, step), step)
        return pltpu.make_async_copy(grid_hbm.at[part], grid_ref.at[part], grid_sem.at[i])

    w_in = pltpu.make_async_copy(w_hbm, w_ref, sem.at[3])
    src_in = pltpu.make_async_copy(src_hbm, src_v, sem.at[0])
    dst_in = pltpu.make_async_copy(dst_hbm, dst_v, sem.at[1])
    wgt_in = pltpu.make_async_copy(wgt_hbm, wgt_s, sem.at[2])
    src_out = pltpu.make_async_copy(src_v, src_s, sem.at[4])
    dst_out = pltpu.make_async_copy(dst_v, dst_s, sem.at[5])
    w_in.start()
    grid_copy(0).start()
    for copy in (src_in, dst_in, wgt_in):
        copy.start()
    for i in range(1, chunks):
        grid_copy(i).start()
    w_in.wait()

    span = accs[0].shape[0] // chunks
    zero = jnp.zeros((span, LANES), F32)

    def project(i, carry):
        grid_copy(i).wait()
        base = pl.multiple_of(i * step, step)
        y = silu(jnp.dot(grid_ref[pl.ds(base, step), :], w_ref[...], preferred_element_type=F32))
        for j in range(parts):
            y_ref[pl.ds(base * parts + j, step, stride=parts), :] = y[:, j * LANES : (j + 1) * LANES]
        for acc in accs:
            acc[pl.ds(pl.multiple_of(i * span, span), span), :] = zero
        return carry

    project(0, 0)
    band, sector = lax.axis_index("lat"), lax.axis_index("lon")
    src_in.wait()
    src_v[...] = (src_v[...] - (band * lon_count + sector) * rows) * parts
    src_out.start()
    dst_in.wait()
    dst = dst_v[...]
    index = around_index(lax.shift_right_logical(dst, nodes.bit_length() - 1), band, sector, lon_count)
    dst_v[...] = (index * nodes + (dst & (nodes - 1))) * parts
    dst_out.start()
    lax.fori_loop(1, chunks, project, 0)
    wgt_in.wait()
    src_out.wait()
    dst_out.wait()

    count = len(accs)
    lines, width = src_s.shape

    def add_edges(i, carry):
        for u in range(0, width, count):
            places, sums = [], []
            for n, acc in enumerate(accs):
                s = pl.multiple_of(src_s[i, u + n], parts)
                d = pl.multiple_of(dst_s[i, u + n], parts)
                places.append(d)
                sums.append(acc[pl.ds(d, parts), :] + wgt_s[i, u + n] * y_ref[pl.ds(s, parts), :])
            for acc, d, total in zip(accs, places, sums):
                acc[pl.ds(d, parts), :] = total
        return carry

    lax.fori_loop(0, lines, add_edges, 0)

    def emit(i, carry):
        base = pl.multiple_of(i * step, step)
        for j in range(parts):
            rows_j = pl.ds(base * parts + j, step, stride=parts)
            total = (accs[0][rows_j, :] + accs[1][rows_j, :]) + (accs[2][rows_j, :] + accs[3][rows_j, :])
            stage_ref[pl.ds(base, step), j * LANES : (j + 1) * LANES] = total.astype(stage_ref.dtype)
        return carry

    copies, start = [], 0
    for n, out in enumerate(outs):
        per = out.shape[0]
        lax.fori_loop(start // step, (start + per) // step, emit, 0)
        copies.append(pltpu.make_async_copy(stage_ref.at[start : start + per], out, out_sem.at[n]))
        copies[-1].start()
        start += per
    for copy in copies:
        copy.wait()


def scatter(src, dst, weight, grid_feat, w_in, nodes, lon_count):
    rows, latent = grid_feat.shape
    parts = latent // LANES
    slots = 9 * nodes
    lines = src.shape[0] // LANES
    outs = tuple(jax.ShapeDtypeStruct((n * nodes, latent), BF16) for n in (2, 1, 2, 1, 2, 1))
    ints = pltpu.VMEM((lines, LANES), jnp.int32)
    return pl.pallas_call(
        functools.partial(scatter_kernel, nodes=nodes, lon_count=lon_count),
        out_shape=outs,
        in_specs=[whole(HBM)] * 5,
        out_specs=(whole(HBM),) * len(outs),
        scratch_shapes=[pltpu.VMEM((slots * parts, LANES), F32)] * 4
        + [
            pltpu.VMEM((rows * parts, LANES), F32),
            pltpu.VMEM((slots, latent), BF16),
            pltpu.VMEM((rows, latent), BF16),
            pltpu.VMEM(w_in.shape, BF16),
            ints,
            ints,
            pltpu.SMEM((lines, LANES), jnp.int32),
            pltpu.SMEM((lines, LANES), jnp.int32),
            pltpu.SMEM((lines, LANES), F32),
            pltpu.SemaphoreType.DMA((rows // 256,)),
            pltpu.SemaphoreType.DMA((6,)),
            pltpu.SemaphoreType.DMA((6,)),
        ],
        compiler_params=pltpu.CompilerParams(vmem_limit_bytes=60 * MIB),
        name="grid_to_mesh",
    )(*(v.reshape(lines, LANES) for v in (src, dst, weight)), grid_feat, w_in)


def add_kernel(a_ref, b_ref, *outs):
    rows = outs[0].shape[0]
    for n, out in enumerate(outs):
        part = slice(n * rows, (n + 1) * rows)
        out[...] = (a_ref[part, :].astype(F32) + b_ref[part, :].astype(F32)).astype(out.dtype)


def add_pieces(a, b, pieces, dtype, name):
    out = jax.ShapeDtypeStruct((a.shape[0] // pieces, a.shape[1]), dtype)
    return pl.pallas_call(
        add_kernel,
        out_shape=(out,) * pieces,
        in_specs=[whole()] * 2,
        out_specs=(whole(),) * pieces,
        compiler_params=pltpu.CompilerParams(vmem_limit_bytes=8 * MIB),
        name=name,
    )(a, b)


def node_kernel(src_ref, mark_ref, own_ref, a_ref, b_ref, near_ref, far_ref, mesh_ref, enc_hbm, send_hbm, recv_hbm, gain, first_ref, q_ref, rows_hbm, rows_ref, w_enc, w_send, w_recv, sem, w_sem):
    tiles, _, _ = rows_ref.shape
    capacity = (rows_ref.shape[1] - MARKS) * LANES // mesh_ref.shape[1]
    parts = mesh_ref.shape[1] // LANES
    loads = [
        pltpu.make_async_copy(hbm, ref, w_sem.at[n])
        for n, (hbm, ref) in enumerate(((enc_hbm, w_enc), (send_hbm, w_send), (recv_hbm, w_recv)))
    ]
    for load in loads:
        load.start()
    nodes = mesh_ref.shape[0]
    pooled = own_ref[...].astype(F32)
    for ref in (a_ref, b_ref, near_ref, far_ref):
        pooled += ref[ref.shape[0] - nodes :, :].astype(F32)
    loads[0].wait()
    update = silu(jnp.dot(pooled.astype(BF16), w_enc[...], preferred_element_type=F32))
    first = (mesh_ref[...].astype(F32) + gain[...] * layer_norm(update)).astype(BF16)
    first_ref[...] = first
    loads[1].wait()
    p = jnp.dot(first, w_send[...], preferred_element_type=F32).astype(BF16)
    blocks, _, block = src_ref.shape
    per = block // capacity
    ids = lax.broadcasted_iota(jnp.int32, (nodes, block), 0)
    copies = []
    for i in range(blocks):
        table = (ids == src_ref[i]).astype(BF16)
        part = pl.ds(i * per, per)
        rows = lax.dot_general(table, p, (((0,), (0,)), ((), ())), preferred_element_type=F32).astype(BF16)
        for j in range(parts):
            rows_ref[part, j * capacity : (j + 1) * capacity, :] = rows[:, j * LANES : (j + 1) * LANES].reshape(
                per, capacity, LANES
            )
        mark = mark_ref[i * per : (i + 1) * per, :]
        rows_ref[part, parts * capacity :, :] = jnp.broadcast_to(mark[:, None, :], (per, MARKS, LANES)).astype(BF16)
        copies.append(pltpu.make_async_copy(rows_ref.at[part], rows_hbm.at[part], sem.at[i]))
        copies[-1].start()
    loads[2].wait()
    q_ref[...] = jnp.dot(first, w_recv[...], preferred_element_type=F32).astype(BF16)
    for copy in copies:
        copy.wait()


def node_stage(src, marks, sums, mesh_feat, w_enc, w_send, w_recv, gain):
    nodes, latent = mesh_feat.shape
    tiles, capacity = src.shape
    block = 512
    steps = tiles * capacity // block
    out = jax.ShapeDtypeStruct((nodes, latent), BF16)
    sent = (tiles, capacity * latent // LANES + MARKS, LANES)
    return pl.pallas_call(
        node_kernel,
        out_shape=(out, out, jax.ShapeDtypeStruct(sent, BF16)),
        in_specs=[whole()] * 8 + [whole(HBM)] * 3 + [whole()],
        out_specs=(whole(), whole(), whole(HBM)),
        scratch_shapes=[pltpu.VMEM(sent, BF16)]
        + [pltpu.VMEM((latent, latent), BF16)] * 3
        + [pltpu.SemaphoreType.DMA((steps,)), pltpu.SemaphoreType.DMA((3,))],
        compiler_params=pltpu.CompilerParams(vmem_limit_bytes=NODE_MIB * MIB),
        name="mesh_encoder",
    )(src.reshape(steps, 1, block), marks, *sums, mesh_feat, w_enc, w_send, w_recv, gain.reshape(1, latent))


def edge_kernel(rows_hbm, q_ref, first_ref, w_sum, w_dec, gain, mesh_ref, dec_ref, rows_ref, sem, *, per):
    tiles, height, _ = rows_ref.shape
    nodes, latent = q_ref.shape
    parts = latent // LANES
    capacity = (height - MARKS) // parts
    side = LANES // capacity
    steps = tiles // per
    loads = []
    for b in range(steps):
        part = pl.ds(b * per, per)
        loads.append(pltpu.make_async_copy(rows_hbm.at[part], rows_ref.at[part], sem.at[b]))
        loads[-1].start()
    lane = lax.broadcasted_iota(jnp.int32, (MARKS, LANES), 1)
    ids = lax.broadcasted_iota(jnp.int32, (nodes // 16, 16, LANES), 0) * 16
    ids = (ids + lax.broadcasted_iota(jnp.int32, ids.shape, 1)).astype(F32).astype(BF16)
    one, zero = jnp.ones((), BF16), jnp.zeros((), BF16)
    total = jnp.zeros((nodes, latent), F32)
    for b in range(steps):
        loads[b].wait()
        pieces = []
        for at in range(b * per, (b + 1) * per, side):
            mark = rows_ref[at, parts * capacity :, :].astype(F32)
            for k in range(1, side):
                mark = jnp.where(lane < k * capacity, mark, rows_ref[at + k, parts * capacity :, :].astype(F32))
            mark = jnp.concatenate([mark] * (16 // MARKS), axis=0).astype(BF16)
            pieces.append(jnp.where(ids == mark[None], one, zero).reshape(nodes, LANES))
        table = jnp.concatenate(pieces, axis=1)
        near = lax.dot_general(table, q_ref[...], (((0,), (0,)), ((), ())), preferred_element_type=F32)
        joined = []
        for j in range(parts):
            rows = rows_ref[b * per : (b + 1) * per, j * capacity : (j + 1) * capacity, :].reshape(per * capacity, LANES)
            joined.append(silu((rows.astype(F32) + near[:, j * LANES : (j + 1) * LANES]).astype(BF16)))
        total += jnp.dot(table, jnp.concatenate(joined, axis=1), preferred_element_type=F32)
    update = silu(jnp.dot(total.astype(BF16), w_sum[...], preferred_element_type=F32))
    out = (first_ref[...].astype(F32) + gain[...] * layer_norm(update)).astype(BF16)
    mesh_ref[...] = out
    dec_ref[...] = jnp.dot(out, w_dec[...], preferred_element_type=F32).astype(BF16)


def edge_stage(rows, q, first, w_sum, w_dec, gain):
    nodes, latent = first.shape
    per = 16
    out = jax.ShapeDtypeStruct((nodes, latent), BF16)
    return pl.pallas_call(
        functools.partial(edge_kernel, per=per),
        out_shape=(out, out),
        in_specs=[whole(HBM)] + [whole()] * 5,
        out_specs=(whole(), whole()),
        scratch_shapes=[pltpu.VMEM(rows.shape, BF16), pltpu.SemaphoreType.DMA((rows.shape[0] // per,))],
        compiler_params=pltpu.CompilerParams(vmem_limit_bytes=EDGE_MIB * MIB),
        name="mesh_edges",
    )(rows, q, first, w_sum, w_dec, gain.reshape(1, latent))


def pick_table(picks, tiles, nodes):
    rows, count = picks.shape[0], picks.shape[1] // 2
    ids = lax.broadcasted_iota(jnp.int32, (rows, LANES), 1).astype(jnp.int16)
    slots = [jnp.broadcast_to(picks[:, k : k + 1], (rows, LANES)).astype(jnp.int32).astype(jnp.int16) for k in range(count)]
    weights = [jnp.broadcast_to(picks[:, count + k : count + k + 1], (rows, LANES)).astype(BF16) for k in range(count)]
    blocks = []
    for j in (t * nodes // LANES + n for t in tiles for n in range(nodes // LANES)):
        at = ids + jnp.int16(j * LANES)
        block = jnp.zeros((rows, LANES), BF16)
        for slot, weight in zip(slots, weights):
            block = jnp.where(slot == at, weight, block)
        blocks.append(block)
    return jnp.concatenate(blocks, axis=1)


def first_kernel(picks_ref, tiles_ref, out_ref, *, tiles, inner):
    nodes = tiles_ref.shape[0] // len(tiles)
    for i in range(out_ref.shape[0] // inner):
        part = slice(i * inner, (i + 1) * inner)
        table = pick_table(picks_ref[part, :], tiles, nodes)
        out_ref[part, :] = jnp.dot(table, tiles_ref[...], preferred_element_type=F32).astype(BF16)


def first_stage(picks, tiles, source):
    rows, latent = picks.shape[0], source.shape[1]
    block = 512
    wide = pl.BlockSpec((block, latent), lambda i: (i, 0))
    return pl.pallas_call(
        functools.partial(first_kernel, tiles=tiles, inner=256),
        grid=(rows // block,),
        out_shape=jax.ShapeDtypeStruct((rows, latent), BF16),
        in_specs=[pl.BlockSpec((block, picks.shape[1]), lambda i: (i, 0)), pl.BlockSpec(source.shape, lambda i: (0, 0))],
        out_specs=wide,
        compiler_params=pltpu.CompilerParams(vmem_limit_bytes=16 * MIB),
        cost_estimate=pl.CostEstimate(
            flops=2 * rows * source.size, bytes_accessed=8 * rows * latent, transcendentals=0
        ),
        name="mesh_to_grid_first",
    )(picks, source)


def grid_kernel(picks_ref, part_ref, near_ref, far_ref, grid_ref, gain, out_ref, *, inner, tiles, nodes):
    width = near_ref.shape[0]
    for i in range(out_ref.shape[0] // inner):
        part = slice(i * inner, (i + 1) * inner)
        table = pick_table(picks_ref[part, :], tiles, nodes)
        total = part_ref[part, :].astype(F32)
        total += jnp.dot(table[:, :width], near_ref[...], preferred_element_type=F32)
        total += jnp.dot(table[:, width:], far_ref[...], preferred_element_type=F32)
        update = silu(total)
        out_ref[part, :] = (grid_ref[part, :].astype(F32) + gain[...] * layer_norm(update)).astype(BF16)


def grid_stage(picks, part, tiles, near, far, grid_feat, gain):
    rows, latent = grid_feat.shape
    block = 512
    full = pl.BlockSpec(near.shape, lambda i: (0, 0))
    wide = pl.BlockSpec((block, latent), lambda i: (i, 0))
    return pl.pallas_call(
        functools.partial(grid_kernel, inner=256, tiles=tiles, nodes=2 * near.shape[0] // len(tiles)),
        grid=(rows // block,),
        out_shape=jax.ShapeDtypeStruct((rows, latent), BF16),
        in_specs=[
            pl.BlockSpec((block, picks.shape[1]), lambda i: (i, 0)),
            wide, full, full, wide,
            pl.BlockSpec((1, latent), lambda i: (0, 0)),
        ],
        out_specs=wide,
        compiler_params=pltpu.CompilerParams(vmem_limit_bytes=16 * MIB),
        name="mesh_to_grid",
    )(picks, part, near, far, grid_feat, gain.reshape(1, latent))


def stack_kernel(near_ref, far_ref, a_ref, b_ref, own_ref, pair_ref, five_ref):
    nodes = own_ref.shape[0]
    for n, ref in enumerate((near_ref, far_ref, a_ref, b_ref, own_ref)):
        five_ref[n * nodes : (n + 1) * nodes, :] = ref[...]
    pair_ref[:nodes, :] = a_ref[...]
    pair_ref[nodes:, :] = b_ref[...]


def stack_tiles(near, far, a, b, own):
    nodes, latent = own.shape
    return pl.pallas_call(
        stack_kernel,
        out_shape=tuple(jax.ShapeDtypeStruct((n * nodes, latent), BF16) for n in (2, 5)),
        in_specs=[whole()] * 5,
        out_specs=(whole(),) * 2,
        compiler_params=pltpu.CompilerParams(vmem_limit_bytes=8 * MIB),
        name="stack_tiles",
    )(near, far, a, b, own)


def swap(block, axis, first):
    size = lax.axis_size(axis)
    pairs = [(i, (i + 1 if (i % 2 == 0) == first else i - 1) % size) for i in range(size)]
    return lax.ppermute(block, axis, pairs)


def on_device(
    grid_feat, mesh_feat, g2m_src, g2m_dst, g2m_weight, mesh_src, mesh_dst, mesh_count, m2g_src, m2g_weight,
    w_in, w_enc, w_send, w_recv, w_edge, w_node, w_dec, w_out, gain_enc, gain_node, gain_out,
):
    grid_rows, latent = grid_feat.shape
    nodes = mesh_feat.shape[0]
    lon_count = lax.axis_size("lon")
    tiles = lax.axis_size("lat") * lon_count
    band = lax.axis_index("lat")
    sector = lax.axis_index("lon")
    tile = band * lon_count + sector

    near_ab, near, far_ab, far, own_ab, own = scatter(g2m_src, g2m_dst, g2m_weight, grid_feat, w_in, nodes, lon_count)
    from_far_ab = swap(far_ab, "lon", False)
    from_near_ab = swap(near_ab, "lon", True)
    from_far = swap(far, "lon", False)
    from_near = swap(near, "lon", True)

    capacity = mesh_src.shape[2]
    live = lax.broadcasted_iota(jnp.int32, (tiles, capacity), 1) < mesh_count[0][:, None]
    marks = jnp.where(live, mesh_dst[0] & (nodes - 1), nodes).astype(F32)
    marks = jnp.tile(marks, (1, LANES // capacity))

    (own_ab,) = add_pieces(own_ab, from_near_ab, 1, F32, "add_near")
    to_a, to_b = add_pieces(own_ab, from_far_ab, 2, BF16, "add_far")
    sums = (own, swap(to_a, "lat", True), swap(to_b, "lat", False), from_near, from_far)

    first, q, rows = node_stage(
        mesh_src[0] - tile * nodes, marks, sums, mesh_feat, w_enc, w_send, w_recv, gain_enc
    )
    rows_in = lax.all_to_all(rows, ("lat", "lon"), split_axis=0, concat_axis=0, tiled=True)

    m2g_src, m2g_weight, first, w_edge, w_dec = lax.optimization_barrier((m2g_src, m2g_weight, first, w_edge, w_dec))
    shift = nodes.bit_length() - 1
    index = around_index(lax.shift_right_logical(m2g_src, shift), band, sector, lon_count)
    slots = index * nodes + (m2g_src & (nodes - 1))
    columns, weights = [slots[:, k] for k in range(slots.shape[1])], [m2g_weight[:, k] for k in range(slots.shape[1])]
    for i in range(len(columns)):
        for j in range(i + 1, len(columns)):
            same = columns[i] == columns[j]
            weights[i] = weights[i] + jnp.where(same, weights[j], 0.0)
            columns[j] = jnp.where(same, -1 - j, columns[j])
    picks = jnp.stack([c.astype(F32) for c in columns] + weights, axis=1)
    edge_node = jnp.dot(w_edge, w_node, preferred_element_type=F32).astype(BF16)
    dec_out = jnp.dot(w_dec, w_out, preferred_element_type=F32).astype(BF16)
    rows_in, picks, edge_node, dec_out = lax.optimization_barrier((rows_in, picks, edge_node, dec_out))

    mesh_out, decoded = edge_stage(rows_in, q, first, edge_node, dec_out, gain_node)

    from_a, from_b = swap(decoded, "lat", True), swap(decoded, "lat", False)
    far, near = swap(decoded, "lon", False), swap(decoded, "lon", True)
    pair, five = stack_tiles(near, far, from_a, from_b, decoded)
    far_pair, near_pair = swap(pair, "lon", False), swap(pair, "lon", True)
    part = first_stage(picks, (NEAR, FAR, A, B, OWN), five)
    late = (NEAR_A, NEAR_B, FAR_A, FAR_B)
    grid_out = grid_stage(picks, part, late, near_pair, far_pair, grid_feat, gain_out)
    return (grid_out, mesh_out)


def solution(mesh):
    tile = ("lat", "lon")
    rows, flat, cube = P(tile, None), P(tile), P(tile, None, None)
    return jax.shard_map(
        on_device,
        mesh=mesh,
        in_specs=(rows, rows, flat, flat, flat, cube, cube, rows, rows, rows) + (P(),) * 11,
        out_specs=(rows, rows),
        check_vma=False,
    )
```

time: 151 us -> 144 us (0.954)
  Pallas kernels: 41.1 us -> 37.5 us
    pallas_call x4 -> x6, Pallas kernels: 18.4 us -> 16.5 us  [the longest x1 5.95 us: edge_stage(): pl.pallas_call(functools.partial(edge_kernel, per=per), out_shape=(out, o...]
    pallas_call x1, Pallas kernels: 16 us -> 14.4 us  [scatter(): pl.pallas_call(functools.partial(scatter_kernel, nodes=nodes, lon_count=l...]
    unnamed x46 -> x42, local copies, waits for them, and re-layouts: 5.21 us -> 4.19 us
  transfers between devices with their start and end apart: 13 -> 13, of which waited for: 6 -> 7; matrix products, arithmetic and copies ran while one was open for 3% -> 2% of each run, Pallas kernels for 2% -> 3%
where the time goes in v3:
time: 144 us
  waiting for transfers between devices  73.8 us (51%)
  Pallas kernels  37.5 us (26%)
  starting transfers between devices  24.6 us (17%)
  local copies, waits for them, and re-layouts  6.16 us (4%)
    all_to_all x1, waiting for transfers between devices, on_device(): lax.all_to_all(rows, ('lat', 'lon'), split_axis=0, concat_axis=0, tiled=T...  54.1 us
    ppermute x12, waiting for transfers between devices, swap(): return lax.ppermute(block, axis, pairs)  19.7 us
    ppermute x12, starting transfers between devices, swap(): return lax.ppermute(block, axis, pairs)  15.8 us
    pallas_call x1, Pallas kernels, scatter(): pl.pallas_call(functools.partial(scatter_kernel, nodes=nodes, lon_count=l...  14.4 us
    all_to_all x1, starting transfers between devices, on_device(): lax.all_to_all(rows, ('lat', 'lon'), split_axis=0, concat_axis=0, tiled=T...  8.81 us
    pallas_call x1, Pallas kernels, node_stage(): pl.pallas_call(node_kernel, out_shape=(out, out, jax.ShapeDtypeStruct(sen...  6.54 us
    pallas_call x1, Pallas kernels, edge_stage(): pl.pallas_call(functools.partial(edge_kernel, per=per), out_shape=(out, o...  5.95 us
    pallas_call x1, Pallas kernels, grid_stage(): pl.pallas_call(functools.partial(grid_kernel, inner=256, tiles=tiles, nod...  5.8 us
  transfers between devices with their start and end apart: 13, of which 7 were waited for; matrix products, arithmetic and copies ran while one was open for 2% of the time, Pallas kernels for 3%

profile of v3, /device:TPU:0, one launch (start us, length us, event | category | flops | bytes accessed | tf_op | source)
XLA Modules:
  0.0 144.0 jit_solution(4262950501306741577)
XLA Ops:
  0.6 0.0 copy-start
  0.7 14.4 %grid_to_mesh.1 = (bf16[512,512]{1,0:T(8,128)(2,1)}, bf16[256,512]{1,0:T(8,128)(2,1)}, bf16[512,512]{1,0:T(8,128)(2,1)}, bf16[256,512]{1,0:T(8,128)(2,1)}, bf16[...) custom-call(s32[32,128]{1,0:T(8,128)} %bitcast.19, s32[32,128]{1,0:T(8,128)} %bitcast.20, f32[32,128]{1,0:T(8,128)} %bitcast.21, ...), custom_call_target="tpu_custom_call" | custom-call | tf_op jit(solution)/shard_map/grid_to_mesh/pallas_call | solution.py:153
  15.1 0.0 copy-start.18
  15.1 0.0 copy-start.20
  15.1 0.1 collective-permute-start
  15.2 5.4 %collective-permute-start.1 = (bf16[512,512]{1,0:T(8,128)(2,1)}, bf16[512,512]{1,0:T(8,128)(2,1)S(1)}, u32[]{:S(2)}, u32[]{:S(2)}) collective-permute-start(bf16[512,512]{1,0:T(8,128)(2,1)} %get-tuple-element.29), channel_id=1, source_target_pairs={{0,31},{1,2},{2,1},{3,4},{4,3},{5,6},{6,5},{7,8},{8,7},{9,10},{10,... | collective-permute-start | bytes 1572872 | tf_op jit(solution)/shard_map/ppermute | solution.py:409
  20.6 0.0 collective-permute-start.4
  20.6 0.9 collective-permute-start.5
  21.5 0.0 collective-permute-done.b_ref
  21.5 1.0 copy-done.2
  22.6 0.1 add_near.1.a_ref
  22.7 5.0 %collective-permute-done.1.b_ref = bf16[512,512]{1,0:T(8,128)(2,1)S(1)} collective-permute-done((bf16[512,512]{1,0:T(8,128)(2,1)}, bf16[512,512]{1,0:T(8,128)(2,1)S(1)}, u32[]{:S(2)}, u32[]{:S(2)}) %collective-permute-start.1) | collective-permute-done | bytes 524320 | tf_op jit(solution)/shard_map/ppermute | solution.py:409
  27.7 0.1 add_far.1
  27.8 2.0 %collective-permute-start.2 = (bf16[256,512]{1,0:T(8,128)(2,1)S(1)}, bf16[256,512]{1,0:T(8,128)(2,1)S(1)}, u32[]{:S(2)}, u32[]{:S(2)}) collective-permute-start(bf16[256,512]{1,0:T(8,128)(2,1)S(1)} %get-tuple-element.30), channel_id=1, source_target_pairs={{0,32},{32,0},{64,96},{96,64},{1,33},{33,1},{65,97},{97,65},{2,34}... | collective-permute-start | bytes 786440 | tf_op jit(solution)/shard_map/ppermute | solution.py:409
  29.7 2.5 %collective-permute-start.3 = (bf16[256,512]{1,0:T(8,128)(2,1)S(1)}, bf16[256,512]{1,0:T(8,128)(2,1)S(1)}, u32[]{:S(2)}, u32[]{:S(2)}) collective-permute-start(bf16[256,512]{1,0:T(8,128)(2,1)S(1)} %get-tuple-element.31), channel_id=1, source_target_pairs={{0,96},{32,64},{64,32},{96,0},{1,97},{33,65},{65,33},{97,1},{2,98}... | collective-permute-start | bytes 786440 | tf_op jit(solution)/shard_map/ppermute | solution.py:409
  32.3 0.1 copy.50
  32.4 0.7 sub.47.src_ref
  33.1 0.0 copy-done.19
  33.1 0.7 copy.52.mark_ref
  33.8 0.0 collective-permute-done.4.near_ref
  33.8 0.0 collective-permute-done.5.far_ref
  33.8 0.0 copy-start.13
  33.9 0.3 collective-permute-done.2.a_ref
  34.2 3.1 %collective-permute-done.3.b_ref = bf16[256,512]{1,0:T(8,128)(2,1)S(1)} collective-permute-done((bf16[256,512]{1,0:T(8,128)(2,1)S(1)}, bf16[256,512]{1,0:T(8,128)(2,1)S(1)}, u32[]{:S(2)}, u32[]{:S(2)}) %collective-permute-start.3) | collective-permute-done | bytes 262176 | tf_op jit(solution)/shard_map/ppermute | solution.py:409
  37.3 0.7 copy-done.15
  38.0 6.5 %mesh_encoder.1 = (bf16[256,512]{1,0:T(8,128)(2,1)}, bf16[256,512]{1,0:T(8,128)(2,1)}, bf16[128,136,128]{2,1,0:T(8,128)(2,1)}) custom-call(s32[8,1,512]{2,1,0:T(1,128)} %sub.47.src_ref, f32[128,128]{1,0:T(8,128)} %copy.52.mark_ref, bf16[256,512]{1,0:T(8,128)(2,1)} %get-tuple-element.26.own_ref, bf16[256,512]{1,0:T(8,128)(2,1)} %copy-done.14, ...), custom_call_target="tpu_custom_call" | custom-call | tf_op jit(solution)/shard_map/mesh_encoder/pallas_call | solution.py:246
  44.6 0.0 copy-start.16
  44.6 0.0 copy-start.17
  44.6 0.0 copy-start.9
  44.6 0.0 copy-start.10
  44.6 0.0 copy-start.11
  44.6 8.8 %all-to-all-start = ((bf16[128,136,128]{2,1,0:T(8,128)(2,1)}), bf16[128,136,128]{2,1,0:T(8,128)(2,1)}, u32[]{:S(2)}, u32[]{:S(2)}) async-start(bf16[128,136,128]{2,1,0:T(8,128)(2,1)} %get-tuple-element.34), calls=%async_computation | async-start | bytes 8912896 | tf_op jit(solution)/shard_map/all_to_all | solution.py:442
  53.5 0.0 copy-start.5
  53.5 0.1 and_add_fusion
  53.7 0.1 stack.2
  53.8 0.0 copy-done
  53.8 0.0 copy-done.9
  53.8 0.4 convolution_convert_fusion.1.w_sum
  54.3 0.0 copy-done.10
  54.3 0.0 copy-done.11
  54.3 0.4 convolution_convert_fusion.w_dec
  54.7 54.1 %all-to-all-done.rows_hbm = bf16[128,136,128]{2,1,0:T(8,128)(2,1)} async-done(((bf16[128,136,128]{2,1,0:T(8,128)(2,1)}), bf16[128,136,128]{2,1,0:T(8,128)(2,1)}, u32[]{:S(2)}, u32[]{:S(2)}) %all-to-all-start) | async-done | bytes 4456480 | tf_op jit(solution)/shard_map/all_to_all | solution.py:442
  108.8 0.0 copy-done.5
  108.8 6.0 %mesh_edges.1 = (bf16[256,512]{1,0:T(8,128)(2,1)}, bf16[256,512]{1,0:T(8,128)(2,1)S(1)}) custom-call(bf16[128,136,128]{2,1,0:T(8,128)(2,1)} %all-to-all-done.rows_hbm, bf16[256,512]{1,0:T(8,128)(2,1)S(1)} %copy-done.4, bf16[256,512]{1,0:T(8,128)(2,1)S(1)} %copy-done.3, bf16[512,512]{1,0:T(8,128)(2,1)S(1)} %convolution_convert_fusion.1.w_sum, ...), custom_call_target="tpu_custom_call" | custom-call | tf_op jit(solution)/shard_map/mesh_edges/pallas_call | solution.py:302
  114.7 0.1 collective-permute-start.6
  114.8 1.2 collective-permute-start.7
  116.0 0.8 collective-permute-start.8
  116.8 0.4 collective-permute-start.9
  117.2 0.0 collective-permute-done.6.near_ref
  117.2 6.8 %collective-permute-done.7.far_ref = bf16[256,512]{1,0:T(8,128)(2,1)S(1)} collective-permute-done((bf16[256,512]{1,0:T(8,128)(2,1)S(1)}, bf16[256,512]{1,0:T(8,128)(2,1)S(1)}, u32[]{:S(2)}, u32[]{:S(2)}) %collective-permute-start.7) | collective-permute-done | bytes 262176 | tf_op jit(solution)/shard_map/ppermute | solution.py:409
  124.0 0.0 collective-permute-done.8.a_ref
  124.0 1.1 collective-permute-done.9.b_ref
  125.1 0.1 stack_tiles.1
  125.2 0.0 copy-start.7
  125.3 1.0 copy-done.7
  126.3 0.0 collective-permute-start.10
  126.3 2.3 %collective-permute-start.11 = (bf16[512,512]{1,0:T(8,128)(2,1)S(1)}, bf16[512,512]{1,0:T(8,128)(2,1)S(1)}, u32[]{:S(2)}, u32[]{:S(2)}) collective-permute-start(bf16[512,512]{1,0:T(8,128)(2,1)S(1)} %get-tuple-element.48), channel_id=1, source_target_pairs={{0,31},{1,2},{2,1},{3,4},{4,3},{5,6},{6,5},{7,8},{8,7},{9,10},{10,... | collective-permute-start | bytes 1572872 | tf_op jit(solution)/shard_map/ppermute | solution.py:409
  128.7 0.4 copy.54.picks_ref
  129.0 0.0 copy-start.8
  129.0 1.3 copy-done.8
  130.3 4.5 %mesh_to_grid_first.1.part_ref = bf16[2048,512]{1,0:T(8,128)(2,1)S(1)} custom-call(f32[2048,6]{1,0:T(8,128)S(1)} %copy.54.picks_ref, bf16[1280,512]{1,0:T(8,128)(2,1)S(1)} %copy-done.8), custom_call_target="tpu_custom_call" | custom-call | flops 2684354560 | bytes 8388608 | tf_op jit(solution)/shard_map/mesh_to_grid_first/pallas_call | solution.py:340
  134.8 0.0 collective-permute-done.10.near_ref
  134.8 3.4 %collective-permute-done.11.far_ref = bf16[512,512]{1,0:T(8,128)(2,1)S(1)} collective-permute-done((bf16[512,512]{1,0:T(8,128)(2,1)S(1)}, bf16[512,512]{1,0:T(8,128)(2,1)S(1)}, u32[]{:S(2)}, u32[]{:S(2)}) %collective-permute-start.11) | collective-permute-done | bytes 524320 | tf_op jit(solution)/shard_map/ppermute | solution.py:409
  138.2 5.8 %mesh_to_grid.1 = bf16[2048,512]{1,0:T(8,128)(2,1)} custom-call(f32[2048,6]{1,0:T(8,128)S(1)} %copy.54.picks_ref, bf16[2048,512]{1,0:T(8,128)(2,1)S(1)} %mesh_to_grid_first.1.part_ref, bf16[512,512]{1,0:T(8,128)(2,1)S(1)} %collective-permute-done.10.near_ref, bf16[512,512]{1,0:T(8,128)(2,1)S(1)} %collective-permute-done.11.far_ref, ...), custom_call_target="tpu_custom_call" | custom-call | tf_op jit(solution)/shard_map/mesh_to_grid/pallas_call | solution.py:371
  (25 shorter events, 0.1 us)
Async XLA Ops:
  0.6 53.2 %copy-start = (bf16[512,512]{1,0:T(8,128)(2,1)S(1)}, bf16[512,512]{1,0:T(8,128)(2,1)}, u32[]{:S(2)}) copy-start(bf16[512,512]{1,0:T(8,128)(2,1)} %param.35) | copy-start | bytes 1572868
  0.6 32.4 %copy-start.19 = (s32[1,128,32]{1,2,0:T(8,128)S(1)}, s32[1,128,32]{1,2,0:T(8,128)}, u32[]{:S(2)}) copy-start(s32[1,128,32]{1,2,0:T(8,128)} %param.27) | copy-start | bytes 49156
  15.1 17.2 %copy-start.18 = (s32[1,128,32]{1,2,0:T(8,128)S(1)}, s32[1,128,32]{1,2,0:T(8,128)}, u32[]{:S(2)}) copy-start(s32[1,128,32]{1,2,0:T(8,128)} %param.26) | copy-start | bytes 49156
  15.1 18.0 %copy-start.20 = (s32[1,128]{1,0:T(1,128)S(1)}, s32[1,128]{1,0:T(1,128)}, u32[]{:S(2)}) copy-start(s32[1,128]{1,0:T(1,128)} %param.28) | copy-start | bytes 1540
  15.1 6.4 %collective-permute-start = (bf16[512,512]{1,0:T(8,128)(2,1)}, bf16[512,512]{1,0:T(8,128)(2,1)S(1)}, u32[]{:S(2)}, u32[]{:S(2)}) collective-permute-start(bf16[512,512]{1,0:T(8,128)(2,1)} %get-tuple-element.28), channel_id=1, source_target_pairs={{0,1},{1,0},{2,3},{3,2},{4,5},{5,4},{6,7},{7,6},{8,9},{9,8},{10,11... | collective-permute-start | bytes 1572872 | tf_op jit(solution)/shard_map/ppermute | solution.py:409
  15.2 12.5 %collective-permute-start.1 = (bf16[512,512]{1,0:T(8,128)(2,1)}, bf16[512,512]{1,0:T(8,128)(2,1)S(1)}, u32[]{:S(2)}, u32[]{:S(2)}) collective-permute-start(bf16[512,512]{1,0:T(8,128)(2,1)} %get-tuple-element.29), channel_id=1, source_target_pairs={{0,31},{1,2},{2,1},{3,4},{4,3},{5,6},{6,5},{7,8},{8,7},{9,10},{10,... | collective-permute-start | bytes 1572872 | tf_op jit(solution)/shard_map/ppermute | solution.py:409
  20.6 13.3 %collective-permute-start.4 = (bf16[256,512]{1,0:T(8,128)(2,1)}, bf16[256,512]{1,0:T(8,128)(2,1)S(1)}, u32[]{:S(2)}, u32[]{:S(2)}) collective-permute-start(bf16[256,512]{1,0:T(8,128)(2,1)} %get-tuple-element.32), channel_id=1, source_target_pairs={{0,1},{1,0},{2,3},{3,2},{4,5},{5,4},{6,7},{7,6},{8,9},{9,8},{10,11... | collective-permute-start | bytes 786440 | tf_op jit(solution)/shard_map/ppermute | solution.py:409
  20.6 13.3 %collective-permute-start.5 = (bf16[256,512]{1,0:T(8,128)(2,1)}, bf16[256,512]{1,0:T(8,128)(2,1)S(1)}, u32[]{:S(2)}, u32[]{:S(2)}) collective-permute-start(bf16[256,512]{1,0:T(8,128)(2,1)} %get-tuple-element.33), channel_id=1, source_target_pairs={{0,31},{1,2},{2,1},{3,4},{4,3},{5,6},{6,5},{7,8},{8,7},{9,10},{10,... | collective-permute-start | bytes 786440 | tf_op jit(solution)/shard_map/ppermute | solution.py:409
  21.5 1.0 copy-start.2
  27.8 6.5 %collective-permute-start.2 = (bf16[256,512]{1,0:T(8,128)(2,1)S(1)}, bf16[256,512]{1,0:T(8,128)(2,1)S(1)}, u32[]{:S(2)}, u32[]{:S(2)}) collective-permute-start(bf16[256,512]{1,0:T(8,128)(2,1)S(1)} %get-tuple-element.30), channel_id=1, source_target_pairs={{0,32},{32,0},{64,96},{96,64},{1,33},{33,1},{65,97},{97,65},{2,34}... | collective-permute-start | bytes 786440 | tf_op jit(solution)/shard_map/ppermute | solution.py:409
  29.7 7.6 %collective-permute-start.3 = (bf16[256,512]{1,0:T(8,128)(2,1)S(1)}, bf16[256,512]{1,0:T(8,128)(2,1)S(1)}, u32[]{:S(2)}, u32[]{:S(2)}) collective-permute-start(bf16[256,512]{1,0:T(8,128)(2,1)S(1)} %get-tuple-element.31), channel_id=1, source_target_pairs={{0,96},{32,64},{64,32},{96,0},{1,97},{33,65},{65,33},{97,1},{2,98}... | collective-permute-start | bytes 786440 | tf_op jit(solution)/shard_map/ppermute | solution.py:409
  33.8 3.5 %copy-start.12 = (bf16[256,512]{1,0:T(8,128)(2,1)}, bf16[256,512]{1,0:T(8,128)(2,1)S(1)}, u32[]{:S(2)}) copy-start(bf16[256,512]{1,0:T(8,128)(2,1)S(1)} %collective-permute-done.4.near_ref) | copy-start | bytes 786436
  33.8 3.5 %copy-start.13 = (bf16[256,512]{1,0:T(8,128)(2,1)}, bf16[256,512]{1,0:T(8,128)(2,1)S(1)}, u32[]{:S(2)}) copy-start(bf16[256,512]{1,0:T(8,128)(2,1)S(1)} %collective-permute-done.5.far_ref) | copy-start | bytes 786436
  34.2 3.1 %copy-start.14 = (bf16[256,512]{1,0:T(8,128)(2,1)}, bf16[256,512]{1,0:T(8,128)(2,1)S(1)}, u32[]{:S(2)}) copy-start(bf16[256,512]{1,0:T(8,128)(2,1)S(1)} %collective-permute-done.2.a_ref) | copy-start | bytes 786436
  37.3 0.7 copy-start.15
  44.6 8.9 %copy-start.16 = (s32[2048,3]{0,1:T(4,128)S(1)}, s32[2048,3]{0,1:T(4,128)}, u32[]{:S(2)}) copy-start(s32[2048,3]{0,1:T(4,128)} %param.29) | copy-start | bytes 73732
  44.6 9.0 %copy-start.17 = (f32[2048,3]{0,1:T(4,128)S(1)}, f32[2048,3]{0,1:T(4,128)}, u32[]{:S(2)}) copy-start(f32[2048,3]{0,1:T(4,128)} %param.30) | copy-start | bytes 73732
  44.6 9.2 %copy-start.9 = (bf16[512,512]{1,0:T(8,128)(2,1)S(1)}, bf16[512,512]{1,0:T(8,128)(2,1)}, u32[]{:S(2)}) copy-start(bf16[512,512]{1,0:T(8,128)(2,1)} %param.36) | copy-start | bytes 1572868
  44.6 9.6 %copy-start.10 = (bf16[512,512]{1,0:T(8,128)(2,1)S(1)}, bf16[512,512]{1,0:T(8,128)(2,1)}, u32[]{:S(2)}) copy-start(bf16[512,512]{1,0:T(8,128)(2,1)} %param.37) | copy-start | bytes 1572868
  44.6 9.6 %copy-start.11 = (bf16[512,512]{1,0:T(8,128)(2,1)S(1)}, bf16[512,512]{1,0:T(8,128)(2,1)}, u32[]{:S(2)}) copy-start(bf16[512,512]{1,0:T(8,128)(2,1)} %param.38) | copy-start | bytes 1572868
  44.6 64.1 %all-to-all-start = ((bf16[128,136,128]{2,1,0:T(8,128)(2,1)}), bf16[128,136,128]{2,1,0:T(8,128)(2,1)}, u32[]{:S(2)}, u32[]{:S(2)}) async-start(bf16[128,136,128]{2,1,0:T(8,128)(2,1)} %get-tuple-element.34), calls=%async_computation | async-start | bytes 8912896 | tf_op jit(solution)/shard_map/all_to_all | solution.py:442
  53.5 55.3 %copy-start.3 = (bf16[256,512]{1,0:T(8,128)(2,1)S(1)}, bf16[256,512]{1,0:T(8,128)(2,1)}, u32[]{:S(2)}) copy-start(bf16[256,512]{1,0:T(8,128)(2,1)} %get-tuple-element.43.first_ref) | copy-start | bytes 786436
  53.5 55.3 %copy-start.4 = (bf16[256,512]{1,0:T(8,128)(2,1)S(1)}, bf16[256,512]{1,0:T(8,128)(2,1)}, u32[]{:S(2)}) copy-start(bf16[256,512]{1,0:T(8,128)(2,1)} %get-tuple-element.42.q_ref) | copy-start | bytes 786436
  53.5 55.3 %copy-start.5 = (f32[512]{0:T(512)S(1)}, f32[512]{0:T(512)}, u32[]{:S(2)}) copy-start(f32[512]{0:T(512)} %param.40) | copy-start | bytes 6148
  114.7 2.5 %collective-permute-start.6 = (bf16[256,512]{1,0:T(8,128)(2,1)S(1)}, bf16[256,512]{1,0:T(8,128)(2,1)S(1)}, u32[]{:S(2)}, u32[]{:S(2)}) collective-permute-start(bf16[256,512]{1,0:T(8,128)(2,1)S(1)} %get-tuple-element.46.own_ref), channel_id=1, source_target_pairs={{0,1},{1,0},{2,3},{3,2},{4,5},{5,4},{6,7},{7,6},{8,9},{9,8},{10,11... | collective-permute-start | bytes 786440 | tf_op jit(solution)/shard_map/ppermute | solution.py:409
  114.8 9.2 %collective-permute-start.7 = (bf16[256,512]{1,0:T(8,128)(2,1)S(1)}, bf16[256,512]{1,0:T(8,128)(2,1)S(1)}, u32[]{:S(2)}, u32[]{:S(2)}) collective-permute-start(bf16[256,512]{1,0:T(8,128)(2,1)S(1)} %get-tuple-element.46.own_ref), channel_id=1, source_target_pairs={{0,31},{1,2},{2,1},{3,4},{4,3},{5,6},{6,5},{7,8},{8,7},{9,10},{10,... | collective-permute-start | bytes 786440 | tf_op jit(solution)/shard_map/ppermute | solution.py:409
  116.0 8.0 %collective-permute-start.8 = (bf16[256,512]{1,0:T(8,128)(2,1)S(1)}, bf16[256,512]{1,0:T(8,128)(2,1)S(1)}, u32[]{:S(2)}, u32[]{:S(2)}) collective-permute-start(bf16[256,512]{1,0:T(8,128)(2,1)S(1)} %get-tuple-element.46.own_ref), channel_id=1, source_target_pairs={{0,32},{32,0},{64,96},{96,64},{1,33},{33,1},{65,97},{97,65},{2,34}... | collective-permute-start | bytes 786440 | tf_op jit(solution)/shard_map/ppermute | solution.py:409
  116.8 8.3 %collective-permute-start.9 = (bf16[256,512]{1,0:T(8,128)(2,1)S(1)}, bf16[256,512]{1,0:T(8,128)(2,1)S(1)}, u32[]{:S(2)}, u32[]{:S(2)}) collective-permute-start(bf16[256,512]{1,0:T(8,128)(2,1)S(1)} %get-tuple-element.46.own_ref), channel_id=1, source_target_pairs={{0,96},{32,64},{64,32},{96,0},{1,97},{33,65},{65,33},{97,1},{2,98}... | collective-permute-start | bytes 786440 | tf_op jit(solution)/shard_map/ppermute | solution.py:409
  125.2 1.1 copy-start.7
  126.3 8.5 %collective-permute-start.10 = (bf16[512,512]{1,0:T(8,128)(2,1)S(1)}, bf16[512,512]{1,0:T(8,128)(2,1)S(1)}, u32[]{:S(2)}, u32[]{:S(2)}) collective-permute-start(bf16[512,512]{1,0:T(8,128)(2,1)S(1)} %get-tuple-element.48), channel_id=1, source_target_pairs={{0,1},{1,0},{2,3},{3,2},{4,5},{5,4},{6,7},{7,6},{8,9},{9,8},{10,11... | collective-permute-start | bytes 1572872 | tf_op jit(solution)/shard_map/ppermute | solution.py:409
  126.3 11.9 %collective-permute-start.11 = (bf16[512,512]{1,0:T(8,128)(2,1)S(1)}, bf16[512,512]{1,0:T(8,128)(2,1)S(1)}, u32[]{:S(2)}, u32[]{:S(2)}) collective-permute-start(bf16[512,512]{1,0:T(8,128)(2,1)S(1)} %get-tuple-element.48), channel_id=1, source_target_pairs={{0,31},{1,2},{2,1},{3,4},{4,3},{5,6},{6,5},{7,8},{8,7},{9,10},{10,... | collective-permute-start | bytes 1572872 | tf_op jit(solution)/shard_map/ppermute | solution.py:409
  129.0 1.3 copy-start.8
  130.3 7.9 %copy-start.1 = (bf16[2048,512]{1,0:T(8,128)(2,1)S(1)}, bf16[2048,512]{1,0:T(8,128)(2,1)}, u32[]{:S(2)}) copy-start(bf16[2048,512]{1,0:T(8,128)(2,1)} %grid_ref.1) | copy-start | bytes 6291460
  130.3 7.9 %copy-start.6 = (f32[512]{0:T(512)S(1)}, f32[512]{0:T(512)}, u32[]{:S(2)}) copy-start(f32[512]{0:T(512)} %param.41) | copy-start | bytes 6148

commit v4 on v3

--- a/solution.py
+++ b/solution.py
@@ -17,6 +17,10 @@
 VMEM = pltpu.VMEM
 SMEM = pltpu.SMEM
 HBM = pltpu.HBM
+
+
+def silu_of_half(half):
+    return half + half * jnp.tanh(half)
 
 
 def silu(v):
@@ -52,10 +56,10 @@
 
 
 def scatter_kernel(src_hbm, dst_hbm, wgt_hbm, grid_hbm, w_hbm, *refs, nodes, lon_count):
-    count = len(refs) - 16
+    count = len(refs) - 17
     outs = refs[:count]
     accs = refs[count : count + 4]
-    y_ref, stage_ref, grid_ref, w_ref, src_v, dst_v, src_s, dst_s, wgt_s, grid_sem, out_sem, sem = refs[count + 4 :]
+    y_ref, stage_ref, grid_ref, w_ref, wide_ref, src_v, dst_v, wgt_v, src_s, dst_s, grid_sem, out_sem, sem = refs[count + 4 :]
     rows, latent = grid_ref.shape
     parts = latent // LANES
     step = 256
@@ -68,15 +72,18 @@
     w_in = pltpu.make_async_copy(w_hbm, w_ref, sem.at[3])
     src_in = pltpu.make_async_copy(src_hbm, src_v, sem.at[0])
     dst_in = pltpu.make_async_copy(dst_hbm, dst_v, sem.at[1])
-    wgt_in = pltpu.make_async_copy(wgt_hbm, wgt_s, sem.at[2])
+    wgt_in = pltpu.make_async_copy(wgt_hbm, wgt_v, sem.at[2])
     src_out = pltpu.make_async_copy(src_v, src_s, sem.at[4])
     dst_out = pltpu.make_async_copy(dst_v, dst_s, sem.at[5])
-    w_in.start()
-    grid_copy(0).start()
-    for copy in (src_in, dst_in, wgt_in):
+    for copy in (wgt_in, w_in, grid_copy(0), src_in, dst_in):
         copy.start()
     for i in range(1, chunks):
         grid_copy(i).start()
+    lines, width = src_s.shape
+    wgt_in.wait()
+    turned = jnp.transpose(wgt_v[...])
+    for i in range(lines):
+        wide_ref[i * width : (i + 1) * width, :] = jnp.broadcast_to(turned[:, i : i + 1], (width, LANES))
     w_in.wait()
 
     span = accs[0].shape[0] // chunks
@@ -103,12 +110,10 @@
     dst_v[...] = (index * nodes + (dst & (nodes - 1))) * parts
     dst_out.start()
     lax.fori_loop(1, chunks, project, 0)
-    wgt_in.wait()
     src_out.wait()
     dst_out.wait()
 
     count = len(accs)
-    lines, width = src_s.shape
 
     def add_edges(i, carry):
         for u in range(0, width, count):
@@ -117,7 +122,8 @@
                 s = pl.multiple_of(src_s[i, u + n], parts)
                 d = pl.multiple_of(dst_s[i, u + n], parts)
                 places.append(d)
-                sums.append(acc[pl.ds(d, parts), :] + wgt_s[i, u + n] * y_ref[pl.ds(s, parts), :])
+                w = wide_ref[pl.ds(i * width + u + n, 1), :]
+                sums.append(acc[pl.ds(d, parts), :] + w * y_ref[pl.ds(s, parts), :])
             for acc, d, total in zip(accs, places, sums):
                 acc[pl.ds(d, parts), :] = total
         return carry
@@ -148,7 +154,7 @@
     parts = latent // LANES
     slots = 9 * nodes
     lines = src.shape[0] // LANES
-    outs = tuple(jax.ShapeDtypeStruct((n * nodes, latent), BF16) for n in (2, 1, 2, 1, 2, 1))
+    outs = tuple(jax.ShapeDtypeStruct((n * nodes, latent), BF16) for n in (2, 1, 1, 1, 1, 2, 1))
     ints = pltpu.VMEM((lines, LANES), jnp.int32)
     return pl.pallas_call(
         functools.partial(scatter_kernel, nodes=nodes, lon_count=lon_count),
@@ -161,13 +167,14 @@
             pltpu.VMEM((slots, latent), BF16),
             pltpu.VMEM((rows, latent), BF16),
             pltpu.VMEM(w_in.shape, BF16),
+            pltpu.VMEM((lines * LANES, LANES), F32),
             ints,
             ints,
+            pltpu.VMEM((lines, LANES), F32),
             pltpu.SMEM((lines, LANES), jnp.int32),
             pltpu.SMEM((lines, LANES), jnp.int32),
-            pltpu.SMEM((lines, LANES), F32),
             pltpu.SemaphoreType.DMA((rows // 256,)),
-            pltpu.SemaphoreType.DMA((6,)),
+            pltpu.SemaphoreType.DMA((7,)),
             pltpu.SemaphoreType.DMA((6,)),
         ],
         compiler_params=pltpu.CompilerParams(vmem_limit_bytes=60 * MIB),
@@ -176,44 +183,61 @@
 
 
 def add_kernel(a_ref, b_ref, *outs):
-    rows = outs[0].shape[0]
-    for n, out in enumerate(outs):
-        part = slice(n * rows, (n + 1) * rows)
+    start = 0
+    for out in outs:
+        part = slice(start, start + out.shape[0])
         out[...] = (a_ref[part, :].astype(F32) + b_ref[part, :].astype(F32)).astype(out.dtype)
-
-
-def add_pieces(a, b, pieces, dtype, name):
-    out = jax.ShapeDtypeStruct((a.shape[0] // pieces, a.shape[1]), dtype)
+        start += out.shape[0]
+
+
+def add_near(own, near):
+    out = jax.ShapeDtypeStruct((own.shape[0] // 2, own.shape[1]), F32)
     return pl.pallas_call(
         add_kernel,
-        out_shape=(out,) * pieces,
+        out_shape=(out, out),
         in_specs=[whole()] * 2,
-        out_specs=(whole(),) * pieces,
+        out_specs=(whole(),) * 2,
         compiler_params=pltpu.CompilerParams(vmem_limit_bytes=8 * MIB),
-        name=name,
-    )(a, b)
-
-
-def node_kernel(src_ref, mark_ref, own_ref, a_ref, b_ref, near_ref, far_ref, mesh_ref, enc_hbm, send_hbm, recv_hbm, gain, first_ref, q_ref, rows_hbm, rows_ref, w_enc, w_send, w_recv, sem, w_sem):
-    tiles, _, _ = rows_ref.shape
-    capacity = (rows_ref.shape[1] - MARKS) * LANES // mesh_ref.shape[1]
-    parts = mesh_ref.shape[1] // LANES
-    loads = [
-        pltpu.make_async_copy(hbm, ref, w_sem.at[n])
-        for n, (hbm, ref) in enumerate(((enc_hbm, w_enc), (send_hbm, w_send), (recv_hbm, w_recv)))
-    ]
+        name="add_near",
+    )(own, near)
+
+
+def add_far(far, own):
+    return pl.pallas_call(
+        add_kernel,
+        out_shape=jax.ShapeDtypeStruct(far.shape, BF16),
+        in_specs=[whole()] * 2,
+        out_specs=whole(),
+        compiler_params=pltpu.CompilerParams(vmem_limit_bytes=8 * MIB),
+        name="add_far",
+    )(far, own)
+
+
+def node_kernel(*refs, pieces):
+    count = pieces + 7
+    sources, (first_hbm, q_hbm, rows_hbm), held = refs[:count], refs[count : count + 3], refs[count + 3 : 2 * count + 3]
+    first_ref, q_ref, rows_ref, in_sem, out_sem, sem = refs[2 * count + 3 :]
+    loads = [pltpu.make_async_copy(a, b, in_sem.at[n]) for n, (a, b) in enumerate(zip(sources, held))]
     for load in loads:
         load.start()
-    nodes = mesh_ref.shape[0]
-    pooled = own_ref[...].astype(F32)
-    for ref in (a_ref, b_ref, near_ref, far_ref):
-        pooled += ref[ref.shape[0] - nodes :, :].astype(F32)
+    w_enc, mesh_ref, gain, w_send, w_recv, src_ref, mark_ref = held[pieces:]
+    nodes, latent = mesh_ref.shape
+    capacity = (rows_ref.shape[1] - MARKS) * LANES // latent
+    parts = latent // LANES
     loads[0].wait()
+    pooled = held[0][...].astype(F32)
+    for n in range(1, pieces):
+        loads[n].wait()
+        pooled += held[n][...].astype(F32)
+    loads[pieces].wait()
     update = silu(jnp.dot(pooled.astype(BF16), w_enc[...], preferred_element_type=F32))
+    for load in loads[pieces + 1 :]:
+        load.wait()
     first = (mesh_ref[...].astype(F32) + gain[...] * layer_norm(update)).astype(BF16)
     first_ref[...] = first
-    loads[1].wait()
-    p = jnp.dot(first, w_send[...], preferred_element_type=F32).astype(BF16)
+    first_out = pltpu.make_async_copy(first_ref, first_hbm, out_sem.at[0])
+    first_out.start()
+    p = (0.5 * jnp.dot(first, w_send[...], preferred_element_type=F32)).astype(BF16)
     blocks, _, block = src_ref.shape
     per = block // capacity
     ids = lax.broadcasted_iota(jnp.int32, (nodes, block), 0)
@@ -230,9 +254,10 @@
         rows_ref[part, parts * capacity :, :] = jnp.broadcast_to(mark[:, None, :], (per, MARKS, LANES)).astype(BF16)
         copies.append(pltpu.make_async_copy(rows_ref.at[part], rows_hbm.at[part], sem.at[i]))
         copies[-1].start()
-    loads[2].wait()
-    q_ref[...] = jnp.dot(first, w_recv[...], preferred_element_type=F32).astype(BF16)
-    for copy in copies:
+    q_ref[...] = (0.5 * jnp.dot(first, w_recv[...], preferred_element_type=F32)).astype(BF16)
+    q_out = pltpu.make_async_copy(q_ref, q_hbm, out_sem.at[1])
+    q_out.start()
+    for copy in (first_out, q_out, *copies):
         copy.wait()
 
 
@@ -243,20 +268,22 @@
     steps = tiles * capacity // block
     out = jax.ShapeDtypeStruct((nodes, latent), BF16)
     sent = (tiles, capacity * latent // LANES + MARKS, LANES)
-    return pl.pallas_call(
-        node_kernel,
+    inputs = (*sums, w_enc, mesh_feat, gain.reshape(1, latent), w_send, w_recv, src.reshape(steps, 1, block), marks)
+    return pl.pallas_call(
+        functools.partial(node_kernel, pieces=len(sums)),
         out_shape=(out, out, jax.ShapeDtypeStruct(sent, BF16)),
-        in_specs=[whole()] * 8 + [whole(HBM)] * 3 + [whole()],
-        out_specs=(whole(), whole(), whole(HBM)),
-        scratch_shapes=[pltpu.VMEM(sent, BF16)]
-        + [pltpu.VMEM((latent, latent), BF16)] * 3
-        + [pltpu.SemaphoreType.DMA((steps,)), pltpu.SemaphoreType.DMA((3,))],
+        in_specs=[whole(HBM)] * len(inputs),
+        out_specs=(whole(HBM),) * 3,
+        scratch_shapes=[pltpu.VMEM(v.shape, v.dtype) for v in inputs]
+        + [pltpu.VMEM((nodes, latent), BF16)] * 2
+        + [pltpu.VMEM(sent, BF16)]
+        + [pltpu.SemaphoreType.DMA((n,)) for n in (len(inputs), 2, steps)],
         compiler_params=pltpu.CompilerParams(vmem_limit_bytes=NODE_MIB * MIB),
         name="mesh_encoder",
-    )(src.reshape(steps, 1, block), marks, *sums, mesh_feat, w_enc, w_send, w_recv, gain.reshape(1, latent))
-
-
-def edge_kernel(rows_hbm, q_ref, first_ref, w_sum, w_dec, gain, mesh_ref, dec_ref, rows_ref, sem, *, per):
+    )(*inputs)
+
+
+def edge_kernel(rows_hbm, q_ref, first_ref, w_sum, w_dec, gain, mesh_hbm, dec_ref, rows_ref, mesh_ref, sem, out_sem, *, per):
     tiles, height, _ = rows_ref.shape
     nodes, latent = q_ref.shape
     parts = latent // LANES
@@ -287,12 +314,15 @@
         joined = []
         for j in range(parts):
             rows = rows_ref[b * per : (b + 1) * per, j * capacity : (j + 1) * capacity, :].reshape(per * capacity, LANES)
-            joined.append(silu((rows.astype(F32) + near[:, j * LANES : (j + 1) * LANES]).astype(BF16)))
+            joined.append(silu_of_half((rows.astype(F32) + near[:, j * LANES : (j + 1) * LANES]).astype(BF16)))
         total += jnp.dot(table, jnp.concatenate(joined, axis=1), preferred_element_type=F32)
     update = silu(jnp.dot(total.astype(BF16), w_sum[...], preferred_element_type=F32))
     out = (first_ref[...].astype(F32) + gain[...] * layer_norm(update)).astype(BF16)
     mesh_ref[...] = out
+    copy = pltpu.make_async_copy(mesh_ref, mesh_hbm, out_sem)
+    copy.start()
     dec_ref[...] = jnp.dot(out, w_dec[...], preferred_element_type=F32).astype(BF16)
+    copy.wait()
 
 
 def edge_stage(rows, q, first, w_sum, w_dec, gain):
@@ -303,8 +333,13 @@
         functools.partial(edge_kernel, per=per),
         out_shape=(out, out),
         in_specs=[whole(HBM)] + [whole()] * 5,
-        out_specs=(whole(), whole()),
-        scratch_shapes=[pltpu.VMEM(rows.shape, BF16), pltpu.SemaphoreType.DMA((rows.shape[0] // per,))],
+        out_specs=(whole(HBM), whole()),
+        scratch_shapes=[
+            pltpu.VMEM(rows.shape, BF16),
+            pltpu.VMEM((nodes, latent), BF16),
+            pltpu.SemaphoreType.DMA((rows.shape[0] // per,)),
+            pltpu.SemaphoreType.DMA,
+        ],
         compiler_params=pltpu.CompilerParams(vmem_limit_bytes=EDGE_MIB * MIB),
         name="mesh_edges",
     )(rows, q, first, w_sum, w_dec, gain.reshape(1, latent))
@@ -325,82 +360,77 @@
     return jnp.concatenate(blocks, axis=1)
 
 
-def first_kernel(picks_ref, tiles_ref, out_ref, *, tiles, inner):
-    nodes = tiles_ref.shape[0] // len(tiles)
+def hold(sources, held_ref):
+    @pl.when(pl.program_id(0) == 0)
+    def _():
+        start = 0
+        for source in sources:
+            held_ref[start : start + source.shape[0], :] = source[...]
+            start += source.shape[0]
+
+
+def first_kernel(picks_ref, *refs, tiles, inner):
+    sources, (out_ref, held_ref) = refs[:-2], refs[-2:]
+    hold(sources, held_ref)
+    nodes = held_ref.shape[0] // len(tiles)
     for i in range(out_ref.shape[0] // inner):
         part = slice(i * inner, (i + 1) * inner)
         table = pick_table(picks_ref[part, :], tiles, nodes)
-        out_ref[part, :] = jnp.dot(table, tiles_ref[...], preferred_element_type=F32).astype(BF16)
-
-
-def first_stage(picks, tiles, source):
-    rows, latent = picks.shape[0], source.shape[1]
+        out_ref[part, :] = jnp.dot(table, held_ref[...], preferred_element_type=F32).astype(BF16)
+
+
+def first_stage(picks, tiles, sources):
+    rows, latent = picks.shape[0], sources[0].shape[1]
     block = 512
+    held = sum(source.shape[0] for source in sources)
     wide = pl.BlockSpec((block, latent), lambda i: (i, 0))
     return pl.pallas_call(
         functools.partial(first_kernel, tiles=tiles, inner=256),
         grid=(rows // block,),
         out_shape=jax.ShapeDtypeStruct((rows, latent), BF16),
-        in_specs=[pl.BlockSpec((block, picks.shape[1]), lambda i: (i, 0)), pl.BlockSpec(source.shape, lambda i: (0, 0))],
+        in_specs=[pl.BlockSpec((block, picks.shape[1]), lambda i: (i, 0))]
+        + [pl.BlockSpec(source.shape, lambda i: (0, 0)) for source in sources],
         out_specs=wide,
+        scratch_shapes=[pltpu.VMEM((held, latent), BF16)],
         compiler_params=pltpu.CompilerParams(vmem_limit_bytes=16 * MIB),
         cost_estimate=pl.CostEstimate(
-            flops=2 * rows * source.size, bytes_accessed=8 * rows * latent, transcendentals=0
+            flops=2 * rows * held * latent, bytes_accessed=8 * rows * latent, transcendentals=0
         ),
         name="mesh_to_grid_first",
-    )(picks, source)
-
-
-def grid_kernel(picks_ref, part_ref, near_ref, far_ref, grid_ref, gain, out_ref, *, inner, tiles, nodes):
-    width = near_ref.shape[0]
+    )(picks, *sources)
+
+
+def grid_kernel(picks_ref, part_ref, grid_ref, gain, *refs, inner, tiles):
+    sources, (out_ref, held_ref) = refs[:-2], refs[-2:]
+    hold(sources, held_ref)
+    nodes = held_ref.shape[0] // len(tiles)
     for i in range(out_ref.shape[0] // inner):
         part = slice(i * inner, (i + 1) * inner)
         table = pick_table(picks_ref[part, :], tiles, nodes)
-        total = part_ref[part, :].astype(F32)
-        total += jnp.dot(table[:, :width], near_ref[...], preferred_element_type=F32)
-        total += jnp.dot(table[:, width:], far_ref[...], preferred_element_type=F32)
-        update = silu(total)
+        half = part_ref[part, :].astype(F32) + jnp.dot(table, held_ref[...], preferred_element_type=F32)
+        update = silu_of_half(half)
         out_ref[part, :] = (grid_ref[part, :].astype(F32) + gain[...] * layer_norm(update)).astype(BF16)
 
 
-def grid_stage(picks, part, tiles, near, far, grid_feat, gain):
+def grid_stage(picks, part, tiles, sources, grid_feat, gain):
     rows, latent = grid_feat.shape
     block = 512
-    full = pl.BlockSpec(near.shape, lambda i: (0, 0))
     wide = pl.BlockSpec((block, latent), lambda i: (i, 0))
     return pl.pallas_call(
-        functools.partial(grid_kernel, inner=256, tiles=tiles, nodes=2 * near.shape[0] // len(tiles)),
+        functools.partial(grid_kernel, inner=256, tiles=tiles),
         grid=(rows // block,),
         out_shape=jax.ShapeDtypeStruct((rows, latent), BF16),
         in_specs=[
             pl.BlockSpec((block, picks.shape[1]), lambda i: (i, 0)),
-            wide, full, full, wide,
+            wide, wide,
             pl.BlockSpec((1, latent), lambda i: (0, 0)),
-        ],
+        ]
+        + [pl.BlockSpec(source.shape, lambda i: (0, 0)) for source in sources],
         out_specs=wide,
+        scratch_shapes=[pltpu.VMEM((sum(source.shape[0] for source in sources), latent), BF16)],
         compiler_params=pltpu.CompilerParams(vmem_limit_bytes=16 * MIB),
         name="mesh_to_grid",
-    )(picks, part, near, far, grid_feat, gain.reshape(1, latent))
-
-
-def stack_kernel(near_ref, far_ref, a_ref, b_ref, own_ref, pair_ref, five_ref):
-    nodes = own_ref.shape[0]
-    for n, ref in enumerate((near_ref, far_ref, a_ref, b_ref, own_ref)):
-        five_ref[n * nodes : (n + 1) * nodes, :] = ref[...]
-    pair_ref[:nodes, :] = a_ref[...]
-    pair_ref[nodes:, :] = b_ref[...]
-
-
-def stack_tiles(near, far, a, b, own):
-    nodes, latent = own.shape
-    return pl.pallas_call(
-        stack_kernel,
-        out_shape=tuple(jax.ShapeDtypeStruct((n * nodes, latent), BF16) for n in (2, 5)),
-        in_specs=[whole()] * 5,
-        out_specs=(whole(),) * 2,
-        compiler_params=pltpu.CompilerParams(vmem_limit_bytes=8 * MIB),
-        name="stack_tiles",
-    )(near, far, a, b, own)
+    )(picks, part, grid_feat, gain.reshape(1, latent), *sources)
 
 
 def swap(block, axis, first):
@@ -421,8 +451,8 @@
     sector = lax.axis_index("lon")
     tile = band * lon_count + sector
 
-    near_ab, near, far_ab, far, own_ab, own = scatter(g2m_src, g2m_dst, g2m_weight, grid_feat, w_in, nodes, lon_count)
-    from_far_ab = swap(far_ab, "lon", False)
+    near_ab, near, far_a, far_b, far, own_ab, own = scatter(g2m_src, g2m_dst, g2m_weight, grid_feat, w_in, nodes, lon_count)
+    from_far_a, from_far_b = swap(far_a, "lon", False), swap(far_b, "lon", False)
     from_near_ab = swap(near_ab, "lon", True)
     from_far = swap(far, "lon", False)
     from_near = swap(near, "lon", True)
@@ -432,9 +462,9 @@
     marks = jnp.where(live, mesh_dst[0] & (nodes - 1), nodes).astype(F32)
     marks = jnp.tile(marks, (1, LANES // capacity))
 
-    (own_ab,) = add_pieces(own_ab, from_near_ab, 1, F32, "add_near")
-    to_a, to_b = add_pieces(own_ab, from_far_ab, 2, BF16, "add_far")
-    sums = (own, swap(to_a, "lat", True), swap(to_b, "lat", False), from_near, from_far)
+    own_a, own_b = add_near(own_ab, from_near_ab)
+    to_a, to_b = add_far(from_far_a, own_a), add_far(from_far_b, own_b)
+    sums = (own, swap(to_a, "lat", True), swap(to_b, "lat", False), from_far, from_near)
 
     first, q, rows = node_stage(
         mesh_src[0] - tile * nodes, marks, sums, mesh_feat, w_enc, w_send, w_recv, gain_enc
@@ -453,18 +483,18 @@
             columns[j] = jnp.where(same, -1 - j, columns[j])
     picks = jnp.stack([c.astype(F32) for c in columns] + weights, axis=1)
     edge_node = jnp.dot(w_edge, w_node, preferred_element_type=F32).astype(BF16)
-    dec_out = jnp.dot(w_dec, w_out, preferred_element_type=F32).astype(BF16)
+    dec_out = (0.5 * jnp.dot(w_dec, w_out, preferred_element_type=F32)).astype(BF16)
     rows_in, picks, edge_node, dec_out = lax.optimization_barrier((rows_in, picks, edge_node, dec_out))
 
     mesh_out, decoded = edge_stage(rows_in, q, first, edge_node, dec_out, gain_node)
 
     from_a, from_b = swap(decoded, "lat", True), swap(decoded, "lat", False)
     far, near = swap(decoded, "lon", False), swap(decoded, "lon", True)
-    pair, five = stack_tiles(near, far, from_a, from_b, decoded)
-    far_pair, near_pair = swap(pair, "lon", False), swap(pair, "lon", True)
-    part = first_stage(picks, (NEAR, FAR, A, B, OWN), five)
-    late = (NEAR_A, NEAR_B, FAR_A, FAR_B)
-    grid_out = grid_stage(picks, part, late, near_pair, far_pair, grid_feat, gain_out)
+    corners = [swap(v, "lon", first) for v in (from_a, from_b) for first in (False, True)]
+    part = first_stage(picks, (A, B, OWN), (from_a, from_b, decoded))
+    grid_out = grid_stage(
+        picks, part, (FAR_A, NEAR_A, FAR_B, NEAR_B, FAR, NEAR), (*corners, far, near), grid_feat, gain_out
+    )
     return (grid_out, mesh_out)
 
 

time: 144 us -> 140 us (0.972)
  waiting for transfers between devices: 73.8 us -> 67 us
  starting transfers between devices: 24.6 us -> 30.2 us
  local copies, waits for them, and re-layouts: 6.16 us -> 3.8 us
    ppermute x12 -> x15, starting transfers between devices: 15.8 us -> 22.8 us  [swap(): return lax.ppermute(block, axis, pairs)]
    ppermute x12 -> x15, waiting for transfers between devices: 19.7 us -> 13.1 us  [swap(): return lax.ppermute(block, axis, pairs)]
    unnamed x42 -> x38, local copies, waits for them, and re-layouts: 4.19 us -> 1.83 us
  transfers between devices with their start and end apart: 13 -> 16, of which waited for: 7 -> 7; matrix products, arithmetic and copies ran while one was open for 2% -> 2% of each run, Pallas kernels for 3% -> 3%
where the time goes in v4:
time: 140 us; the launch traced here: 139 us
  waiting for transfers between devices  67 us (48%)
  Pallas kernels  36.3 us (26%)
  starting transfers between devices  30.2 us (22%)
  local copies, waits for them, and re-layouts  3.8 us (3%)
    all_to_all x1, waiting for transfers between devices, on_device(): lax.all_to_all(rows, ('lat', 'lon'), split_axis=0, concat_axis=0, tiled=T...  53.9 us
    ppermute x15, starting transfers between devices, swap(): return lax.ppermute(block, axis, pairs)  22.8 us
    pallas_call x1, Pallas kernels, scatter(): pl.pallas_call(functools.partial(scatter_kernel, nodes=nodes, lon_count=l...  13.8 us
    ppermute x15, waiting for transfers between devices, swap(): return lax.ppermute(block, axis, pairs)  13.1 us
    all_to_all x1, starting transfers between devices, on_device(): lax.all_to_all(rows, ('lat', 'lon'), split_axis=0, concat_axis=0, tiled=T...  7.49 us
    pallas_call x1, Pallas kernels, grid_stage(): pl.pallas_call(functools.partial(grid_kernel, inner=256, tiles=tiles), gr...  6.87 us
    pallas_call x1, Pallas kernels, edge_stage(): pl.pallas_call(functools.partial(edge_kernel, per=per), out_shape=(out, o...  5.95 us
    pallas_call x1, Pallas kernels, node_stage(): pl.pallas_call(functools.partial(node_kernel, pieces=len(sums)), out_shap...  5.07 us
  transfers between devices with their start and end apart: 16, of which 7 were waited for; matrix products, arithmetic and copies ran while one was open for 2% of the time, Pallas kernels for 3%

profile of v4, /device:TPU:0, one launch (start us, length us, event | category | flops | bytes accessed | tf_op | source)
XLA Modules:
  0.0 139.4 jit_solution(9066498714688067192)
XLA Ops:
  0.6 0.0 copy-start
  0.6 0.0 copy-start.15
  0.7 13.8 %grid_to_mesh.1 = (bf16[512,512]{1,0:T(8,128)(2,1)}, bf16[256,512]{1,0:T(8,128)(2,1)}, bf16[256,512]{1,0:T(8,128)(2,1)}, bf16[256,512]{1,0:T(8,128)(2,1)}, bf16[...) custom-call(s32[32,128]{1,0:T(8,128)} %bitcast.19, s32[32,128]{1,0:T(8,128)} %bitcast.20, ...), custom_call_target="tpu_custom_call" | custom-call | tf_op jit(solution)/shard_map/grid_to_mesh/pallas_call | solution.py:159
  14.5 0.0 copy-start.14
  14.5 0.0 copy-start.16
  14.5 0.1 collective-permute-start.1
  14.6 5.4 %collective-permute-start = (bf16[256,512]{1,0:T(8,128)(2,1)}, bf16[256,512]{1,0:T(8,128)(2,1)S(1)}, u32[]{:S(2)}, u32[]{:S(2)}) collective-permute-start(bf16[256,512]{1,0:T(8,128)(2,1)} %get-tuple-element.26), channel_id=1, source_target_pairs={{0,31},{1,2},{2,1},{3,4},{4,3},{5,6},{6,5},{7,8},{8,7},{9,10},{10,... | collective-permute-start | bytes 786440 | tf_op jit(solution)/shard_map/ppermute | solution.py:439
  20.0 0.0 collective-permute-start.3
  20.0 5.0 %collective-permute-start.5 = (bf16[256,512]{1,0:T(8,128)(2,1)}, bf16[256,512]{1,0:T(8,128)(2,1)S(1)}, u32[]{:S(2)}, u32[]{:S(2)}) collective-permute-start(bf16[256,512]{1,0:T(8,128)(2,1)} %get-tuple-element.32), channel_id=1, source_target_pairs={{0,31},{1,2},{2,1},{3,4},{4,3},{5,6},{6,5},{7,8},{8,7},{9,10},{10,... | collective-permute-start | bytes 786440 | tf_op jit(solution)/shard_map/ppermute | solution.py:439
  25.0 0.0 collective-permute-start.6
  25.0 0.0 collective-permute-done.1.b_ref
  25.0 1.0 copy-done.2
  26.1 0.1 add_near.1
  26.2 0.0 collective-permute-done.a_ref
  26.3 2.0 %collective-permute-start.2 = (bf16[256,512]{1,0:T(8,128)(2,1)S(1)}, bf16[256,512]{1,0:T(8,128)(2,1)S(1)}, u32[]{:S(2)}, u32[]{:S(2)}) collective-permute-start(bf16[256,512]{1,0:T(8,128)(2,1)S(1)} %add_far.2), channel_id=1, source_target_pairs={{0,32},{32,0},{64,96},{96,64},{1,33},{33,1},{65,97},{97,65},{2,34}... | collective-permute-start | bytes 786440 | tf_op jit(solution)/shard_map/ppermute | solution.py:439
  28.3 1.0 collective-permute-done.3.a_ref
  29.3 4.1 %collective-permute-start.4 = (bf16[256,512]{1,0:T(8,128)(2,1)S(1)}, bf16[256,512]{1,0:T(8,128)(2,1)S(1)}, u32[]{:S(2)}, u32[]{:S(2)}) collective-permute-start(bf16[256,512]{1,0:T(8,128)(2,1)S(1)} %add_far.3), channel_id=1, source_target_pairs={{0,96},{32,64},{64,32},{96,0},{1,97},{33,65},{65,33},{97,1},{2,98}... | collective-permute-start | bytes 786440 | tf_op jit(solution)/shard_map/ppermute | solution.py:439
  33.5 0.1 copy.50
  33.6 0.7 sub.47.refs_10_
  34.3 0.0 copy-done.15
  34.3 0.7 copy.52.refs_11_
  35.0 0.0 collective-permute-done.5.refs_3_
  35.0 0.0 collective-permute-done.6.refs_4_
  35.0 0.0 copy-start.9
  35.0 0.2 collective-permute-done.2.refs_1_
  35.2 2.8 %collective-permute-done.4.refs_2_ = bf16[256,512]{1,0:T(8,128)(2,1)S(1)} collective-permute-done((bf16[256,512]{1,0:T(8,128)(2,1)S(1)}, bf16[256,512]{1,0:T(8,128)(2,1)S(1)}, u32[]{:S(2)}, u32[]{:S(2)}) %collective-permute-start.4) | collective-permute-done | bytes 262176 | tf_op jit(solution)/shard_map/ppermute | solution.py:439
  38.1 0.0 copy-done.9
  38.1 0.7 copy-done.11
  38.7 5.1 %mesh_encoder.1 = (bf16[256,512]{1,0:T(8,128)(2,1)}, bf16[256,512]{1,0:T(8,128)(2,1)}, bf16[128,136,128]{2,1,0:T(8,128)(2,1)}) custom-call(bf16[256,512]{1,0:T(8,128)(2,1)} %get-tuple-element.25.refs_0_, bf16[256,512]{1,0:T(8,128)(2,1)} %copy-done.10, bf16[256,512]{1,0:T(8,128)(2,1)} %copy-done.11, bf16[256,512]{1,0:T(8,128)(2,1)} %copy-done.8, ...), custom_call_target="tpu_custom_call" | custom-call | tf_op jit(solution)/shard_map/mesh_encoder/pallas_call | solution.py:272
  43.8 0.0 copy-start.12
  43.8 0.0 copy-start.13
  43.8 0.0 copy-start.7
  43.9 0.0 copy-start.17
  43.9 0.0 copy-start.18
  43.9 7.5 %all-to-all-start = ((bf16[128,136,128]{2,1,0:T(8,128)(2,1)}), bf16[128,136,128]{2,1,0:T(8,128)(2,1)}, u32[]{:S(2)}, u32[]{:S(2)}) async-start(bf16[128,136,128]{2,1,0:T(8,128)(2,1)} %get-tuple-element.34), calls=%async_computation | async-start | bytes 8912896 | tf_op jit(solution)/shard_map/all_to_all | solution.py:472
  51.4 0.0 copy-start.5
  51.4 0.1 and_add_fusion
  51.6 0.1 stack.2
  51.7 0.4 convolution_convert_fusion.w_sum
  52.2 0.4 fusion.w_dec
  52.6 53.9 %all-to-all-done.rows_hbm = bf16[128,136,128]{2,1,0:T(8,128)(2,1)} async-done(((bf16[128,136,128]{2,1,0:T(8,128)(2,1)}), bf16[128,136,128]{2,1,0:T(8,128)(2,1)}, u32[]{:S(2)}, u32[]{:S(2)}) %all-to-all-start) | async-done | bytes 4456480 | tf_op jit(solution)/shard_map/all_to_all | solution.py:472
  106.5 0.0 copy-done.4
  106.5 6.0 %mesh_edges.1 = (bf16[256,512]{1,0:T(8,128)(2,1)}, bf16[256,512]{1,0:T(8,128)(2,1)S(1)}) custom-call(bf16[128,136,128]{2,1,0:T(8,128)(2,1)} %all-to-all-done.rows_hbm, bf16[256,512]{1,0:T(8,128)(2,1)S(1)} %copy-done.4, bf16[256,512]{1,0:T(8,128)(2,1)S(1)} %copy-done.3, bf16[512,512]{1,0:T(8,128)(2,1)S(1)} %convolution_convert_fusion.w_sum, ...), custom_call_target="tpu_custom_call" | custom-call | tf_op jit(solution)/shard_map/mesh_edges/pallas_call | solution.py:332
  112.5 0.3 collective-permute-start.7
  112.8 0.6 collective-permute-start.8
  113.4 0.5 collective-permute-start.13
  113.9 0.3 collective-permute-start.14
  114.2 6.2 %collective-permute-done.7.refs_0_ = bf16[256,512]{1,0:T(8,128)(2,1)} collective-permute-done((bf16[256,512]{1,0:T(8,128)(2,1)S(1)}, bf16[256,512]{1,0:T(8,128)(2,1)}, u32[]{:S(2)}, u32[]{:S(2)}) %collective-permute-start.7) | collective-permute-done | bytes 262176 | tf_op jit(solution)/shard_map/ppermute | solution.py:439
  120.4 0.3 collective-permute-start.9
  120.7 0.3 collective-permute-start.10
  121.0 0.7 collective-permute-done.8.refs_1_
  121.7 3.8 %collective-permute-start.11 = (bf16[256,512]{1,0:T(8,128)(2,1)}, bf16[256,512]{1,0:T(8,128)(2,1)S(1)}, u32[]{:S(2)}, u32[]{:S(2)}) collective-permute-start(bf16[256,512]{1,0:T(8,128)(2,1)} %collective-permute-done.8.refs_1_), channel_id=1, source_target_pairs={{0,31},{1,2},{2,1},{3,4},{4,3},{5,6},{6,5},{7,8},{8,7},{9,10},{10,... | collective-permute-start | bytes 786440 | tf_op jit(solution)/shard_map/ppermute | solution.py:439
  125.5 0.0 collective-permute-done.13.refs_4_
  125.5 0.0 collective-permute-start.12
  125.5 0.4 copy.54.picks_ref
  125.8 0.0 copy-start.1
  125.9 0.0 copy-start.6
  125.9 4.4 %mesh_to_grid_first.1.part_ref = bf16[2048,512]{1,0:T(8,128)(2,1)S(1)} custom-call(f32[2048,6]{1,0:T(8,128)S(1)} %copy.54.picks_ref, bf16[256,512]{1,0:T(8,128)(2,1)} %collective-permute-done.7.refs_0_, bf16[256,512]{1,0:T(8,128)(2,1)} %collective-permute-done.8.refs_1_, bf16[256,512]{1,0:T(8,128)(2,1)S(1)} %get-tuple-element.46.refs_2_), custom_call_target="tpu_custom_call" | custom-call | flops 1610612736 | bytes 8388608 | tf_op jit(solution)/shard_map/mesh_to_grid_first/pallas_call | solution.py:387
  130.3 0.0 collective-permute-done.14.refs_5_
  130.3 0.0 collective-permute-done.9.refs_0_
  130.3 0.0 collective-permute-done.10.refs_1_
  130.4 2.2 %collective-permute-done.11.refs_2_ = bf16[256,512]{1,0:T(8,128)(2,1)S(1)} collective-permute-done((bf16[256,512]{1,0:T(8,128)(2,1)}, bf16[256,512]{1,0:T(8,128)(2,1)S(1)}, u32[]{:S(2)}, u32[]{:S(2)}) %collective-permute-start.11) | collective-permute-done | bytes 262176 | tf_op jit(solution)/shard_map/ppermute | solution.py:439
  132.5 0.0 collective-permute-done.12.refs_3_
  132.5 6.9 %mesh_to_grid.1 = bf16[2048,512]{1,0:T(8,128)(2,1)} custom-call(f32[2048,6]{1,0:T(8,128)S(1)} %copy.54.picks_ref, bf16[2048,512]{1,0:T(8,128)(2,1)S(1)} %mesh_to_grid_first.1.part_ref, bf16[2048,512]{1,0:T(8,128)(2,1)S(1)} %copy-done.1, f32[1,512]{1,0:T(1,128)S(1)} %bitcast.17, bf16[256,512]{1,0:T(8,128)(2,1)S(1)} %collective-permute-done.9.refs_0_, ...), custom_call_target="tpu_custom_call" | custom-call | tf_op jit(solution)/shard_map/mesh_to_grid/pallas_call | solution.py:419
  (27 shorter events, 0.2 us)
Async XLA Ops:
  0.6 51.1 %copy-start = (bf16[512,512]{1,0:T(8,128)(2,1)S(1)}, bf16[512,512]{1,0:T(8,128)(2,1)}, u32[]{:S(2)}) copy-start(bf16[512,512]{1,0:T(8,128)(2,1)} %param.35) | copy-start | bytes 1572868
  0.6 33.6 %copy-start.15 = (s32[1,128,32]{1,2,0:T(8,128)S(1)}, s32[1,128,32]{1,2,0:T(8,128)}, u32[]{:S(2)}) copy-start(s32[1,128,32]{1,2,0:T(8,128)} %param.27) | copy-start | bytes 49156
  14.5 19.0 %copy-start.14 = (s32[1,128,32]{1,2,0:T(8,128)S(1)}, s32[1,128,32]{1,2,0:T(8,128)}, u32[]{:S(2)}) copy-start(s32[1,128,32]{1,2,0:T(8,128)} %param.26) | copy-start | bytes 49156
  14.5 19.8 %copy-start.16 = (s32[1,128]{1,0:T(1,128)S(1)}, s32[1,128]{1,0:T(1,128)}, u32[]{:S(2)}) copy-start(s32[1,128]{1,0:T(1,128)} %param.28) | copy-start | bytes 1540
  14.5 10.5 %collective-permute-start.1 = (bf16[512,512]{1,0:T(8,128)(2,1)}, bf16[512,512]{1,0:T(8,128)(2,1)S(1)}, u32[]{:S(2)}, u32[]{:S(2)}) collective-permute-start(bf16[512,512]{1,0:T(8,128)(2,1)} %get-tuple-element.28), channel_id=1, source_target_pairs={{0,1},{1,0},{2,3},{3,2},{4,5},{5,4},{6,7},{7,6},{8,9},{9,8},{10,11... | collective-permute-start | bytes 1572872 | tf_op jit(solution)/shard_map/ppermute | solution.py:439
  14.6 11.6 %collective-permute-start = (bf16[256,512]{1,0:T(8,128)(2,1)}, bf16[256,512]{1,0:T(8,128)(2,1)S(1)}, u32[]{:S(2)}, u32[]{:S(2)}) collective-permute-start(bf16[256,512]{1,0:T(8,128)(2,1)} %get-tuple-element.26), channel_id=1, source_target_pairs={{0,31},{1,2},{2,1},{3,4},{4,3},{5,6},{6,5},{7,8},{8,7},{9,10},{10,... | collective-permute-start | bytes 786440 | tf_op jit(solution)/shard_map/ppermute | solution.py:439
  20.0 9.3 %collective-permute-start.3 = (bf16[256,512]{1,0:T(8,128)(2,1)}, bf16[256,512]{1,0:T(8,128)(2,1)S(1)}, u32[]{:S(2)}, u32[]{:S(2)}) collective-permute-start(bf16[256,512]{1,0:T(8,128)(2,1)} %get-tuple-element.30), channel_id=1, source_target_pairs={{0,31},{1,2},{2,1},{3,4},{4,3},{5,6},{6,5},{7,8},{8,7},{9,10},{10,... | collective-permute-start | bytes 786440 | tf_op jit(solution)/shard_map/ppermute | solution.py:439
  20.0 15.0 %collective-permute-start.5 = (bf16[256,512]{1,0:T(8,128)(2,1)}, bf16[256,512]{1,0:T(8,128)(2,1)S(1)}, u32[]{:S(2)}, u32[]{:S(2)}) collective-permute-start(bf16[256,512]{1,0:T(8,128)(2,1)} %get-tuple-element.32), channel_id=1, source_target_pairs={{0,31},{1,2},{2,1},{3,4},{4,3},{5,6},{6,5},{7,8},{8,7},{9,10},{10,... | collective-permute-start | bytes 786440 | tf_op jit(solution)/shard_map/ppermute | solution.py:439
  25.0 10.0 %collective-permute-start.6 = (bf16[256,512]{1,0:T(8,128)(2,1)}, bf16[256,512]{1,0:T(8,128)(2,1)S(1)}, u32[]{:S(2)}, u32[]{:S(2)}) collective-permute-start(bf16[256,512]{1,0:T(8,128)(2,1)} %get-tuple-element.33), channel_id=1, source_target_pairs={{0,1},{1,0},{2,3},{3,2},{4,5},{5,4},{6,7},{7,6},{8,9},{9,8},{10,11... | collective-permute-start | bytes 786440 | tf_op jit(solution)/shard_map/ppermute | solution.py:439
  25.0 1.0 copy-start.2
  26.3 9.0 %collective-permute-start.2 = (bf16[256,512]{1,0:T(8,128)(2,1)S(1)}, bf16[256,512]{1,0:T(8,128)(2,1)S(1)}, u32[]{:S(2)}, u32[]{:S(2)}) collective-permute-start(bf16[256,512]{1,0:T(8,128)(2,1)S(1)} %add_far.2), channel_id=1, source_target_pairs={{0,32},{32,0},{64,96},{96,64},{1,33},{33,1},{65,97},{97,65},{2,34}... | collective-permute-start | bytes 786440 | tf_op jit(solution)/shard_map/ppermute | solution.py:439
  29.3 8.7 %collective-permute-start.4 = (bf16[256,512]{1,0:T(8,128)(2,1)S(1)}, bf16[256,512]{1,0:T(8,128)(2,1)S(1)}, u32[]{:S(2)}, u32[]{:S(2)}) collective-permute-start(bf16[256,512]{1,0:T(8,128)(2,1)S(1)} %add_far.3), channel_id=1, source_target_pairs={{0,96},{32,64},{64,32},{96,0},{1,97},{33,65},{65,33},{97,1},{2,98}... | collective-permute-start | bytes 786440 | tf_op jit(solution)/shard_map/ppermute | solution.py:439
  35.0 3.0 %copy-start.8 = (bf16[256,512]{1,0:T(8,128)(2,1)}, bf16[256,512]{1,0:T(8,128)(2,1)S(1)}, u32[]{:S(2)}) copy-start(bf16[256,512]{1,0:T(8,128)(2,1)S(1)} %collective-permute-done.5.refs_3_) | copy-start | bytes 786436
  35.0 3.0 %copy-start.9 = (bf16[256,512]{1,0:T(8,128)(2,1)}, bf16[256,512]{1,0:T(8,128)(2,1)S(1)}, u32[]{:S(2)}) copy-start(bf16[256,512]{1,0:T(8,128)(2,1)S(1)} %collective-permute-done.6.refs_4_) | copy-start | bytes 786436
  35.2 2.8 %copy-start.10 = (bf16[256,512]{1,0:T(8,128)(2,1)}, bf16[256,512]{1,0:T(8,128)(2,1)S(1)}, u32[]{:S(2)}) copy-start(bf16[256,512]{1,0:T(8,128)(2,1)S(1)} %collective-permute-done.2.refs_1_) | copy-start | bytes 786436
  38.0 0.7 copy-start.11
  43.8 7.6 %copy-start.12 = (s32[2048,3]{0,1:T(4,128)S(1)}, s32[2048,3]{0,1:T(4,128)}, u32[]{:S(2)}) copy-start(s32[2048,3]{0,1:T(4,128)} %param.29) | copy-start | bytes 73732
  43.8 7.7 %copy-start.13 = (f32[2048,3]{0,1:T(4,128)S(1)}, f32[2048,3]{0,1:T(4,128)}, u32[]{:S(2)}) copy-start(f32[2048,3]{0,1:T(4,128)} %param.30) | copy-start | bytes 73732
  43.8 7.9 %copy-start.7 = (bf16[512,512]{1,0:T(8,128)(2,1)S(1)}, bf16[512,512]{1,0:T(8,128)(2,1)}, u32[]{:S(2)}) copy-start(bf16[512,512]{1,0:T(8,128)(2,1)} %param.36) | copy-start | bytes 1572868
  43.9 8.3 %copy-start.17 = (bf16[512,512]{1,0:T(8,128)(2,1)S(1)}, bf16[512,512]{1,0:T(8,128)(2,1)}, u32[]{:S(2)}) copy-start(bf16[512,512]{1,0:T(8,128)(2,1)} %param.37) | copy-start | bytes 1572868
  43.9 8.3 %copy-start.18 = (bf16[512,512]{1,0:T(8,128)(2,1)S(1)}, bf16[512,512]{1,0:T(8,128)(2,1)}, u32[]{:S(2)}) copy-start(bf16[512,512]{1,0:T(8,128)(2,1)} %param.38) | copy-start | bytes 1572868
  43.9 62.6 %all-to-all-start = ((bf16[128,136,128]{2,1,0:T(8,128)(2,1)}), bf16[128,136,128]{2,1,0:T(8,128)(2,1)}, u32[]{:S(2)}, u32[]{:S(2)}) async-start(bf16[128,136,128]{2,1,0:T(8,128)(2,1)} %get-tuple-element.34), calls=%async_computation | async-start | bytes 8912896 | tf_op jit(solution)/shard_map/all_to_all | solution.py:472
  51.4 55.1 %copy-start.3 = (bf16[256,512]{1,0:T(8,128)(2,1)S(1)}, bf16[256,512]{1,0:T(8,128)(2,1)}, u32[]{:S(2)}) copy-start(bf16[256,512]{1,0:T(8,128)(2,1)} %get-tuple-element.43.first_ref) | copy-start | bytes 786436
  51.4 55.1 %copy-start.4 = (bf16[256,512]{1,0:T(8,128)(2,1)S(1)}, bf16[256,512]{1,0:T(8,128)(2,1)}, u32[]{:S(2)}) copy-start(bf16[256,512]{1,0:T(8,128)(2,1)} %get-tuple-element.42.q_ref) | copy-start | bytes 786436
  51.4 55.1 %copy-start.5 = (f32[512]{0:T(512)S(1)}, f32[512]{0:T(512)}, u32[]{:S(2)}) copy-start(f32[512]{0:T(512)} %param.40) | copy-start | bytes 6148
  112.5 7.9 %collective-permute-start.7 = (bf16[256,512]{1,0:T(8,128)(2,1)S(1)}, bf16[256,512]{1,0:T(8,128)(2,1)}, u32[]{:S(2)}, u32[]{:S(2)}) collective-permute-start(bf16[256,512]{1,0:T(8,128)(2,1)S(1)} %get-tuple-element.46.refs_2_), channel_id=1, source_target_pairs={{0,32},{32,0},{64,96},{96,64},{1,33},{33,1},{65,97},{97,65},{2,34}... | collective-permute-start | bytes 786440 | tf_op jit(solution)/shard_map/ppermute | solution.py:439
  112.8 8.9 %collective-permute-start.8 = (bf16[256,512]{1,0:T(8,128)(2,1)S(1)}, bf16[256,512]{1,0:T(8,128)(2,1)}, u32[]{:S(2)}, u32[]{:S(2)}) collective-permute-start(bf16[256,512]{1,0:T(8,128)(2,1)S(1)} %get-tuple-element.46.refs_2_), channel_id=1, source_target_pairs={{0,96},{32,64},{64,32},{96,0},{1,97},{33,65},{65,33},{97,1},{2,98}... | collective-permute-start | bytes 786440 | tf_op jit(solution)/shard_map/ppermute | solution.py:439
  113.4 12.0 %collective-permute-start.13 = (bf16[256,512]{1,0:T(8,128)(2,1)S(1)}, bf16[256,512]{1,0:T(8,128)(2,1)S(1)}, u32[]{:S(2)}, u32[]{:S(2)}) collective-permute-start(bf16[256,512]{1,0:T(8,128)(2,1)S(1)} %get-tuple-element.46.refs_2_), channel_id=1, source_target_pairs={{0,31},{1,2},{2,1},{3,4},{4,3},{5,6},{6,5},{7,8},{8,7},{9,10},{10,... | collective-permute-start | bytes 786440 | tf_op jit(solution)/shard_map/ppermute | solution.py:439
  113.9 16.4 %collective-permute-start.14 = (bf16[256,512]{1,0:T(8,128)(2,1)S(1)}, bf16[256,512]{1,0:T(8,128)(2,1)S(1)}, u32[]{:S(2)}, u32[]{:S(2)}) collective-permute-start(bf16[256,512]{1,0:T(8,128)(2,1)S(1)} %get-tuple-element.46.refs_2_), channel_id=1, source_target_pairs={{0,1},{1,0},{2,3},{3,2},{4,5},{5,4},{6,7},{7,6},{8,9},{9,8},{10,11... | collective-permute-start | bytes 786440 | tf_op jit(solution)/shard_map/ppermute | solution.py:439
  120.4 9.9 %collective-permute-start.9 = (bf16[256,512]{1,0:T(8,128)(2,1)}, bf16[256,512]{1,0:T(8,128)(2,1)S(1)}, u32[]{:S(2)}, u32[]{:S(2)}) collective-permute-start(bf16[256,512]{1,0:T(8,128)(2,1)} %collective-permute-done.7.refs_0_), channel_id=1, source_target_pairs={{0,31},{1,2},{2,1},{3,4},{4,3},{5,6},{6,5},{7,8},{8,7},{9,10},{10,... | collective-permute-start | bytes 786440 | tf_op jit(solution)/shard_map/ppermute | solution.py:439
  120.7 9.7 %collective-permute-start.10 = (bf16[256,512]{1,0:T(8,128)(2,1)}, bf16[256,512]{1,0:T(8,128)(2,1)S(1)}, u32[]{:S(2)}, u32[]{:S(2)}) collective-permute-start(bf16[256,512]{1,0:T(8,128)(2,1)} %collective-permute-done.7.refs_0_), channel_id=1, source_target_pairs={{0,1},{1,0},{2,3},{3,2},{4,5},{5,4},{6,7},{7,6},{8,9},{9,8},{10,11... | collective-permute-start | bytes 786440 | tf_op jit(solution)/shard_map/ppermute | solution.py:439
  121.7 10.8 %collective-permute-start.11 = (bf16[256,512]{1,0:T(8,128)(2,1)}, bf16[256,512]{1,0:T(8,128)(2,1)S(1)}, u32[]{:S(2)}, u32[]{:S(2)}) collective-permute-start(bf16[256,512]{1,0:T(8,128)(2,1)} %collective-permute-done.8.refs_1_), channel_id=1, source_target_pairs={{0,31},{1,2},{2,1},{3,4},{4,3},{5,6},{6,5},{7,8},{8,7},{9,10},{10,... | collective-permute-start | bytes 786440 | tf_op jit(solution)/shard_map/ppermute | solution.py:439
  125.5 7.1 %collective-permute-start.12 = (bf16[256,512]{1,0:T(8,128)(2,1)}, bf16[256,512]{1,0:T(8,128)(2,1)S(1)}, u32[]{:S(2)}, u32[]{:S(2)}) collective-permute-start(bf16[256,512]{1,0:T(8,128)(2,1)} %collective-permute-done.8.refs_1_), channel_id=1, source_target_pairs={{0,1},{1,0},{2,3},{3,2},{4,5},{5,4},{6,7},{7,6},{8,9},{9,8},{10,11... | collective-permute-start | bytes 786440 | tf_op jit(solution)/shard_map/ppermute | solution.py:439
  125.8 6.7 %copy-start.1 = (bf16[2048,512]{1,0:T(8,128)(2,1)S(1)}, bf16[2048,512]{1,0:T(8,128)(2,1)}, u32[]{:S(2)}) copy-start(bf16[2048,512]{1,0:T(8,128)(2,1)} %grid_ref.1) | copy-start | bytes 6291460
  125.9 6.7 %copy-start.6 = (f32[512]{0:T(512)S(1)}, f32[512]{0:T(512)}, u32[]{:S(2)}) copy-start(f32[512]{0:T(512)} %param.41) | copy-start | bytes 6148

commit v5 on v4

--- a/solution.py
+++ b/solution.py
@@ -327,7 +327,7 @@
 
 def edge_stage(rows, q, first, w_sum, w_dec, gain):
     nodes, latent = first.shape
-    per = 16
+    per = 32
     out = jax.ShapeDtypeStruct((nodes, latent), BF16)
     return pl.pallas_call(
         functools.partial(edge_kernel, per=per),

time: 140 us -> 139 us (level)
  no operation moved by 1% of the time
where the time goes in v5:
time: 139 us
  waiting for transfers between devices  67.2 us (48%)
  Pallas kernels  35.7 us (26%)
  starting transfers between devices  30.3 us (22%)
  local copies, waits for them, and re-layouts  3.8 us (3%)
    all_to_all x1, waiting for transfers between devices, on_device(): lax.all_to_all(rows, ('lat', 'lon'), split_axis=0, concat_axis=0, tiled=T...  54.1 us
    ppermute x15, starting transfers between devices, swap(): return lax.ppermute(block, axis, pairs)  23 us
    pallas_call x1, Pallas kernels, scatter(): pl.pallas_call(functools.partial(scatter_kernel, nodes=nodes, lon_count=l...  13.8 us
    ppermute x15, waiting for transfers between devices, swap(): return lax.ppermute(block, axis, pairs)  13.1 us
    all_to_all x1, starting transfers between devices, on_device(): lax.all_to_all(rows, ('lat', 'lon'), split_axis=0, concat_axis=0, tiled=T...  7.3 us
    pallas_call x1, Pallas kernels, grid_stage(): pl.pallas_call(functools.partial(grid_kernel, inner=256, tiles=tiles), gr...  6.87 us
    pallas_call x1, Pallas kernels, edge_stage(): pl.pallas_call(functools.partial(edge_kernel, per=per), out_shape=(out, o...  5.33 us
    pallas_call x1, Pallas kernels, node_stage(): pl.pallas_call(functools.partial(node_kernel, pieces=len(sums)), out_shap...  5.07 us
  transfers between devices with their start and end apart: 16, of which 7 were waited for; matrix products, arithmetic and copies ran while one was open for 2% of the time, Pallas kernels for 3%

profile of v5, /device:TPU:0, one launch (start us, length us, event | category | flops | bytes accessed | tf_op | source)
XLA Modules:
  0.0 139.0 jit_solution(6729819160180326854)
XLA Ops:
  0.6 0.0 copy-start
  0.7 13.8 %grid_to_mesh.1 = (bf16[512,512]{1,0:T(8,128)(2,1)}, bf16[256,512]{1,0:T(8,128)(2,1)}, bf16[256,512]{1,0:T(8,128)(2,1)}, bf16[256,512]{1,0:T(8,128)(2,1)}, bf16[...) custom-call(s32[32,128]{1,0:T(8,128)} %bitcast.19, s32[32,128]{1,0:T(8,128)} %bitcast.20, ...), custom_call_target="tpu_custom_call" | custom-call | tf_op jit(solution)/shard_map/grid_to_mesh/pallas_call | solution.py:159
  14.5 0.0 copy-start.14
  14.5 0.0 copy-start.16
  14.5 0.1 collective-permute-start.1
  14.6 5.4 %collective-permute-start = (bf16[256,512]{1,0:T(8,128)(2,1)}, bf16[256,512]{1,0:T(8,128)(2,1)S(1)}, u32[]{:S(2)}, u32[]{:S(2)}) collective-permute-start(bf16[256,512]{1,0:T(8,128)(2,1)} %get-tuple-element.26), channel_id=1, source_target_pairs={{0,31},{1,2},{2,1},{3,4},{4,3},{5,6},{6,5},{7,8},{8,7},{9,10},{10,... | collective-permute-start | bytes 786440 | tf_op jit(solution)/shard_map/ppermute | solution.py:439
  20.0 0.0 collective-permute-start.3
  20.0 5.0 %collective-permute-start.5 = (bf16[256,512]{1,0:T(8,128)(2,1)}, bf16[256,512]{1,0:T(8,128)(2,1)S(1)}, u32[]{:S(2)}, u32[]{:S(2)}) collective-permute-start(bf16[256,512]{1,0:T(8,128)(2,1)} %get-tuple-element.32), channel_id=1, source_target_pairs={{0,31},{1,2},{2,1},{3,4},{4,3},{5,6},{6,5},{7,8},{8,7},{9,10},{10,... | collective-permute-start | bytes 786440 | tf_op jit(solution)/shard_map/ppermute | solution.py:439
  25.0 0.0 collective-permute-start.6
  25.0 0.0 collective-permute-done.1.b_ref
  25.1 1.0 copy-done.2
  26.1 0.1 add_near.1
  26.2 0.0 collective-permute-done.a_ref
  26.3 2.0 %collective-permute-start.2 = (bf16[256,512]{1,0:T(8,128)(2,1)S(1)}, bf16[256,512]{1,0:T(8,128)(2,1)S(1)}, u32[]{:S(2)}, u32[]{:S(2)}) collective-permute-start(bf16[256,512]{1,0:T(8,128)(2,1)S(1)} %add_far.2), channel_id=1, source_target_pairs={{0,32},{32,0},{64,96},{96,64},{1,33},{33,1},{65,97},{97,65},{2,34}... | collective-permute-start | bytes 786440 | tf_op jit(solution)/shard_map/ppermute | solution.py:439
  28.3 1.0 collective-permute-done.3.a_ref
  29.4 4.1 %collective-permute-start.4 = (bf16[256,512]{1,0:T(8,128)(2,1)S(1)}, bf16[256,512]{1,0:T(8,128)(2,1)S(1)}, u32[]{:S(2)}, u32[]{:S(2)}) collective-permute-start(bf16[256,512]{1,0:T(8,128)(2,1)S(1)} %add_far.3), channel_id=1, source_target_pairs={{0,96},{32,64},{64,32},{96,0},{1,97},{33,65},{65,33},{97,1},{2,98}... | collective-permute-start | bytes 786440 | tf_op jit(solution)/shard_map/ppermute | solution.py:439
  33.5 0.1 copy.50
  33.6 0.7 sub.47.refs_10_
  34.3 0.7 copy.52.refs_11_
  35.0 0.0 collective-permute-done.5.refs_3_
  35.0 0.0 collective-permute-done.6.refs_4_
  35.0 0.0 copy-start.9
  35.1 0.2 collective-permute-done.2.refs_1_
  35.2 2.8 %collective-permute-done.4.refs_2_ = bf16[256,512]{1,0:T(8,128)(2,1)S(1)} collective-permute-done((bf16[256,512]{1,0:T(8,128)(2,1)S(1)}, bf16[256,512]{1,0:T(8,128)(2,1)S(1)}, u32[]{:S(2)}, u32[]{:S(2)}) %collective-permute-start.4) | collective-permute-done | bytes 262176 | tf_op jit(solution)/shard_map/ppermute | solution.py:439
  38.1 0.0 copy-done.9
  38.1 0.7 copy-done.11
  38.8 5.1 %mesh_encoder.1 = (bf16[256,512]{1,0:T(8,128)(2,1)}, bf16[256,512]{1,0:T(8,128)(2,1)}, bf16[128,136,128]{2,1,0:T(8,128)(2,1)}) custom-call(bf16[256,512]{1,0:T(8,128)(2,1)} %get-tuple-element.25.refs_0_, bf16[256,512]{1,0:T(8,128)(2,1)} %copy-done.10, bf16[256,512]{1,0:T(8,128)(2,1)} %copy-done.11, bf16[256,512]{1,0:T(8,128)(2,1)} %copy-done.8, ...), custom_call_target="tpu_custom_call" | custom-call | tf_op jit(solution)/shard_map/mesh_encoder/pallas_call | solution.py:272
  43.8 0.0 copy-start.12
  43.8 0.0 copy-start.13
  43.8 0.0 copy-start.7
  43.9 0.0 copy-start.17
  43.9 0.0 copy-start.18
  43.9 7.3 %all-to-all-start = ((bf16[128,136,128]{2,1,0:T(8,128)(2,1)}), bf16[128,136,128]{2,1,0:T(8,128)(2,1)}, u32[]{:S(2)}, u32[]{:S(2)}) async-start(bf16[128,136,128]{2,1,0:T(8,128)(2,1)} %get-tuple-element.34), calls=%async_computation | async-start | bytes 8912896 | tf_op jit(solution)/shard_map/all_to_all | solution.py:472
  51.2 0.0 copy-start.5
  51.2 0.1 and_add_fusion
  51.3 0.0 copy-done.13
  51.4 0.1 stack.2
  51.5 0.0 copy-done
  51.5 0.0 copy-done.7
  51.5 0.4 convolution_convert_fusion.w_sum
  52.0 0.4 fusion.w_dec
  52.4 54.1 %all-to-all-done.rows_hbm = bf16[128,136,128]{2,1,0:T(8,128)(2,1)} async-done(((bf16[128,136,128]{2,1,0:T(8,128)(2,1)}), bf16[128,136,128]{2,1,0:T(8,128)(2,1)}, u32[]{:S(2)}, u32[]{:S(2)}) %all-to-all-start) | async-done | bytes 4456480 | tf_op jit(solution)/shard_map/all_to_all | solution.py:472
  106.5 5.3 %mesh_edges.1 = (bf16[256,512]{1,0:T(8,128)(2,1)}, bf16[256,512]{1,0:T(8,128)(2,1)S(1)}) custom-call(bf16[128,136,128]{2,1,0:T(8,128)(2,1)} %all-to-all-done.rows_hbm, bf16[256,512]{1,0:T(8,128)(2,1)S(1)} %copy-done.4, bf16[256,512]{1,0:T(8,128)(2,1)S(1)} %copy-done.3, bf16[512,512]{1,0:T(8,128)(2,1)S(1)} %convolution_convert_fusion.w_sum, ...), custom_call_target="tpu_custom_call" | custom-call | tf_op jit(solution)/shard_map/mesh_edges/pallas_call | solution.py:332
  111.8 0.5 collective-permute-start.7
  112.4 0.6 collective-permute-start.8
  113.0 0.5 collective-permute-start.13
  113.5 0.3 collective-permute-start.14
  113.8 6.2 %collective-permute-done.7.refs_0_ = bf16[256,512]{1,0:T(8,128)(2,1)} collective-permute-done((bf16[256,512]{1,0:T(8,128)(2,1)S(1)}, bf16[256,512]{1,0:T(8,128)(2,1)}, u32[]{:S(2)}, u32[]{:S(2)}) %collective-permute-start.7) | collective-permute-done | bytes 262176 | tf_op jit(solution)/shard_map/ppermute | solution.py:439
  120.0 0.3 collective-permute-start.9
  120.2 0.3 collective-permute-start.10
  120.6 0.7 collective-permute-done.8.refs_1_
  121.3 3.8 %collective-permute-start.11 = (bf16[256,512]{1,0:T(8,128)(2,1)}, bf16[256,512]{1,0:T(8,128)(2,1)S(1)}, u32[]{:S(2)}, u32[]{:S(2)}) collective-permute-start(bf16[256,512]{1,0:T(8,128)(2,1)} %collective-permute-done.8.refs_1_), channel_id=1, source_target_pairs={{0,31},{1,2},{2,1},{3,4},{4,3},{5,6},{6,5},{7,8},{8,7},{9,10},{10,... | collective-permute-start | bytes 786440 | tf_op jit(solution)/shard_map/ppermute | solution.py:439
  125.0 0.0 collective-permute-done.13.refs_4_
  125.0 0.0 collective-permute-start.12
  125.0 0.4 copy.54.picks_ref
  125.4 0.0 copy-start.1
  125.4 0.0 copy-start.6
  125.4 4.4 %mesh_to_grid_first.1.part_ref = bf16[2048,512]{1,0:T(8,128)(2,1)S(1)} custom-call(f32[2048,6]{1,0:T(8,128)S(1)} %copy.54.picks_ref, bf16[256,512]{1,0:T(8,128)(2,1)} %collective-permute-done.7.refs_0_, bf16[256,512]{1,0:T(8,128)(2,1)} %collective-permute-done.8.refs_1_, bf16[256,512]{1,0:T(8,128)(2,1)S(1)} %get-tuple-element.46.refs_2_), custom_call_target="tpu_custom_call" | custom-call | flops 1610612736 | bytes 8388608 | tf_op jit(solution)/shard_map/mesh_to_grid_first/pallas_call | solution.py:387
  129.9 0.0 collective-permute-done.14.refs_5_
  129.9 0.0 collective-permute-done.9.refs_0_
  129.9 0.0 collective-permute-done.10.refs_1_
  129.9 2.2 %collective-permute-done.11.refs_2_ = bf16[256,512]{1,0:T(8,128)(2,1)S(1)} collective-permute-done((bf16[256,512]{1,0:T(8,128)(2,1)}, bf16[256,512]{1,0:T(8,128)(2,1)S(1)}, u32[]{:S(2)}, u32[]{:S(2)}) %collective-permute-start.11) | collective-permute-done | bytes 262176 | tf_op jit(solution)/shard_map/ppermute | solution.py:439
  132.1 0.0 collective-permute-done.12.refs_3_
  132.1 6.9 %mesh_to_grid.1 = bf16[2048,512]{1,0:T(8,128)(2,1)} custom-call(f32[2048,6]{1,0:T(8,128)S(1)} %copy.54.picks_ref, bf16[2048,512]{1,0:T(8,128)(2,1)S(1)} %mesh_to_grid_first.1.part_ref, bf16[2048,512]{1,0:T(8,128)(2,1)S(1)} %copy-done.1, f32[1,512]{1,0:T(1,128)S(1)} %bitcast.17, bf16[256,512]{1,0:T(8,128)(2,1)S(1)} %collective-permute-done.9.refs_0_, ...), custom_call_target="tpu_custom_call" | custom-call | tf_op jit(solution)/shard_map/mesh_to_grid/pallas_call | solution.py:419
  (27 shorter events, 0.2 us)
Async XLA Ops:
  0.6 50.9 %copy-start = (bf16[512,512]{1,0:T(8,128)(2,1)S(1)}, bf16[512,512]{1,0:T(8,128)(2,1)}, u32[]{:S(2)}) copy-start(bf16[512,512]{1,0:T(8,128)(2,1)} %param.35) | copy-start | bytes 1572868
  0.6 33.6 %copy-start.15 = (s32[1,128,32]{1,2,0:T(8,128)S(1)}, s32[1,128,32]{1,2,0:T(8,128)}, u32[]{:S(2)}) copy-start(s32[1,128,32]{1,2,0:T(8,128)} %param.27) | copy-start | bytes 49156
  14.5 19.0 %copy-start.14 = (s32[1,128,32]{1,2,0:T(8,128)S(1)}, s32[1,128,32]{1,2,0:T(8,128)}, u32[]{:S(2)}) copy-start(s32[1,128,32]{1,2,0:T(8,128)} %param.26) | copy-start | bytes 49156
  14.5 19.8 %copy-start.16 = (s32[1,128]{1,0:T(1,128)S(1)}, s32[1,128]{1,0:T(1,128)}, u32[]{:S(2)}) copy-start(s32[1,128]{1,0:T(1,128)} %param.28) | copy-start | bytes 1540
  14.5 10.6 %collective-permute-start.1 = (bf16[512,512]{1,0:T(8,128)(2,1)}, bf16[512,512]{1,0:T(8,128)(2,1)S(1)}, u32[]{:S(2)}, u32[]{:S(2)}) collective-permute-start(bf16[512,512]{1,0:T(8,128)(2,1)} %get-tuple-element.28), channel_id=1, source_target_pairs={{0,1},{1,0},{2,3},{3,2},{4,5},{5,4},{6,7},{7,6},{8,9},{9,8},{10,11... | collective-permute-start | bytes 1572872 | tf_op jit(solution)/shard_map/ppermute | solution.py:439
  14.6 11.6 %collective-permute-start = (bf16[256,512]{1,0:T(8,128)(2,1)}, bf16[256,512]{1,0:T(8,128)(2,1)S(1)}, u32[]{:S(2)}, u32[]{:S(2)}) collective-permute-start(bf16[256,512]{1,0:T(8,128)(2,1)} %get-tuple-element.26), channel_id=1, source_target_pairs={{0,31},{1,2},{2,1},{3,4},{4,3},{5,6},{6,5},{7,8},{8,7},{9,10},{10,... | collective-permute-start | bytes 786440 | tf_op jit(solution)/shard_map/ppermute | solution.py:439
  20.0 9.3 %collective-permute-start.3 = (bf16[256,512]{1,0:T(8,128)(2,1)}, bf16[256,512]{1,0:T(8,128)(2,1)S(1)}, u32[]{:S(2)}, u32[]{:S(2)}) collective-permute-start(bf16[256,512]{1,0:T(8,128)(2,1)} %get-tuple-element.30), channel_id=1, source_target_pairs={{0,31},{1,2},{2,1},{3,4},{4,3},{5,6},{6,5},{7,8},{8,7},{9,10},{10,... | collective-permute-start | bytes 786440 | tf_op jit(solution)/shard_map/ppermute | solution.py:439
  20.0 15.0 %collective-permute-start.5 = (bf16[256,512]{1,0:T(8,128)(2,1)}, bf16[256,512]{1,0:T(8,128)(2,1)S(1)}, u32[]{:S(2)}, u32[]{:S(2)}) collective-permute-start(bf16[256,512]{1,0:T(8,128)(2,1)} %get-tuple-element.32), channel_id=1, source_target_pairs={{0,31},{1,2},{2,1},{3,4},{4,3},{5,6},{6,5},{7,8},{8,7},{9,10},{10,... | collective-permute-start | bytes 786440 | tf_op jit(solution)/shard_map/ppermute | solution.py:439
  25.0 10.0 %collective-permute-start.6 = (bf16[256,512]{1,0:T(8,128)(2,1)}, bf16[256,512]{1,0:T(8,128)(2,1)S(1)}, u32[]{:S(2)}, u32[]{:S(2)}) collective-permute-start(bf16[256,512]{1,0:T(8,128)(2,1)} %get-tuple-element.33), channel_id=1, source_target_pairs={{0,1},{1,0},{2,3},{3,2},{4,5},{5,4},{6,7},{7,6},{8,9},{9,8},{10,11... | collective-permute-start | bytes 786440 | tf_op jit(solution)/shard_map/ppermute | solution.py:439
  25.0 1.0 copy-start.2
  26.3 9.0 %collective-permute-start.2 = (bf16[256,512]{1,0:T(8,128)(2,1)S(1)}, bf16[256,512]{1,0:T(8,128)(2,1)S(1)}, u32[]{:S(2)}, u32[]{:S(2)}) collective-permute-start(bf16[256,512]{1,0:T(8,128)(2,1)S(1)} %add_far.2), channel_id=1, source_target_pairs={{0,32},{32,0},{64,96},{96,64},{1,33},{33,1},{65,97},{97,65},{2,34}... | collective-permute-start | bytes 786440 | tf_op jit(solution)/shard_map/ppermute | solution.py:439
  29.4 8.7 %collective-permute-start.4 = (bf16[256,512]{1,0:T(8,128)(2,1)S(1)}, bf16[256,512]{1,0:T(8,128)(2,1)S(1)}, u32[]{:S(2)}, u32[]{:S(2)}) collective-permute-start(bf16[256,512]{1,0:T(8,128)(2,1)S(1)} %add_far.3), channel_id=1, source_target_pairs={{0,96},{32,64},{64,32},{96,0},{1,97},{33,65},{65,33},{97,1},{2,98}... | collective-permute-start | bytes 786440 | tf_op jit(solution)/shard_map/ppermute | solution.py:439
  35.0 3.0 %copy-start.8 = (bf16[256,512]{1,0:T(8,128)(2,1)}, bf16[256,512]{1,0:T(8,128)(2,1)S(1)}, u32[]{:S(2)}) copy-start(bf16[256,512]{1,0:T(8,128)(2,1)S(1)} %collective-permute-done.5.refs_3_) | copy-start | bytes 786436
  35.0 3.0 %copy-start.9 = (bf16[256,512]{1,0:T(8,128)(2,1)}, bf16[256,512]{1,0:T(8,128)(2,1)S(1)}, u32[]{:S(2)}) copy-start(bf16[256,512]{1,0:T(8,128)(2,1)S(1)} %collective-permute-done.6.refs_4_) | copy-start | bytes 786436
  35.2 2.8 %copy-start.10 = (bf16[256,512]{1,0:T(8,128)(2,1)}, bf16[256,512]{1,0:T(8,128)(2,1)S(1)}, u32[]{:S(2)}) copy-start(bf16[256,512]{1,0:T(8,128)(2,1)S(1)} %collective-permute-done.2.refs_1_) | copy-start | bytes 786436
  38.0 0.7 copy-start.11
  43.8 7.4 %copy-start.12 = (s32[2048,3]{0,1:T(4,128)S(1)}, s32[2048,3]{0,1:T(4,128)}, u32[]{:S(2)}) copy-start(s32[2048,3]{0,1:T(4,128)} %param.29) | copy-start | bytes 73732
  43.8 7.5 %copy-start.13 = (f32[2048,3]{0,1:T(4,128)S(1)}, f32[2048,3]{0,1:T(4,128)}, u32[]{:S(2)}) copy-start(f32[2048,3]{0,1:T(4,128)} %param.30) | copy-start | bytes 73732
  43.8 7.7 %copy-start.7 = (bf16[512,512]{1,0:T(8,128)(2,1)S(1)}, bf16[512,512]{1,0:T(8,128)(2,1)}, u32[]{:S(2)}) copy-start(bf16[512,512]{1,0:T(8,128)(2,1)} %param.36) | copy-start | bytes 1572868
  43.9 8.1 %copy-start.17 = (bf16[512,512]{1,0:T(8,128)(2,1)S(1)}, bf16[512,512]{1,0:T(8,128)(2,1)}, u32[]{:S(2)}) copy-start(bf16[512,512]{1,0:T(8,128)(2,1)} %param.37) | copy-start | bytes 1572868
  43.9 8.1 %copy-start.18 = (bf16[512,512]{1,0:T(8,128)(2,1)S(1)}, bf16[512,512]{1,0:T(8,128)(2,1)}, u32[]{:S(2)}) copy-start(bf16[512,512]{1,0:T(8,128)(2,1)} %param.38) | copy-start | bytes 1572868
  43.9 62.6 %all-to-all-start = ((bf16[128,136,128]{2,1,0:T(8,128)(2,1)}), bf16[128,136,128]{2,1,0:T(8,128)(2,1)}, u32[]{:S(2)}, u32[]{:S(2)}) async-start(bf16[128,136,128]{2,1,0:T(8,128)(2,1)} %get-tuple-element.34), calls=%async_computation | async-start | bytes 8912896 | tf_op jit(solution)/shard_map/all_to_all | solution.py:472
  51.2 55.3 %copy-start.3 = (bf16[256,512]{1,0:T(8,128)(2,1)S(1)}, bf16[256,512]{1,0:T(8,128)(2,1)}, u32[]{:S(2)}) copy-start(bf16[256,512]{1,0:T(8,128)(2,1)} %get-tuple-element.43.first_ref) | copy-start | bytes 786436
  51.2 55.3 %copy-start.4 = (bf16[256,512]{1,0:T(8,128)(2,1)S(1)}, bf16[256,512]{1,0:T(8,128)(2,1)}, u32[]{:S(2)}) copy-start(bf16[256,512]{1,0:T(8,128)(2,1)} %get-tuple-element.42.q_ref) | copy-start | bytes 786436
  51.2 55.3 %copy-start.5 = (f32[512]{0:T(512)S(1)}, f32[512]{0:T(512)}, u32[]{:S(2)}) copy-start(f32[512]{0:T(512)} %param.40) | copy-start | bytes 6148
  111.8 8.1 %collective-permute-start.7 = (bf16[256,512]{1,0:T(8,128)(2,1)S(1)}, bf16[256,512]{1,0:T(8,128)(2,1)}, u32[]{:S(2)}, u32[]{:S(2)}) collective-permute-start(bf16[256,512]{1,0:T(8,128)(2,1)S(1)} %get-tuple-element.46.refs_2_), channel_id=1, source_target_pairs={{0,32},{32,0},{64,96},{96,64},{1,33},{33,1},{65,97},{97,65},{2,34}... | collective-permute-start | bytes 786440 | tf_op jit(solution)/shard_map/ppermute | solution.py:439
  112.4 8.9 %collective-permute-start.8 = (bf16[256,512]{1,0:T(8,128)(2,1)S(1)}, bf16[256,512]{1,0:T(8,128)(2,1)}, u32[]{:S(2)}, u32[]{:S(2)}) collective-permute-start(bf16[256,512]{1,0:T(8,128)(2,1)S(1)} %get-tuple-element.46.refs_2_), channel_id=1, source_target_pairs={{0,96},{32,64},{64,32},{96,0},{1,97},{33,65},{65,33},{97,1},{2,98}... | collective-permute-start | bytes 786440 | tf_op jit(solution)/shard_map/ppermute | solution.py:439
  113.0 12.0 %collective-permute-start.13 = (bf16[256,512]{1,0:T(8,128)(2,1)S(1)}, bf16[256,512]{1,0:T(8,128)(2,1)S(1)}, u32[]{:S(2)}, u32[]{:S(2)}) collective-permute-start(bf16[256,512]{1,0:T(8,128)(2,1)S(1)} %get-tuple-element.46.refs_2_), channel_id=1, source_target_pairs={{0,31},{1,2},{2,1},{3,4},{4,3},{5,6},{6,5},{7,8},{8,7},{9,10},{10,... | collective-permute-start | bytes 786440 | tf_op jit(solution)/shard_map/ppermute | solution.py:439
  113.5 16.4 %collective-permute-start.14 = (bf16[256,512]{1,0:T(8,128)(2,1)S(1)}, bf16[256,512]{1,0:T(8,128)(2,1)S(1)}, u32[]{:S(2)}, u32[]{:S(2)}) collective-permute-start(bf16[256,512]{1,0:T(8,128)(2,1)S(1)} %get-tuple-element.46.refs_2_), channel_id=1, source_target_pairs={{0,1},{1,0},{2,3},{3,2},{4,5},{5,4},{6,7},{7,6},{8,9},{9,8},{10,11... | collective-permute-start | bytes 786440 | tf_op jit(solution)/shard_map/ppermute | solution.py:439
  120.0 9.9 %collective-permute-start.9 = (bf16[256,512]{1,0:T(8,128)(2,1)}, bf16[256,512]{1,0:T(8,128)(2,1)S(1)}, u32[]{:S(2)}, u32[]{:S(2)}) collective-permute-start(bf16[256,512]{1,0:T(8,128)(2,1)} %collective-permute-done.7.refs_0_), channel_id=1, source_target_pairs={{0,31},{1,2},{2,1},{3,4},{4,3},{5,6},{6,5},{7,8},{8,7},{9,10},{10,... | collective-permute-start | bytes 786440 | tf_op jit(solution)/shard_map/ppermute | solution.py:439
  120.2 9.7 %collective-permute-start.10 = (bf16[256,512]{1,0:T(8,128)(2,1)}, bf16[256,512]{1,0:T(8,128)(2,1)S(1)}, u32[]{:S(2)}, u32[]{:S(2)}) collective-permute-start(bf16[256,512]{1,0:T(8,128)(2,1)} %collective-permute-done.7.refs_0_), channel_id=1, source_target_pairs={{0,1},{1,0},{2,3},{3,2},{4,5},{5,4},{6,7},{7,6},{8,9},{9,8},{10,11... | collective-permute-start | bytes 786440 | tf_op jit(solution)/shard_map/ppermute | solution.py:439
  121.3 10.8 %collective-permute-start.11 = (bf16[256,512]{1,0:T(8,128)(2,1)}, bf16[256,512]{1,0:T(8,128)(2,1)S(1)}, u32[]{:S(2)}, u32[]{:S(2)}) collective-permute-start(bf16[256,512]{1,0:T(8,128)(2,1)} %collective-permute-done.8.refs_1_), channel_id=1, source_target_pairs={{0,31},{1,2},{2,1},{3,4},{4,3},{5,6},{6,5},{7,8},{8,7},{9,10},{10,... | collective-permute-start | bytes 786440 | tf_op jit(solution)/shard_map/ppermute | solution.py:439
  125.0 7.1 %collective-permute-start.12 = (bf16[256,512]{1,0:T(8,128)(2,1)}, bf16[256,512]{1,0:T(8,128)(2,1)S(1)}, u32[]{:S(2)}, u32[]{:S(2)}) collective-permute-start(bf16[256,512]{1,0:T(8,128)(2,1)} %collective-permute-done.8.refs_1_), channel_id=1, source_target_pairs={{0,1},{1,0},{2,3},{3,2},{4,5},{5,4},{6,7},{7,6},{8,9},{9,8},{10,11... | collective-permute-start | bytes 786440 | tf_op jit(solution)/shard_map/ppermute | solution.py:439
  125.4 6.7 %copy-start.1 = (bf16[2048,512]{1,0:T(8,128)(2,1)S(1)}, bf16[2048,512]{1,0:T(8,128)(2,1)}, u32[]{:S(2)}) copy-start(bf16[2048,512]{1,0:T(8,128)(2,1)} %grid_ref.1) | copy-start | bytes 6291460
  125.4 6.7 %copy-start.6 = (f32[512]{0:T(512)S(1)}, f32[512]{0:T(512)}, u32[]{:S(2)}) copy-start(f32[512]{0:T(512)} %param.41) | copy-start | bytes 6148

commit v6 on v5

--- a/solution.py
+++ b/solution.py
@@ -10,7 +10,7 @@
 BF16 = jnp.bfloat16
 F32 = jnp.float32
 LANES = 128
-MARKS = 8
+MARKS = 16
 MIB = 1024 * 1024
 EDGE_MIB = 24
 NODE_MIB = 57

time: 139 us -> 142 us (1.022)
  waiting for transfers between devices: 67.2 us -> 69.9 us
    all_to_all x1, waiting for transfers between devices: 54.1 us -> 56.9 us  [on_device(): lax.all_to_all(rows, ('lat', 'lon'), split_axis=0, concat_axis=0, tiled=T...]
where the time goes in v6:
time: 142 us
  waiting for transfers between devices  69.9 us (49%)
  Pallas kernels  35.9 us (25%)
  starting transfers between devices  30.3 us (21%)
  local copies, waits for them, and re-layouts  3.8 us (3%)
    all_to_all x1, waiting for transfers between devices, on_device(): lax.all_to_all(rows, ('lat', 'lon'), split_axis=0, concat_axis=0, tiled=T...  56.9 us
    ppermute x15, starting transfers between devices, swap(): return lax.ppermute(block, axis, pairs)  23 us
    pallas_call x1, Pallas kernels, scatter(): pl.pallas_call(functools.partial(scatter_kernel, nodes=nodes, lon_count=l...  13.8 us
    ppermute x15, waiting for transfers between devices, swap(): return lax.ppermute(block, axis, pairs)  13.1 us
    all_to_all x1, starting transfers between devices, on_device(): lax.all_to_all(rows, ('lat', 'lon'), split_axis=0, concat_axis=0, tiled=T...  7.31 us
    pallas_call x1, Pallas kernels, grid_stage(): pl.pallas_call(functools.partial(grid_kernel, inner=256, tiles=tiles), gr...  6.87 us
    pallas_call x1, Pallas kernels, edge_stage(): pl.pallas_call(functools.partial(edge_kernel, per=per), out_shape=(out, o...  5.32 us
    pallas_call x1, Pallas kernels, node_stage(): pl.pallas_call(functools.partial(node_kernel, pieces=len(sums)), out_shap...  5.22 us
  transfers between devices with their start and end apart: 16, of which 7 were waited for; matrix products, arithmetic and copies ran while one was open for 2% of the time, Pallas kernels for 3%

profile of v6, /device:TPU:0, one launch (start us, length us, event | category | flops | bytes accessed | tf_op | source)
XLA Modules:
  0.0 142.0 jit_solution(241695145328996076)
XLA Ops:
  0.6 0.0 copy-start
  0.7 13.8 %grid_to_mesh.1 = (bf16[512,512]{1,0:T(8,128)(2,1)}, bf16[256,512]{1,0:T(8,128)(2,1)}, bf16[256,512]{1,0:T(8,128)(2,1)}, bf16[256,512]{1,0:T(8,128)(2,1)}, bf16[...) custom-call(s32[32,128]{1,0:T(8,128)} %bitcast.19, s32[32,128]{1,0:T(8,128)} %bitcast.20, ...), custom_call_target="tpu_custom_call" | custom-call | tf_op jit(solution)/shard_map/grid_to_mesh/pallas_call | solution.py:159
  14.5 0.0 copy-start.14
  14.5 0.0 copy-start.16
  14.5 0.1 collective-permute-start.1
  14.6 5.4 %collective-permute-start = (bf16[256,512]{1,0:T(8,128)(2,1)}, bf16[256,512]{1,0:T(8,128)(2,1)S(1)}, u32[]{:S(2)}, u32[]{:S(2)}) collective-permute-start(bf16[256,512]{1,0:T(8,128)(2,1)} %get-tuple-element.26), channel_id=1, source_target_pairs={{0,31},{1,2},{2,1},{3,4},{4,3},{5,6},{6,5},{7,8},{8,7},{9,10},{10,... | collective-permute-start | bytes 786440 | tf_op jit(solution)/shard_map/ppermute | solution.py:439
  20.0 0.0 collective-permute-start.3
  20.1 5.0 %collective-permute-start.5 = (bf16[256,512]{1,0:T(8,128)(2,1)}, bf16[256,512]{1,0:T(8,128)(2,1)S(1)}, u32[]{:S(2)}, u32[]{:S(2)}) collective-permute-start(bf16[256,512]{1,0:T(8,128)(2,1)} %get-tuple-element.32), channel_id=1, source_target_pairs={{0,31},{1,2},{2,1},{3,4},{4,3},{5,6},{6,5},{7,8},{8,7},{9,10},{10,... | collective-permute-start | bytes 786440 | tf_op jit(solution)/shard_map/ppermute | solution.py:439
  25.1 0.0 collective-permute-start.6
  25.1 0.0 collective-permute-done.1.b_ref
  25.1 1.0 copy-done.2
  26.2 0.1 add_near.1
  26.3 0.0 collective-permute-done.a_ref
  26.3 2.0 %collective-permute-start.2 = (bf16[256,512]{1,0:T(8,128)(2,1)S(1)}, bf16[256,512]{1,0:T(8,128)(2,1)S(1)}, u32[]{:S(2)}, u32[]{:S(2)}) collective-permute-start(bf16[256,512]{1,0:T(8,128)(2,1)S(1)} %add_far.2), channel_id=1, source_target_pairs={{0,32},{32,0},{64,96},{96,64},{1,33},{33,1},{65,97},{97,65},{2,34}... | collective-permute-start | bytes 786440 | tf_op jit(solution)/shard_map/ppermute | solution.py:439
  28.3 1.1 collective-permute-done.3.a_ref
  29.4 4.1 %collective-permute-start.4 = (bf16[256,512]{1,0:T(8,128)(2,1)S(1)}, bf16[256,512]{1,0:T(8,128)(2,1)S(1)}, u32[]{:S(2)}, u32[]{:S(2)}) collective-permute-start(bf16[256,512]{1,0:T(8,128)(2,1)S(1)} %add_far.3), channel_id=1, source_target_pairs={{0,96},{32,64},{64,32},{96,0},{1,97},{33,65},{65,33},{97,1},{2,98}... | collective-permute-start | bytes 786440 | tf_op jit(solution)/shard_map/ppermute | solution.py:439
  33.5 0.1 copy.50
  33.6 0.7 sub.47.refs_10_
  34.3 0.0 copy-done.15
  34.4 0.7 copy.52.refs_11_
  35.1 0.0 collective-permute-done.5.refs_3_
  35.1 0.0 collective-permute-done.6.refs_4_
  35.1 0.0 copy-start.9
  35.1 0.2 collective-permute-done.2.refs_1_
  35.3 2.8 %collective-permute-done.4.refs_2_ = bf16[256,512]{1,0:T(8,128)(2,1)S(1)} collective-permute-done((bf16[256,512]{1,0:T(8,128)(2,1)S(1)}, bf16[256,512]{1,0:T(8,128)(2,1)S(1)}, u32[]{:S(2)}, u32[]{:S(2)}) %collective-permute-start.4) | collective-permute-done | bytes 262176 | tf_op jit(solution)/shard_map/ppermute | solution.py:439
  38.1 0.7 copy-done.11
  38.8 5.2 %mesh_encoder.1 = (bf16[256,512]{1,0:T(8,128)(2,1)}, bf16[256,512]{1,0:T(8,128)(2,1)}, bf16[128,144,128]{2,1,0:T(8,128)(2,1)}) custom-call(bf16[256,512]{1,0:T(8,128)(2,1)} %get-tuple-element.25.refs_0_, bf16[256,512]{1,0:T(8,128)(2,1)} %copy-done.10, bf16[256,512]{1,0:T(8,128)(2,1)} %copy-done.11, bf16[256,512]{1,0:T(8,128)(2,1)} %copy-done.8, ...), custom_call_target="tpu_custom_call" | custom-call | tf_op jit(solution)/shard_map/mesh_encoder/pallas_call | solution.py:272
  44.0 0.0 copy-start.12
  44.0 0.0 copy-start.13
  44.1 0.0 copy-start.7
  44.1 0.0 copy-start.17
  44.1 0.0 copy-start.18
  44.1 7.3 %all-to-all-start = ((bf16[128,144,128]{2,1,0:T(8,128)(2,1)}), bf16[128,144,128]{2,1,0:T(8,128)(2,1)}, u32[]{:S(2)}, u32[]{:S(2)}) async-start(bf16[128,144,128]{2,1,0:T(8,128)(2,1)} %get-tuple-element.34), calls=%async_computation | async-start | bytes 9437184 | tf_op jit(solution)/shard_map/all_to_all | solution.py:472
  51.4 0.0 copy-start.5
  51.5 0.1 and_add_fusion
  51.5 0.0 copy-done.13
  51.6 0.1 stack.2
  51.7 0.0 copy-done
  51.7 0.0 copy-done.7
  51.7 0.4 convolution_convert_fusion.w_sum
  52.2 0.4 fusion.w_dec
  52.7 56.9 %all-to-all-done.rows_hbm = bf16[128,144,128]{2,1,0:T(8,128)(2,1)} async-done(((bf16[128,144,128]{2,1,0:T(8,128)(2,1)}), bf16[128,144,128]{2,1,0:T(8,128)(2,1)}, u32[]{:S(2)}, u32[]{:S(2)}) %all-to-all-start) | async-done | bytes 4718624 | tf_op jit(solution)/shard_map/all_to_all | solution.py:472
  109.5 5.3 %mesh_edges.1 = (bf16[256,512]{1,0:T(8,128)(2,1)}, bf16[256,512]{1,0:T(8,128)(2,1)S(1)}) custom-call(bf16[128,144,128]{2,1,0:T(8,128)(2,1)} %all-to-all-done.rows_hbm, bf16[256,512]{1,0:T(8,128)(2,1)S(1)} %copy-done.4, bf16[256,512]{1,0:T(8,128)(2,1)S(1)} %copy-done.3, bf16[512,512]{1,0:T(8,128)(2,1)S(1)} %convolution_convert_fusion.w_sum, ...), custom_call_target="tpu_custom_call" | custom-call | tf_op jit(solution)/shard_map/mesh_edges/pallas_call | solution.py:332
  114.9 0.5 collective-permute-start.7
  115.3 0.7 collective-permute-start.8
  116.0 0.5 collective-permute-start.13
  116.5 0.3 collective-permute-start.14
  116.8 6.1 %collective-permute-done.7.refs_0_ = bf16[256,512]{1,0:T(8,128)(2,1)} collective-permute-done((bf16[256,512]{1,0:T(8,128)(2,1)S(1)}, bf16[256,512]{1,0:T(8,128)(2,1)}, u32[]{:S(2)}, u32[]{:S(2)}) %collective-permute-start.7) | collective-permute-done | bytes 262176 | tf_op jit(solution)/shard_map/ppermute | solution.py:439
  122.9 0.4 collective-permute-start.9
  123.3 0.3 collective-permute-start.10
  123.6 0.7 collective-permute-done.8.refs_1_
  124.2 3.8 %collective-permute-start.11 = (bf16[256,512]{1,0:T(8,128)(2,1)}, bf16[256,512]{1,0:T(8,128)(2,1)S(1)}, u32[]{:S(2)}, u32[]{:S(2)}) collective-permute-start(bf16[256,512]{1,0:T(8,128)(2,1)} %collective-permute-done.8.refs_1_), channel_id=1, source_target_pairs={{0,31},{1,2},{2,1},{3,4},{4,3},{5,6},{6,5},{7,8},{8,7},{9,10},{10,... | collective-permute-start | bytes 786440 | tf_op jit(solution)/shard_map/ppermute | solution.py:439
  128.0 0.0 collective-permute-done.13.refs_4_
  128.0 0.0 collective-permute-start.12
  128.0 0.4 copy.54.picks_ref
  128.4 0.0 copy-start.1
  128.4 0.0 copy-start.6
  128.4 4.4 %mesh_to_grid_first.1.part_ref = bf16[2048,512]{1,0:T(8,128)(2,1)S(1)} custom-call(f32[2048,6]{1,0:T(8,128)S(1)} %copy.54.picks_ref, bf16[256,512]{1,0:T(8,128)(2,1)} %collective-permute-done.7.refs_0_, bf16[256,512]{1,0:T(8,128)(2,1)} %collective-permute-done.8.refs_1_, bf16[256,512]{1,0:T(8,128)(2,1)S(1)} %get-tuple-element.46.refs_2_), custom_call_target="tpu_custom_call" | custom-call | flops 1610612736 | bytes 8388608 | tf_op jit(solution)/shard_map/mesh_to_grid_first/pallas_call | solution.py:387
  132.9 0.0 collective-permute-done.14.refs_5_
  132.9 0.0 collective-permute-done.9.refs_0_
  132.9 0.0 collective-permute-done.10.refs_1_
  132.9 2.2 %collective-permute-done.11.refs_2_ = bf16[256,512]{1,0:T(8,128)(2,1)S(1)} collective-permute-done((bf16[256,512]{1,0:T(8,128)(2,1)}, bf16[256,512]{1,0:T(8,128)(2,1)S(1)}, u32[]{:S(2)}, u32[]{:S(2)}) %collective-permute-start.11) | collective-permute-done | bytes 262176 | tf_op jit(solution)/shard_map/ppermute | solution.py:439
  135.1 0.0 collective-permute-done.12.refs_3_
  135.1 6.9 %mesh_to_grid.1 = bf16[2048,512]{1,0:T(8,128)(2,1)} custom-call(f32[2048,6]{1,0:T(8,128)S(1)} %copy.54.picks_ref, bf16[2048,512]{1,0:T(8,128)(2,1)S(1)} %mesh_to_grid_first.1.part_ref, bf16[2048,512]{1,0:T(8,128)(2,1)S(1)} %copy-done.1, f32[1,512]{1,0:T(1,128)S(1)} %bitcast.17, bf16[256,512]{1,0:T(8,128)(2,1)S(1)} %collective-permute-done.9.refs_0_, ...), custom_call_target="tpu_custom_call" | custom-call | tf_op jit(solution)/shard_map/mesh_to_grid/pallas_call | solution.py:419
  (27 shorter events, 0.2 us)
Async XLA Ops:
  0.6 51.1 %copy-start = (bf16[512,512]{1,0:T(8,128)(2,1)S(1)}, bf16[512,512]{1,0:T(8,128)(2,1)}, u32[]{:S(2)}) copy-start(bf16[512,512]{1,0:T(8,128)(2,1)} %param.35) | copy-start | bytes 1572868
  0.6 33.7 %copy-start.15 = (s32[1,128,32]{1,2,0:T(8,128)S(1)}, s32[1,128,32]{1,2,0:T(8,128)}, u32[]{:S(2)}) copy-start(s32[1,128,32]{1,2,0:T(8,128)} %param.27) | copy-start | bytes 49156
  14.5 19.0 %copy-start.14 = (s32[1,128,32]{1,2,0:T(8,128)S(1)}, s32[1,128,32]{1,2,0:T(8,128)}, u32[]{:S(2)}) copy-start(s32[1,128,32]{1,2,0:T(8,128)} %param.26) | copy-start | bytes 49156
  14.5 19.8 %copy-start.16 = (s32[1,128]{1,0:T(1,128)S(1)}, s32[1,128]{1,0:T(1,128)}, u32[]{:S(2)}) copy-start(s32[1,128]{1,0:T(1,128)} %param.28) | copy-start | bytes 1540
  14.5 10.6 %collective-permute-start.1 = (bf16[512,512]{1,0:T(8,128)(2,1)}, bf16[512,512]{1,0:T(8,128)(2,1)S(1)}, u32[]{:S(2)}, u32[]{:S(2)}) collective-permute-start(bf16[512,512]{1,0:T(8,128)(2,1)} %get-tuple-element.28), channel_id=1, source_target_pairs={{0,1},{1,0},{2,3},{3,2},{4,5},{5,4},{6,7},{7,6},{8,9},{9,8},{10,11... | collective-permute-start | bytes 1572872 | tf_op jit(solution)/shard_map/ppermute | solution.py:439
  14.6 11.6 %collective-permute-start = (bf16[256,512]{1,0:T(8,128)(2,1)}, bf16[256,512]{1,0:T(8,128)(2,1)S(1)}, u32[]{:S(2)}, u32[]{:S(2)}) collective-permute-start(bf16[256,512]{1,0:T(8,128)(2,1)} %get-tuple-element.26), channel_id=1, source_target_pairs={{0,31},{1,2},{2,1},{3,4},{4,3},{5,6},{6,5},{7,8},{8,7},{9,10},{10,... | collective-permute-start | bytes 786440 | tf_op jit(solution)/shard_map/ppermute | solution.py:439
  20.0 9.3 %collective-permute-start.3 = (bf16[256,512]{1,0:T(8,128)(2,1)}, bf16[256,512]{1,0:T(8,128)(2,1)S(1)}, u32[]{:S(2)}, u32[]{:S(2)}) collective-permute-start(bf16[256,512]{1,0:T(8,128)(2,1)} %get-tuple-element.30), channel_id=1, source_target_pairs={{0,31},{1,2},{2,1},{3,4},{4,3},{5,6},{6,5},{7,8},{8,7},{9,10},{10,... | collective-permute-start | bytes 786440 | tf_op jit(solution)/shard_map/ppermute | solution.py:439
  20.1 15.0 %collective-permute-start.5 = (bf16[256,512]{1,0:T(8,128)(2,1)}, bf16[256,512]{1,0:T(8,128)(2,1)S(1)}, u32[]{:S(2)}, u32[]{:S(2)}) collective-permute-start(bf16[256,512]{1,0:T(8,128)(2,1)} %get-tuple-element.32), channel_id=1, source_target_pairs={{0,31},{1,2},{2,1},{3,4},{4,3},{5,6},{6,5},{7,8},{8,7},{9,10},{10,... | collective-permute-start | bytes 786440 | tf_op jit(solution)/shard_map/ppermute | solution.py:439
  25.1 10.0 %collective-permute-start.6 = (bf16[256,512]{1,0:T(8,128)(2,1)}, bf16[256,512]{1,0:T(8,128)(2,1)S(1)}, u32[]{:S(2)}, u32[]{:S(2)}) collective-permute-start(bf16[256,512]{1,0:T(8,128)(2,1)} %get-tuple-element.33), channel_id=1, source_target_pairs={{0,1},{1,0},{2,3},{3,2},{4,5},{5,4},{6,7},{7,6},{8,9},{9,8},{10,11... | collective-permute-start | bytes 786440 | tf_op jit(solution)/shard_map/ppermute | solution.py:439
  25.1 1.0 copy-start.2
  26.3 9.0 %collective-permute-start.2 = (bf16[256,512]{1,0:T(8,128)(2,1)S(1)}, bf16[256,512]{1,0:T(8,128)(2,1)S(1)}, u32[]{:S(2)}, u32[]{:S(2)}) collective-permute-start(bf16[256,512]{1,0:T(8,128)(2,1)S(1)} %add_far.2), channel_id=1, source_target_pairs={{0,32},{32,0},{64,96},{96,64},{1,33},{33,1},{65,97},{97,65},{2,34}... | collective-permute-start | bytes 786440 | tf_op jit(solution)/shard_map/ppermute | solution.py:439
  29.4 8.7 %collective-permute-start.4 = (bf16[256,512]{1,0:T(8,128)(2,1)S(1)}, bf16[256,512]{1,0:T(8,128)(2,1)S(1)}, u32[]{:S(2)}, u32[]{:S(2)}) collective-permute-start(bf16[256,512]{1,0:T(8,128)(2,1)S(1)} %add_far.3), channel_id=1, source_target_pairs={{0,96},{32,64},{64,32},{96,0},{1,97},{33,65},{65,33},{97,1},{2,98}... | collective-permute-start | bytes 786440 | tf_op jit(solution)/shard_map/ppermute | solution.py:439
  35.1 3.0 %copy-start.8 = (bf16[256,512]{1,0:T(8,128)(2,1)}, bf16[256,512]{1,0:T(8,128)(2,1)S(1)}, u32[]{:S(2)}) copy-start(bf16[256,512]{1,0:T(8,128)(2,1)S(1)} %collective-permute-done.5.refs_3_) | copy-start | bytes 786436
  35.1 3.0 %copy-start.9 = (bf16[256,512]{1,0:T(8,128)(2,1)}, bf16[256,512]{1,0:T(8,128)(2,1)S(1)}, u32[]{:S(2)}) copy-start(bf16[256,512]{1,0:T(8,128)(2,1)S(1)} %collective-permute-done.6.refs_4_) | copy-start | bytes 786436
  35.3 2.8 %copy-start.10 = (bf16[256,512]{1,0:T(8,128)(2,1)}, bf16[256,512]{1,0:T(8,128)(2,1)S(1)}, u32[]{:S(2)}) copy-start(bf16[256,512]{1,0:T(8,128)(2,1)S(1)} %collective-permute-done.2.refs_1_) | copy-start | bytes 786436
  38.1 0.7 copy-start.11
  44.0 7.4 %copy-start.12 = (s32[2048,3]{0,1:T(4,128)S(1)}, s32[2048,3]{0,1:T(4,128)}, u32[]{:S(2)}) copy-start(s32[2048,3]{0,1:T(4,128)} %param.29) | copy-start | bytes 73732
  44.0 7.5 %copy-start.13 = (f32[2048,3]{0,1:T(4,128)S(1)}, f32[2048,3]{0,1:T(4,128)}, u32[]{:S(2)}) copy-start(f32[2048,3]{0,1:T(4,128)} %param.30) | copy-start | bytes 73732
  44.1 7.7 %copy-start.7 = (bf16[512,512]{1,0:T(8,128)(2,1)S(1)}, bf16[512,512]{1,0:T(8,128)(2,1)}, u32[]{:S(2)}) copy-start(bf16[512,512]{1,0:T(8,128)(2,1)} %param.36) | copy-start | bytes 1572868
  44.1 8.1 %copy-start.17 = (bf16[512,512]{1,0:T(8,128)(2,1)S(1)}, bf16[512,512]{1,0:T(8,128)(2,1)}, u32[]{:S(2)}) copy-start(bf16[512,512]{1,0:T(8,128)(2,1)} %param.37) | copy-start | bytes 1572868
  44.1 8.1 %copy-start.18 = (bf16[512,512]{1,0:T(8,128)(2,1)S(1)}, bf16[512,512]{1,0:T(8,128)(2,1)}, u32[]{:S(2)}) copy-start(bf16[512,512]{1,0:T(8,128)(2,1)} %param.38) | copy-start | bytes 1572868
  44.1 65.4 %all-to-all-start = ((bf16[128,144,128]{2,1,0:T(8,128)(2,1)}), bf16[128,144,128]{2,1,0:T(8,128)(2,1)}, u32[]{:S(2)}, u32[]{:S(2)}) async-start(bf16[128,144,128]{2,1,0:T(8,128)(2,1)} %get-tuple-element.34), calls=%async_computation | async-start | bytes 9437184 | tf_op jit(solution)/shard_map/all_to_all | solution.py:472
  51.4 58.1 %copy-start.3 = (bf16[256,512]{1,0:T(8,128)(2,1)S(1)}, bf16[256,512]{1,0:T(8,128)(2,1)}, u32[]{:S(2)}) copy-start(bf16[256,512]{1,0:T(8,128)(2,1)} %get-tuple-element.43.first_ref) | copy-start | bytes 786436
  51.4 58.1 %copy-start.4 = (bf16[256,512]{1,0:T(8,128)(2,1)S(1)}, bf16[256,512]{1,0:T(8,128)(2,1)}, u32[]{:S(2)}) copy-start(bf16[256,512]{1,0:T(8,128)(2,1)} %get-tuple-element.42.q_ref) | copy-start | bytes 786436
  51.4 58.1 %copy-start.5 = (f32[512]{0:T(512)S(1)}, f32[512]{0:T(512)}, u32[]{:S(2)}) copy-start(f32[512]{0:T(512)} %param.40) | copy-start | bytes 6148
  114.9 8.1 %collective-permute-start.7 = (bf16[256,512]{1,0:T(8,128)(2,1)S(1)}, bf16[256,512]{1,0:T(8,128)(2,1)}, u32[]{:S(2)}, u32[]{:S(2)}) collective-permute-start(bf16[256,512]{1,0:T(8,128)(2,1)S(1)} %get-tuple-element.46.refs_2_), channel_id=1, source_target_pairs={{0,32},{32,0},{64,96},{96,64},{1,33},{33,1},{65,97},{97,65},{2,34}... | collective-permute-start | bytes 786440 | tf_op jit(solution)/shard_map/ppermute | solution.py:439
  115.3 8.9 %collective-permute-start.8 = (bf16[256,512]{1,0:T(8,128)(2,1)S(1)}, bf16[256,512]{1,0:T(8,128)(2,1)}, u32[]{:S(2)}, u32[]{:S(2)}) collective-permute-start(bf16[256,512]{1,0:T(8,128)(2,1)S(1)} %get-tuple-element.46.refs_2_), channel_id=1, source_target_pairs={{0,96},{32,64},{64,32},{96,0},{1,97},{33,65},{65,33},{97,1},{2,98}... | collective-permute-start | bytes 786440 | tf_op jit(solution)/shard_map/ppermute | solution.py:439
  116.0 12.0 %collective-permute-start.13 = (bf16[256,512]{1,0:T(8,128)(2,1)S(1)}, bf16[256,512]{1,0:T(8,128)(2,1)S(1)}, u32[]{:S(2)}, u32[]{:S(2)}) collective-permute-start(bf16[256,512]{1,0:T(8,128)(2,1)S(1)} %get-tuple-element.46.refs_2_), channel_id=1, source_target_pairs={{0,31},{1,2},{2,1},{3,4},{4,3},{5,6},{6,5},{7,8},{8,7},{9,10},{10,... | collective-permute-start | bytes 786440 | tf_op jit(solution)/shard_map/ppermute | solution.py:439
  116.5 16.3 %collective-permute-start.14 = (bf16[256,512]{1,0:T(8,128)(2,1)S(1)}, bf16[256,512]{1,0:T(8,128)(2,1)S(1)}, u32[]{:S(2)}, u32[]{:S(2)}) collective-permute-start(bf16[256,512]{1,0:T(8,128)(2,1)S(1)} %get-tuple-element.46.refs_2_), channel_id=1, source_target_pairs={{0,1},{1,0},{2,3},{3,2},{4,5},{5,4},{6,7},{7,6},{8,9},{9,8},{10,11... | collective-permute-start | bytes 786440 | tf_op jit(solution)/shard_map/ppermute | solution.py:439
  122.9 9.9 %collective-permute-start.9 = (bf16[256,512]{1,0:T(8,128)(2,1)}, bf16[256,512]{1,0:T(8,128)(2,1)S(1)}, u32[]{:S(2)}, u32[]{:S(2)}) collective-permute-start(bf16[256,512]{1,0:T(8,128)(2,1)} %collective-permute-done.7.refs_0_), channel_id=1, source_target_pairs={{0,31},{1,2},{2,1},{3,4},{4,3},{5,6},{6,5},{7,8},{8,7},{9,10},{10,... | collective-permute-start | bytes 786440 | tf_op jit(solution)/shard_map/ppermute | solution.py:439
  123.3 9.6 %collective-permute-start.10 = (bf16[256,512]{1,0:T(8,128)(2,1)}, bf16[256,512]{1,0:T(8,128)(2,1)S(1)}, u32[]{:S(2)}, u32[]{:S(2)}) collective-permute-start(bf16[256,512]{1,0:T(8,128)(2,1)} %collective-permute-done.7.refs_0_), channel_id=1, source_target_pairs={{0,1},{1,0},{2,3},{3,2},{4,5},{5,4},{6,7},{7,6},{8,9},{9,8},{10,11... | collective-permute-start | bytes 786440 | tf_op jit(solution)/shard_map/ppermute | solution.py:439
  124.2 10.8 %collective-permute-start.11 = (bf16[256,512]{1,0:T(8,128)(2,1)}, bf16[256,512]{1,0:T(8,128)(2,1)S(1)}, u32[]{:S(2)}, u32[]{:S(2)}) collective-permute-start(bf16[256,512]{1,0:T(8,128)(2,1)} %collective-permute-done.8.refs_1_), channel_id=1, source_target_pairs={{0,31},{1,2},{2,1},{3,4},{4,3},{5,6},{6,5},{7,8},{8,7},{9,10},{10,... | collective-permute-start | bytes 786440 | tf_op jit(solution)/shard_map/ppermute | solution.py:439
  128.0 7.1 %collective-permute-start.12 = (bf16[256,512]{1,0:T(8,128)(2,1)}, bf16[256,512]{1,0:T(8,128)(2,1)S(1)}, u32[]{:S(2)}, u32[]{:S(2)}) collective-permute-start(bf16[256,512]{1,0:T(8,128)(2,1)} %collective-permute-done.8.refs_1_), channel_id=1, source_target_pairs={{0,1},{1,0},{2,3},{3,2},{4,5},{5,4},{6,7},{7,6},{8,9},{9,8},{10,11... | collective-permute-start | bytes 786440 | tf_op jit(solution)/shard_map/ppermute | solution.py:439
  128.4 6.7 %copy-start.1 = (bf16[2048,512]{1,0:T(8,128)(2,1)S(1)}, bf16[2048,512]{1,0:T(8,128)(2,1)}, u32[]{:S(2)}) copy-start(bf16[2048,512]{1,0:T(8,128)(2,1)} %grid_ref.1) | copy-start | bytes 6291460
  128.4 6.7 %copy-start.6 = (f32[512]{0:T(512)S(1)}, f32[512]{0:T(512)}, u32[]{:S(2)}) copy-start(f32[512]{0:T(512)} %param.41) | copy-start | bytes 6148
